TPU v7x, 512 devices: a whole 4x8x8 slice. The times are simulated.
512 devices in a mesh: dp: 8 (over z), seq: 64 (over y, x, core).
Axes of the slice: x: 4, y: 8, z: 8, core: 2. Of those that a mesh axis runs over, the one named last changes fastest.
Arguments:
- tokens: bfloat16 [8, 8192, 1280], P('dp', 'seq'), may hold values from -6 to 6
- place: int32 [64, 128], P('seq'), may hold values from 0 to 127, each once within a row
- kernel: float32 [27, 1280], replicated, may hold values from -1.25 to 1.25
- proj_weight: bfloat16 [1280, 3840], P('seq'), may hold values from -0.15625 to 0.15625
- d_projected: bfloat16 [8, 8192, 3840], P('dp', 'seq'), may hold values from -6 to 6
Outputs:
- projected: bfloat16 [8, 8192, 3840], P('dp', 'seq')
- d_tokens: bfloat16 [8, 8192, 1280], P('dp', 'seq')
- d_kernel: float32 [27, 1280], replicated
Inputs may be any that keep to these rules, and one draw needn't show every extreme that they name: Each row of place holds every number 0 to 127 once.
All inputs are finite; a program needn't handle non-finite values.
Results may differ from a plain program's by a relative error of at most 0.005.
Values may be sent and summed in bfloat16 or wider, within the bound.
No kernel may reach another device: no remote copies, remote signals or barrier semaphores. Data moves between devices by JAX's collectives and lax.ppermute only.
A program may use at most 128 MiB of HBM per device.

v0:
```python
import jax
import jax.numpy as jnp
from jax import lax
from jax.sharding import PartitionSpec as P

INLINE = 8
CROSS = 8


def with_halo(value, sides, width):
    for axis, dim in sides:
        size, length = (lax.axis_size(axis), value.shape[dim])
        up = [(i, (i + 1) % size) for i in range(size - 1)]
        down = [(j, i) for i, j in up]
        last = lax.slice_in_dim(value, length - width, length, axis=dim)
        first = lax.slice_in_dim(value, 0, width, axis=dim)
        before = lax.ppermute(last, axis, up)
        after = lax.ppermute(first, axis, down)
        value = jnp.concatenate([before, value, after], axis=dim)
    return value


def brick_cells(landed, inverse):
    tokens_dev = inverse.shape[0]
    width = landed.shape[-1]
    slots = landed.reshape(tokens_dev, width)
    cells = jnp.take(slots, inverse, axis=0)
    return cells.reshape(tokens_dev // (INLINE * CROSS), INLINE, CROSS, width)


def scan_pieces(cells, order, count):
    width = cells.shape[-1]
    tokens_dev = order.shape[0]
    slots = jnp.take(cells.reshape(tokens_dev, width), order, axis=0)
    return slots.reshape(count, tokens_dev // count, width)


def to_bricks(rows, inverse, count):
    tokens_dev, width = rows.shape
    landed = lax.all_to_all(
        rows.reshape(count, tokens_dev // count, width),
        "seq",
        split_axis=0,
        concat_axis=0,
        tiled=True,
    )
    return brick_cells(landed, inverse)


def to_scan(cells, order, count):
    landed = lax.all_to_all(
        scan_pieces(cells, order, count), "seq", split_axis=0, concat_axis=0, tiled=True
    )
    return landed.reshape(order.shape[0], cells.shape[-1])


def with_faces(block):
    deeper = with_halo(block, (("seq", 0),), 1)
    return jnp.pad(deeper, ((0, 0), (1, 1), (1, 1), (0, 0)))


def window(field, depth_dev, start_z, start_i, start_c):
    return field[
        start_z : start_z + depth_dev, start_i : start_i + INLINE, start_c : start_c + CROSS
    ].astype(jnp.float32)


def forward_conv(grid_x, pad_x, kernel, depth_dev):
    conv = jnp.zeros(grid_x.shape, jnp.float32)
    for offset in range(27):
        conv = conv + kernel[offset] * window(
            pad_x, depth_dev, offset // 9, offset // 3 % 3, offset % 3
        )
    return (grid_x.astype(jnp.float32) + conv).astype(jnp.bfloat16)


def backward_conv(grid_d, pad_d, pad_x, kernel, depth_dev):
    grid_float = grid_d.astype(jnp.float32)
    back = grid_float
    partial_value = []
    for offset in range(27):
        dz, di, dc = (offset // 9, offset // 3 % 3, offset % 3)
        back = back + kernel[offset] * window(pad_d, depth_dev, 2 - dz, 2 - di, 2 - dc)
        partial_value.append(
            jnp.sum(grid_float * window(pad_x, depth_dev, dz, di, dc), axis=(0, 1, 2))
        )
    return (back.astype(jnp.bfloat16), jnp.stack(partial_value))


def shards(tokens, place, kernel, proj_weight, d_projected):
    count = lax.axis_size("seq")
    order = place[0]
    inverse = jnp.argsort(order)
    rows_x = tokens[0]
    d_rows = d_projected[0]
    depth_dev = rows_x.shape[0] // (INLINE * CROSS)
    d_y = lax.dot_general(
        d_rows,
        lax.all_gather(proj_weight, "seq", axis=0, tiled=True),
        (((1,), (1,)), ((), ())),
        preferred_element_type=jnp.float32,
    )
    d_y = d_y.astype(jnp.bfloat16)
    grid_x = to_bricks(rows_x, inverse, count)
    pad_x = with_faces(grid_x)
    grid_y = forward_conv(grid_x, pad_x, kernel, depth_dev)
    rows_y = to_scan(grid_y, order, count)
    grid_d = to_bricks(d_y, inverse, count)
    pad_d = with_faces(grid_d)
    back, partial_value = backward_conv(grid_d, pad_d, pad_x, kernel, depth_dev)
    d_tokens = to_scan(back, order, count)
    projected = jnp.dot(
        rows_y,
        lax.all_gather(proj_weight, "seq", axis=0, tiled=True),
        preferred_element_type=jnp.float32,
    )
    projected = projected.astype(jnp.bfloat16)
    d_kernel = lax.psum(partial_value, ("dp", "seq"))
    return (projected[None], d_tokens[None], d_kernel)


def solution(mesh):
    placed = (P("dp", "seq", None), P("seq", None), P(), P("seq", None), P("dp", "seq", None))
    return jax.shard_map(
        shards,
        mesh=mesh,
        in_specs=placed,
        out_specs=(P("dp", "seq", None), P("dp", "seq", None), P()),
        check_vma=False,
    )
```

profile of v0, /device:TPU:1, one launch (start us, length us, event | category | flops | bytes accessed | tf_op | source)
XLA Modules:
  0.0 491.7 jit_solution(6049392206160936502)
XLA Ops:
  7.2 0.0 copy-start
  7.2 0.0 all-gather.3.cloned.1.call-start
  7.2 0.7 all-gather.3.cloned.1.call-update
  7.9 1.8 reshape_squeeze.3
  9.7 11.6 %all-to-all-start = ((bf16[64,2,1280]{2,1,0:T(2,128)(2,1)}), bf16[64,2,1280]{2,1,0:T(2,128)(2,1)S(1)}, u32[]{:S(2)}, u32[]{:S(2)}) async-start(bf16[64,2,1280]{2,1,0:T(2,128)(2,1)} %reshape_squeeze.3), calls=%async_computation | async-start | bytes 655360 | tf_op jit(solution)/shard_map/all_to_all | solution.py:40
  21.4 3.2 sort.17
  24.6 1.9 slice_reduce_fusion.25
  26.5 0.7 compare_select_fusion
  27.1 83.8 %all-gather.3.cloned.1.call-done = bf16[64,20,3840]{2,1,0:T(8,128)(2,1)} async-done(((bf16[1,20,3840]{2,1,0:T(8,128)(2,1)}), bf16[64,20,3840]{2,1,0:T(8,128)(2,1)}) %all-gather.3.cloned.1.call-update) | async-done | bytes 9830416 | tf_op jit(solution)/shard_map/all_gather | solution.py:114
  110.9 13.7 %reshape.119 = bf16[1280,3840]{1,0:T(8,128)(2,1)} reshape(bf16[64,20,3840]{2,1,0:T(8,128)(2,1)} %all-gather.3.cloned.1.call-done) | data formatting | bytes 19660800
  124.6 0.0 copy-done
  124.6 7.1 %convolution_convert_fusion.1 = bf16[128,1280]{1,0:T(8,128)(2,1)S(1)} fusion(bf16[1280,3840]{1,0:T(8,128)(2,1)} %reshape.119, bf16[1,128,3840]{2,1,0:T(8,128)(2,1)S(1)} %copy-done), kind=kOutput, calls=%fused_computation.41 | convolution fusion | flops 1258455040 | bytes 11141120 | tf_op jit(solution)/shard_map/dot_general | solution.py:97
  131.7 0.9 reshape.77
  132.6 0.0 all-to-all-done
  132.6 5.7 %all-to-all-start.2 = ((bf16[64,2,1280]{2,1,0:T(2,128)(2,1)}), bf16[64,2,1280]{2,1,0:T(2,128)(2,1)S(1)}, u32[]{:S(2)}, u32[]{:S(2)}) async-start(bf16[64,2,1280]{2,1,0:T(2,128)(2,1)} %reshape.77), calls=%async_computation.2 | async-start | bytes 655360 | tf_op jit(solution)/shard_map/all_to_all | solution.py:40
  138.3 0.6 pad_clamp_fusion
  138.8 0.9 slice_reduce_fusion.26
  139.7 0.0 copy-done.19
  139.7 0.5 compare_and_fusion
  140.2 0.1 reshape.72
  140.3 0.9 gather_fusion
  141.2 11.2 %all-to-all-done.2 = bf16[64,2,1280]{2,1,0:T(2,128)(2,1)S(1)} async-done(((bf16[64,2,1280]{2,1,0:T(2,128)(2,1)}), bf16[64,2,1280]{2,1,0:T(2,128)(2,1)S(1)}, u32[]{:S(2)}, u32[]{:S(2)}) %all-to-all-start.2) | async-done | bytes 327712 | tf_op jit(solution)/shard_map/all_to_all | solution.py:40
  152.4 0.1 reshape.78
  152.6 0.9 gather_fusion.2
  153.6 0.8 multiply_reduce_fusion
  154.4 2.1 collective-permute-start.1
  156.5 3.5 collective-permute-start
  160.0 0.7 slice_bitcast_fusion.1
  160.7 1.9 collective-permute-start.2
  162.7 3.1 collective-permute-start.3
  165.7 0.0 collective-permute-done.1
  165.7 0.0 collective-permute-done
  165.8 0.6 select_maximum_fusion.2
  166.5 2.5 fusion.83
  168.9 0.0 copy-done.1
  169.0 0.0 copy-done.3
  169.0 1.7 gather_fusion.1
  170.7 0.0 collective-permute-done.2
  170.7 0.0 collective-permute-done.3
  170.7 1.5 select_maximum_fusion
  172.2 3.4 add_convert_fusion
  175.7 1.9 gather_fusion.3
  177.5 1.9 broadcast_select_fusion
  179.4 1.8 reshape.75
  181.3 9.7 %all-to-all-start.1 = ((bf16[64,2,1280]{2,1,0:T(2,128)(2,1)}), bf16[64,2,1280]{2,1,0:T(2,128)(2,1)}, u32[]{:S(2)}, u32[]{:S(2)}) async-start(bf16[64,2,1280]{2,1,0:T(2,128)(2,1)} %reshape.75), calls=%async_computation.1 | async-start | bytes 655360 | tf_op jit(solution)/shard_map/all_to_all | solution.py:51
  190.9 0.6 stack.97
  191.5 0.8 reshape.81
  192.4 2.4 fusion.82
  194.8 10.2 %all-to-all-done.1 = bf16[64,2,1280]{2,1,0:T(2,128)(2,1)} async-done(((bf16[64,2,1280]{2,1,0:T(2,128)(2,1)}), bf16[64,2,1280]{2,1,0:T(2,128)(2,1)}, u32[]{:S(2)}, u32[]{:S(2)}) %all-to-all-start.1) | async-done | bytes 327712 | tf_op jit(solution)/shard_map/all_to_all | solution.py:51
  205.0 5.2 %all-to-all-start.3 = ((bf16[64,2,1280]{2,1,0:T(2,128)(2,1)}), bf16[64,2,1280]{2,1,0:T(2,128)(2,1)}, u32[]{:S(2)}, u32[]{:S(2)}) async-start(bf16[64,2,1280]{2,1,0:T(2,128)(2,1)} %reshape.81), calls=%async_computation.3 | async-start | bytes 655360 | tf_op jit(solution)/shard_map/all_to_all | solution.py:51
  210.3 0.0 all-reduce.4.cloned.1.call-start
  210.3 1.5 fusion.78
  211.9 0.7 stack.110
  212.7 0.7 stack.109
  213.4 0.7 stack.108
  214.1 0.7 stack.107
  215.0 3.4 stack.111
  218.3 0.0 all-reduce.4.cloned.1.call-update
  218.4 1.1 reshape.76
  219.5 6.2 %fusion = bf16[1,128,3840]{2,1,0:T(8,128)(2,1)} fusion(bf16[128,1280]{1,0:T(8,128)(2,1)S(1)} %reshape.76, bf16[1280,3840]{1,0:T(8,128)(2,1)} %reshape.119), kind=kOutput, calls=%fused_computation.37 | convolution fusion | flops 1258782720 | bytes 11141120 | tf_op jit(solution)/shard_map/dot_general | solution.py:112
  225.7 0.0 all-to-all-done.3
  225.7 1.8 broadcast_in_dim_reshape.3
  227.5 255.8 %all-reduce.4.cloned.1.call-done = f32[27,1280]{1,0:T(8,128)} async-done(((f32[27,1280]{1,0:T(8,128)}), f32[27,1280]{1,0:T(8,128)}) %all-reduce.4.cloned.1.call-update) | async-done | bytes 138256 | tf_op jit(solution)/shard_map/psum | solution.py:118
  483.3 1.6 copy.9
  (62 shorter events, 0.2 us)
Async XLA Ops:
  7.2 117.5 %copy-start = (bf16[1,128,3840]{2,1,0:T(8,128)(2,1)S(1)}, bf16[1,128,3840]{2,1,0:T(8,128)(2,1)}, u32[]{:S(2)}) copy-start(bf16[1,128,3840]{2,1,0:T(8,128)(2,1)} %param.11) | copy-start | bytes 2949124
  7.2 103.8 %all-gather.3.cloned.1.call-start = ((), (), s32[]{:S(2)}) async-start(), calls=%async_computation.5 | async-start | bytes 11980800 | tf_op jit(solution)/shard_map/all_gather | solution.py:114
  9.7 122.8 %all-to-all-start = ((bf16[64,2,1280]{2,1,0:T(2,128)(2,1)}), bf16[64,2,1280]{2,1,0:T(2,128)(2,1)S(1)}, u32[]{:S(2)}, u32[]{:S(2)}) async-start(bf16[64,2,1280]{2,1,0:T(2,128)(2,1)} %reshape_squeeze.3), calls=%async_computation | async-start | bytes 655360 | tf_op jit(solution)/shard_map/all_to_all | solution.py:40
  124.6 14.2 %copy-start.4 = (f32[27,1280]{1,0:T(8,128)S(1)}, f32[27,1280]{1,0:T(8,128)}, u32[]{:S(2)}) copy-start(f32[27,1280]{1,0:T(8,128)} %param.9) | copy-start | bytes 414724
  124.6 15.1 %copy-start.19 = (s32[1,128]{1,0:T(1,128)S(1)}, s32[1,128]{1,0:T(1,128)}, u32[]{:S(2)}) copy-start(s32[1,128]{1,0:T(1,128)} %param.8) | copy-start | bytes 1540
  132.6 19.9 %all-to-all-start.2 = ((bf16[64,2,1280]{2,1,0:T(2,128)(2,1)}), bf16[64,2,1280]{2,1,0:T(2,128)(2,1)S(1)}, u32[]{:S(2)}, u32[]{:S(2)}) async-start(bf16[64,2,1280]{2,1,0:T(2,128)(2,1)} %reshape.77), calls=%async_computation.2 | async-start | bytes 655360 | tf_op jit(solution)/shard_map/all_to_all | solution.py:40
  153.5 12.9 %copy-start.5 = (f32[1280]{0:T(1024)S(1)}, f32[1280]{0:T(1024)}, u32[]{:S(2)}) copy-start(f32[1280]{0:T(1024)} %get-tuple-element.52) | copy-start | bytes 15364
  153.5 12.9 %copy-start.6 = (f32[1280]{0:T(1024)S(1)}, f32[1280]{0:T(1024)}, u32[]{:S(2)}) copy-start(f32[1280]{0:T(1024)} %get-tuple-element.53) | copy-start | bytes 15364
  153.5 12.9 %copy-start.7 = (f32[1280]{0:T(1024)S(1)}, f32[1280]{0:T(1024)}, u32[]{:S(2)}) copy-start(f32[1280]{0:T(1024)} %get-tuple-element.54) | copy-start | bytes 15364
  153.5 12.9 %copy-start.8 = (f32[1280]{0:T(1024)S(1)}, f32[1280]{0:T(1024)}, u32[]{:S(2)}) copy-start(f32[1280]{0:T(1024)} %get-tuple-element.55) | copy-start | bytes 15364
  153.5 12.9 %copy-start.9 = (f32[1280]{0:T(1024)S(1)}, f32[1280]{0:T(1024)}, u32[]{:S(2)}) copy-start(f32[1280]{0:T(1024)} %get-tuple-element.56) | copy-start | bytes 15364
  153.5 12.9 %copy-start.10 = (f32[1280]{0:T(1024)S(1)}, f32[1280]{0:T(1024)}, u32[]{:S(2)}) copy-start(f32[1280]{0:T(1024)} %get-tuple-element.57) | copy-start | bytes 15364
  153.5 12.9 %copy-start.11 = (f32[1280]{0:T(1024)S(1)}, f32[1280]{0:T(1024)}, u32[]{:S(2)}) copy-start(f32[1280]{0:T(1024)} %get-tuple-element.58) | copy-start | bytes 15364
  153.5 12.9 %copy-start.12 = (f32[1280]{0:T(1024)S(1)}, f32[1280]{0:T(1024)}, u32[]{:S(2)}) copy-start(f32[1280]{0:T(1024)} %get-tuple-element.59) | copy-start | bytes 15364
  153.5 12.9 %copy-start.13 = (f32[1280]{0:T(1024)S(1)}, f32[1280]{0:T(1024)}, u32[]{:S(2)}) copy-start(f32[1280]{0:T(1024)} %get-tuple-element.60) | copy-start | bytes 15364
  153.6 12.9 %copy-start.14 = (f32[1280]{0:T(1024)S(1)}, f32[1280]{0:T(1024)}, u32[]{:S(2)}) copy-start(f32[1280]{0:T(1024)} %get-tuple-element.61) | copy-start | bytes 15364
  153.6 12.9 %copy-start.15 = (f32[1280]{0:T(1024)S(1)}, f32[1280]{0:T(1024)}, u32[]{:S(2)}) copy-start(f32[1280]{0:T(1024)} %get-tuple-element.62) | copy-start | bytes 15364
  153.6 12.9 %copy-start.16 = (f32[1280]{0:T(1024)S(1)}, f32[1280]{0:T(1024)}, u32[]{:S(2)}) copy-start(f32[1280]{0:T(1024)} %get-tuple-element.63) | copy-start | bytes 15364
  153.6 12.9 %copy-start.17 = (f32[1280]{0:T(1024)S(1)}, f32[1280]{0:T(1024)}, u32[]{:S(2)}) copy-start(f32[1280]{0:T(1024)} %get-tuple-element.64) | copy-start | bytes 15364
  154.4 14.5 %copy-start.1 = (bf16[128,1280]{1,0:T(8,128)(2,1)}, bf16[128,1280]{1,0:T(8,128)(2,1)S(1)}, u32[]{:S(2)}) copy-start(bf16[128,1280]{1,0:T(8,128)(2,1)S(1)} %get-tuple-element.67) | copy-start | bytes 983044
  154.4 11.3 %collective-permute-start.1 = (bf16[1,8,8,1280]{3,2,1,0:T(8,128)(2,1)S(1)}, bf16[1,8,8,1280]{3,2,1,0:T(8,128)(2,1)S(1)}, u32[]{:S(2)}, u32[]{:S(2)}) collective-permute-start(bf16[1,8,8,1280]{3,2,1,0:T(8,128)(2,1)S(1)} %get-tuple-element.70), channel_id=1, source_target_pairs={{1,0},{2,1},{3,2},{4,3},{5,4},{6,5},{7,6},{8,7},{9,8},{10,9},{11,1... | collective-permute-start | bytes 491528 | tf_op jit(solution)/shard_map/ppermute | solution.py:18
  156.5 9.2 %collective-permute-start = (bf16[1,8,8,1280]{3,2,1,0:T(8,128)(2,1)S(1)}, bf16[1,8,8,1280]{3,2,1,0:T(8,128)(2,1)S(1)}, u32[]{:S(2)}, u32[]{:S(2)}) collective-permute-start(bf16[1,8,8,1280]{3,2,1,0:T(8,128)(2,1)S(1)} %get-tuple-element.71), channel_id=1, source_target_pairs={{0,1},{1,2},{2,3},{3,4},{4,5},{5,6},{6,7},{7,8},{8,9},{9,10},{10,1... | collective-permute-start | bytes 491528 | tf_op jit(solution)/shard_map/ppermute | solution.py:17
  160.7 10.0 %collective-permute-start.2 = (bf16[1,8,8,1280]{3,2,1,0:T(8,128)(2,1)}, bf16[1,8,8,1280]{3,2,1,0:T(8,128)(2,1)}, u32[]{:S(2)}, u32[]{:S(2)}) collective-permute-start(bf16[1,8,8,1280]{3,2,1,0:T(8,128)(2,1)} %get-tuple-element.68), channel_id=1, source_target_pairs={{0,1},{1,2},{2,3},{3,4},{4,5},{5,6},{6,7},{7,8},{8,9},{9,10},{10,1... | collective-permute-start | bytes 491528 | tf_op jit(solution)/shard_map/ppermute | solution.py:17
  162.7 8.0 %collective-permute-start.3 = (bf16[1,8,8,1280]{3,2,1,0:T(8,128)(2,1)}, bf16[1,8,8,1280]{3,2,1,0:T(8,128)(2,1)}, u32[]{:S(2)}, u32[]{:S(2)}) collective-permute-start(bf16[1,8,8,1280]{3,2,1,0:T(8,128)(2,1)} %get-tuple-element.69), channel_id=1, source_target_pairs={{1,0},{2,1},{3,2},{4,3},{5,4},{6,5},{7,6},{8,7},{9,8},{10,9},{11,1... | collective-permute-start | bytes 491528 | tf_op jit(solution)/shard_map/ppermute | solution.py:18
  165.7 3.2 copy-start.3
  175.6 15.3 %copy-start.18 = (f32[1280]{0:T(1024)S(1)}, f32[1280]{0:T(1024)}, u32[]{:S(2)}) copy-start(f32[1280]{0:T(1024)} %get-tuple-element.65) | copy-start | bytes 15364
  181.3 23.8 %all-to-all-start.1 = ((bf16[64,2,1280]{2,1,0:T(2,128)(2,1)}), bf16[64,2,1280]{2,1,0:T(2,128)(2,1)}, u32[]{:S(2)}, u32[]{:S(2)}) async-start(bf16[64,2,1280]{2,1,0:T(2,128)(2,1)} %reshape.75), calls=%async_computation.1 | async-start | bytes 655360 | tf_op jit(solution)/shard_map/all_to_all | solution.py:51
  192.4 18.0 %copy-start.2 = (bf16[128,1280]{1,0:T(8,128)(2,1)S(1)}, bf16[128,1280]{1,0:T(8,128)(2,1)}, u32[]{:S(2)}) copy-start(bf16[128,1280]{1,0:T(8,128)(2,1)} %copy-done.1) | copy-start | bytes 983044
  205.0 20.6 %all-to-all-start.3 = ((bf16[64,2,1280]{2,1,0:T(2,128)(2,1)}), bf16[64,2,1280]{2,1,0:T(2,128)(2,1)}, u32[]{:S(2)}, u32[]{:S(2)}) async-start(bf16[64,2,1280]{2,1,0:T(2,128)(2,1)} %reshape.81), calls=%async_computation.3 | async-start | bytes 655360 | tf_op jit(solution)/shard_map/all_to_all | solution.py:51
  210.3 273.0 %all-reduce.4.cloned.1.call-start = ((), (), s32[]{:S(2)}) async-start(), calls=%async_computation.4 | async-start | bytes 327680 | tf_op jit(solution)/shard_map/psum | solution.py:118
Sparse Core Ops, SparseCore 0:
  11.3 99.6 all-gather.2
  218.5 264.7 all-reduce.3
where the time goes:
time: 493 us; the launch traced here: 492 us
  waiting for transfers between devices  362 us (73%)
  starting transfers between devices  42.8 us (9%)
  local copies, waits for them, and re-layouts  39.6 us (8%)
  other arithmetic  19.6 us (4%)
  between operations  14.6 us (3%)
  matrix products  13.3 us (3%)
    psum x1, waiting for transfers between devices, shards(): d_kernel = lax.psum(partial_value, ('dp', 'seq'))  256 us
    all_gather x1, waiting for transfers between devices, shards(): lax.all_gather(proj_weight, 'seq', axis=0, tiled=True)  83.8 us
    all_to_all x2, starting transfers between devices, to_bricks(): lax.all_to_all(rows.reshape(count, tokens_dev // count, width), 'seq', sp...  17.3 us
    unnamed x42, local copies, waits for them, and re-layouts  15.4 us
    all_to_all x2, starting transfers between devices, to_scan(): lax.all_to_all(scan_pieces(cells, order, count), 'seq', split_axis=0, con...  14.9 us
    all_to_all x2, waiting for transfers between devices, to_bricks(): lax.all_to_all(rows.reshape(count, tokens_dev // count, width), 'seq', sp...  11.2 us
    all_to_all x2, waiting for transfers between devices, to_scan(): lax.all_to_all(scan_pieces(cells, order, count), 'seq', split_axis=0, con...  10.3 us
  transfers between devices with their start and end apart: 10, of which 4 were waited for; matrix products, arithmetic and copies ran while one was open for 12% of the time, Pallas kernels for 0%

commit v1 on v0

v1 whole, which is shorter than its diff:
```python
import functools

import jax
import jax.numpy as jnp
import numpy as np
from jax import lax
from jax.experimental import pallas as pl
from jax.experimental.pallas import tpu as pltpu
from jax.sharding import Mesh
from jax.sharding import PartitionSpec as P

NY, NX, NC = 8, 4, 2
CHIPS = NY * NX
LAYER = 64
BF16, F32 = jnp.bfloat16, jnp.float32


def swap(value):
    return lax.ppermute(value, "c", [(0, 1), (1, 0)])


def in_order(core, own, other, axis):
    first = jnp.where(core == 0, own, other)
    second = jnp.where(core == 0, other, own)
    return jnp.concatenate([first, second], axis=axis)


def half(value, core):
    width = value.shape[-1] // 2
    return lax.dynamic_slice_in_dim(value, core * width, width, axis=value.ndim - 1)


def spread(value, axis, size):
    return lax.all_to_all(
        jnp.broadcast_to(value[None], (size, *value.shape)), axis, 0, 0, tiled=True
    )


def shift(value, axis, size, step):
    return lax.ppermute(value, axis, [(i, (i + step) % size) for i in range(size)])


def weight_pieces(block):
    rows = block.shape[0] // 2
    up, down = block, block
    pieces = [block]
    for _ in range(3):
        up, down = shift(up, "y", NY, 1), shift(down, "y", NY, -1)
        pieces += [up, down]
    pieces += [shift(up[:rows], "y", NY, 1), shift(down[rows:], "y", NY, -1)]
    return pieces


def assemble(y_ref, pieces, weight, sems):
    rows = pieces[0].shape[0]
    places = [(0, 0), (-1, 0), (1, 0), (-2, 0), (2, 0), (-3, 0), (3, 0), (4, 0), (4, rows // 2)]
    copies = []
    for i, (piece, (step, skip)) in enumerate(zip(pieces, places)):
        at = lax.rem(y_ref[0] + step + NY, NY) * rows + skip
        at = pl.multiple_of(at, 16)
        copies.append(
            pltpu.make_async_copy(piece, weight.at[pl.ds(at, piece.shape[0])], sems.at[i])
        )
    for copy in copies:
        copy.start()
    return copies


def weight_call(body, pieces, out_shape, vmem):
    columns = pieces[0].shape[1]
    total = pieces[0].shape[0] * NY
    return pl.pallas_call(
        body,
        out_shape=out_shape,
        in_specs=[pl.BlockSpec(memory_space=pltpu.SMEM), pl.BlockSpec(memory_space=pltpu.VMEM)]
        + [pl.BlockSpec(memory_space=pl.ANY)] * len(pieces),
        scratch_shapes=[
            pltpu.VMEM((total, columns), BF16),
            pltpu.SemaphoreType.DMA((len(pieces),)),
        ],
        compiler_params=pltpu.CompilerParams(vmem_limit_bytes=vmem),
        cost_estimate=pl.CostEstimate(
            flops=2 * 256 * total * columns, bytes_accessed=8_000_000, transcendentals=0
        ),
    )


def back_kernel(where_ref, rows_ref, *refs):
    pieces, (keep_ref, send_ref, weight, sems) = refs[:9], refs[9:]
    for copy in assemble(where_ref, pieces, weight, sems):
        copy.wait()
    width = keep_ref.shape[1]
    core = where_ref[1]
    for out, which in ((send_ref, 1 - core), (keep_ref, core)):
        for at, size in ((0, 256), (256, 256), (512, 128)):
            start = pl.multiple_of(which * width + at, 128)
            out[:, at : at + size] = lax.dot_general(
                rows_ref[...],
                weight[pl.ds(start, size), :],
                (((1,), (1,)), ((), ())),
                preferred_element_type=F32,
            )


def forward_kernel(where_ref, rows_ref, *refs):
    pieces, (out_ref, weight, sems) = refs[:9], refs[9:]
    for copy in assemble(where_ref, pieces, weight, sems):
        copy.wait()
    for at in range(0, out_ref.shape[1], 384):
        out_ref[:, at : at + 384] = jnp.dot(
            rows_ref[...], weight[:, at : at + 384], preferred_element_type=F32
        ).astype(BF16)


def cells_kernel(cell_ref, rows_ref, out_ref):
    count = rows_ref.shape[0]
    pick = lax.broadcasted_iota(jnp.int32, (count, count), 0) == cell_ref[...]
    pick = jnp.where(pick, 1.0, 0.0).astype(BF16)
    out_ref[...] = jnp.dot(pick, rows_ref[...], preferred_element_type=F32).astype(BF16)


def to_cells(rows, cell_row):
    return pl.pallas_call(
        cells_kernel,
        out_shape=jax.ShapeDtypeStruct(rows.shape, BF16),
        in_specs=[pl.BlockSpec(memory_space=pltpu.VMEM)] * 2,
        out_specs=pl.BlockSpec(memory_space=pltpu.VMEM),
    )(cell_row, rows)


def fill(before_ref, cells_ref, after_ref, field):
    parts = (before_ref[...], cells_ref[...], after_ref[...])
    lanes = cells_ref.shape[1]
    wide = jnp.concatenate([p.astype(F32) for p in parts], axis=0)
    wide = wide.reshape(6 * 8, 8, lanes)
    column = lax.broadcasted_iota(jnp.int32, wide.shape, 1)
    lower = jnp.where(column == 0, 0.0, jnp.roll(wide, 1, axis=1))
    upper = jnp.where(column == 7, 0.0, jnp.roll(wide, -1, axis=1))
    zero = jnp.zeros((6, 1, 8, lanes), F32)
    for s, value in enumerate((lower, wide, upper)):
        field[s, :, 0:1] = zero
        field[s, :, 9:10] = zero
        field[s, :, 1:9] = value.reshape(6, 8, 8, lanes)


def conv_kernel(cell_ref, kernel_ref, before_ref, cells_ref, after_ref, out_ref, field):
    fill(before_ref, cells_ref, after_ref, field)
    count, lanes = cells_ref.shape
    layers = []
    for z in range(4):
        total = jnp.zeros((8, 8, lanes), F32)
        for o in range(27):
            dz, di, dc = o // 9, o // 3 % 3, o % 3
            total = total + kernel_ref[o : o + 1, :][None] * field[dc, z + dz, di : di + 8]
        layers.append(total)
    conv = jnp.stack(layers).reshape(count, lanes)
    result = (cells_ref[...].astype(F32) + conv).astype(BF16)
    pick = lax.broadcasted_iota(jnp.int32, (count, count), 1) == cell_ref[...]
    pick = jnp.where(pick, 1.0, 0.0).astype(BF16)
    out_ref[...] = jnp.dot(pick, result, preferred_element_type=F32).astype(BF16)


def tall(rows, lanes=128):
    return pl.BlockSpec((rows, lanes), lambda t: (0, t))


def conv_rows(cells, before, after, kernel, cell_column):
    count, width = cells.shape
    return pl.pallas_call(
        conv_kernel,
        out_shape=jax.ShapeDtypeStruct(cells.shape, BF16),
        grid=(width // 128,),
        in_specs=[
            pl.BlockSpec((count, 1), lambda t: (0, 0)),
            tall(kernel.shape[0]),
            tall(LAYER),
            tall(count),
            tall(LAYER),
        ],
        out_specs=tall(count),
        scratch_shapes=[pltpu.VMEM((3, 6, 10, 8, 128), F32)],
    )(cell_column, kernel, before, cells, after)


def grad_kernel(grad_ref, before_ref, cells_ref, after_ref, out_ref, field):
    fill(before_ref, cells_ref, after_ref, field)
    lanes = cells_ref.shape[1]
    grad = grad_ref[...].astype(F32).reshape(4, 8, 8, lanes)
    sums = []
    for o in range(27):
        dz, di, dc = o // 9, o // 3 % 3, o % 3
        part = grad * field[dc, dz : dz + 4, di : di + 8]
        sums.append(jnp.sum(part.reshape(32, 8, lanes), axis=0))
    sums += [jnp.zeros((8, lanes), F32)] * 5
    out_ref[...] = jnp.sum(jnp.stack(sums), axis=1)


def kernel_grad(grad, cells, before, after):
    count, width = cells.shape
    return pl.pallas_call(
        grad_kernel,
        out_shape=jax.ShapeDtypeStruct((32, width), F32),
        grid=(width // 128,),
        in_specs=[tall(count), tall(LAYER), tall(count), tall(LAYER)],
        out_specs=tall(32),
        scratch_shapes=[pltpu.VMEM((3, 6, 10, 8, 128), F32)],
    )(grad, before, cells, after)


def to_bricks(rows):
    width = rows.shape[-1]
    sent = rows.reshape(2, CHIPS, 4, width).transpose(1, 0, 2, 3).reshape(CHIPS, 8, width)
    return lax.all_to_all(sent, ("y", "x"), 0, 0, tiled=True).reshape(CHIPS * 8, width)


def to_scan(rows):
    width = rows.shape[-1]
    landed = lax.all_to_all(rows.reshape(CHIPS, 8, width), ("y", "x"), 0, 0, tiled=True)
    return landed.reshape(CHIPS, 2, 4, width).transpose(1, 0, 2, 3).reshape(2, 4 * CHIPS, width)


def faces(cells):
    up = [(i, i + 1) for i in range(CHIPS - 1)]
    down = [(j, i) for i, j in up]
    before = lax.ppermute(cells[-LAYER:], ("y", "x"), up)
    after = lax.ppermute(cells[:LAYER], ("y", "x"), down)
    return before, after


def shards(planes, tokens, place, kernel, proj_weight, d_projected):
    core = lax.axis_index("c")
    rows_x, rows_d = tokens[0], d_projected[0]
    where = jnp.stack([lax.axis_index("y"), core]).astype(jnp.int32)

    places = in_order(core, place, swap(place), 0)
    cell = places.reshape(2, CHIPS, 2, 2) + jnp.array([0, 128], jnp.int32)[:, None, None, None]
    cell = cell.transpose(1, 2, 0, 3).reshape(4 * CHIPS * 2)
    cell_row, cell_column = cell[None, :], cell[:, None]

    block = in_order(core, half(proj_weight, core), swap(half(proj_weight, 1 - core)), 0)
    block = spread(block, "x", NX).reshape(NX * block.shape[0], block.shape[1])
    pieces = weight_pieces(block)

    d_pair = in_order(core, half(rows_d, core), swap(half(rows_d, 1 - core)), 0)
    x_pair = in_order(core, half(rows_x, core)[None], swap(half(rows_x, 1 - core))[None], 0)
    kern = half(kernel, core)

    cells_x = to_cells(to_bricks(x_pair), cell_row)
    before_x, after_x = faces(cells_x)
    rows_y = conv_rows(cells_x, before_x, after_x, kern, cell_column)
    y_half = to_scan(rows_y)
    y_full = in_order(core, y_half, swap(y_half), 2)
    y_full = y_full.reshape(-1, y_full.shape[-1])

    count, width = y_full.shape
    part = jax.ShapeDtypeStruct((count, width // 2), F32)
    keep, send = weight_call(back_kernel, pieces, (part, part), 40 << 20)(where, d_pair, *pieces)
    d_y = (keep + swap(send)).astype(BF16)
    cells_d = to_cells(to_bricks(d_y.reshape(2, count // 2, width // 2)), cell_row)
    before_d, after_d = faces(cells_d)
    partial_value = kernel_grad(cells_d, cells_x, before_x, after_x)
    back = conv_rows(cells_d, before_d, after_d, kern[::-1], cell_column)
    d_half = to_scan(back)
    d_own = lax.dynamic_index_in_dim(d_half, core, 0, keepdims=False)
    d_other = swap(lax.dynamic_index_in_dim(d_half, 1 - core, 0, keepdims=False))
    d_tokens = in_order(core, d_own, d_other, 1)

    tiles = partial_value.reshape(4, 8, 5, 128).transpose(0, 2, 1, 3)
    tiles = jnp.sum(lax.all_to_all(tiles, "x", 0, 0, tiled=True).reshape(NX, 5, 8, 128), axis=0)
    tiles = jnp.sum(spread(tiles, "y", NY), axis=0)
    if planes > 1:
        tiles = jnp.sum(spread(tiles, "z", planes), axis=0)
    tiles = spread(tiles, ("x", "c"), NX * NC).reshape(NX, NC, 5, 8, 128)
    d_kernel = tiles.transpose(0, 3, 1, 2, 4).reshape(32, 1280)[: kernel.shape[0]]

    columns = pieces[0].shape[1]
    out = jax.ShapeDtypeStruct((count, columns), BF16)
    p_pair = weight_call(forward_kernel, pieces, out, 40 << 20)(where, y_full, *pieces)
    p_pair = p_pair.reshape(2, count // 2, columns)
    p_own = lax.dynamic_index_in_dim(p_pair, core, 0, keepdims=False)
    p_other = swap(lax.dynamic_index_in_dim(p_pair, 1 - core, 0, keepdims=False))
    projected = in_order(core, p_own, p_other, 1)
    return projected[None], d_tokens[None], d_kernel


def solution(mesh):
    planes = mesh.shape["dp"]
    devices = np.asarray(mesh.devices).reshape(planes, NY, NX, NC)
    grid = Mesh(devices, ("z", "y", "x", "c"))
    seq = ("y", "x", "c")
    return jax.shard_map(
        functools.partial(shards, planes),
        mesh=grid,
        in_specs=(P("z", seq, None), P(seq, None), P(), P(seq, None), P("z", seq, None)),
        out_specs=(P("z", seq, None), P("z", seq, None), P()),
        check_vma=False,
    )
```

time: 493 us -> 254 us (0.52)
  waiting for transfers between devices: 362 us -> 52.2 us
  starting transfers between devices: 42.8 us -> 127 us
  Pallas kernels: 0 us -> 27.3 us
  local copies, waits for them, and re-layouts: 39.6 us -> 22.9 us
  matrix products: 13.3 us -> 0 us
  between operations: 14.6 us -> 1.3 us
  blocking collectives: 0 us -> 12.7 us
  other arithmetic: 19.6 us -> 8.42 us
    psum x1 -> x0, waiting for transfers between devices: 256 us -> none  [shards(): d_kernel = lax.psum(partial_value, ('dp', 'seq'))]
    all_gather x1 -> x0, waiting for transfers between devices: 83.8 us -> none  [shards(): lax.all_gather(proj_weight, 'seq', axis=0, tiled=True)]
    ppermute x4 -> x20, starting transfers between devices: 10.5 us -> 71.1 us  [the longest x8 38.3 us: swap(): return lax.ppermute(value, 'c', [(0, 1), (1, 0)])]
    pallas_call x0 -> x7, Pallas kernels: none -> 27.3 us  [the longest x2 9.67 us: conv_rows(): pl.pallas_call(conv_kernel, out_shape=jax.ShapeDtypeStruct(cells.shape, B...]
    ppermute x4 -> x20, waiting for transfers between devices: 0.01 us -> 24.2 us  [the longest x8 16.8 us: shift(): lax.ppermute(value, axis, [(i, (i + step) % size) for i in range(size)])]
    all_to_all x4 -> x8, starting transfers between devices: 32.2 us -> 56 us  [the longest x2 23 us: to_scan(): lax.all_to_all(rows.reshape(CHIPS, 8, width), ('y', 'x'), 0, 0, tiled=True)]
    dot_general x2 -> x0, matrix products: 13.3 us -> none  [the longest x1 7.08 us: shards(): lax.dot_general(d_rows, lax.all_gather(proj_weight, 'seq', axis=0, tiled=...]
    all_to_all x0 -> x1, blocking collectives: none -> 12.7 us  [spread(): lax.all_to_all(jnp.broadcast_to(value[None], (size, *value.shape)), axis,...]
  transfers between devices with their start and end apart: 10 -> 28, of which waited for: 4 -> 13; matrix products, arithmetic and copies ran while one was open for 12% -> 7% of each run, Pallas kernels for 0% -> 6%
where the time goes in v1:
time: 254 us; the launch traced here: 252 us
  starting transfers between devices  127 us (50%)
  waiting for transfers between devices  52.2 us (21%)
  Pallas kernels  27.3 us (11%)
  local copies, waits for them, and re-layouts  22.9 us (9%)
  blocking collectives  12.7 us (5%)
  other arithmetic  8.42 us (3%)
    ppermute x8, starting transfers between devices, swap(): return lax.ppermute(value, 'c', [(0, 1), (1, 0)])  38.3 us
    ppermute x8, starting transfers between devices, shift(): lax.ppermute(value, axis, [(i, (i + step) % size) for i in range(size)])  25.9 us
    all_to_all x2, starting transfers between devices, to_scan(): lax.all_to_all(rows.reshape(CHIPS, 8, width), ('y', 'x'), 0, 0, tiled=True)  23 us
    all_to_all x3, starting transfers between devices, spread(): lax.all_to_all(jnp.broadcast_to(value[None], (size, *value.shape)), axis,...  19.3 us
    all_to_all x2, waiting for transfers between devices, to_scan(): lax.all_to_all(rows.reshape(CHIPS, 8, width), ('y', 'x'), 0, 0, tiled=True)  18.8 us
    ppermute x8, waiting for transfers between devices, shift(): lax.ppermute(value, axis, [(i, (i + step) % size) for i in range(size)])  16.8 us
    all_to_all x1, blocking collectives, spread(): lax.all_to_all(jnp.broadcast_to(value[None], (size, *value.shape)), axis,...  12.7 us
    all_to_all x2, starting transfers between devices, to_bricks(): lax.all_to_all(sent, ('y', 'x'), 0, 0, tiled=True).reshape(CHIPS * 8, width)  9.83 us
  transfers between devices with their start and end apart: 28, of which 13 were waited for; matrix products, arithmetic and copies ran while one was open for 7% of the time, Pallas kernels for 6%

profile of v1, /device:TPU:1, one launch (start us, length us, event | category | flops | bytes accessed | tf_op | source)
XLA Modules:
  0.0 251.9 jit_solution(1318564488475943992)
XLA Ops:
  0.7 0.9 constant_dynamic-slice_fusion
  1.6 8.8 %collective-permute-start.5 = (bf16[20,1920]{1,0:T(8,128)(2,1)S(1)}, bf16[20,1920]{1,0:T(8,128)(2,1)S(1)}, u32[]{:S(2)}, u32[]{:S(2)}) collective-permute-start(bf16[20,1920]{1,0:T(8,128)(2,1)S(1)} %constant_dynamic-slice_fusion), channel_id=1, source_target_pairs={{0,1},{1,0},{2,3},{3,2},{4,5},{5,4},{6,7},{7,6},{8,9},{9,8},{10,11... | collective-permute-start | bytes 230408 | tf_op jit(solution)/shard_map/ppermute | solution.py:19
  10.4 0.9 collective-permute-done.5
  11.3 0.9 broadcast_select_fusion.3
  12.3 12.7 %all_to_all.45 = bf16[4,40,1920]{2,1,0:T(8,128)(2,1)S(1)} all-to-all(bf16[4,40,1920]{2,1,0:T(8,128)(2,1)S(1)} %broadcast_in_dim.15), channel_id=1, replica_groups=mesh['z'=8,'y'=8,'x'=4,'c'=2] {'x'}, dimensions={0} | all-to-all | bytes 1228800 | tf_op jit(solution)/shard_map/all_to_all | solution.py:34
  25.1 1.9 collective-permute-start.6
  27.0 4.6 %collective-permute-start.7 = (bf16[160,1920]{1,0:T(8,128)(2,1)S(1)}, bf16[160,1920]{1,0:T(8,128)(2,1)S(1)}, u32[]{:S(2)}, u32[]{:S(2)}) collective-permute-start(bf16[160,1920]{1,0:T(8,128)(2,1)S(1)} %bitcast.51), channel_id=1, source_target_pairs={{0,56},{8,0},{16,8},{24,16},{32,24},{40,32},{48,40},{56,48},{1,57}... | collective-permute-start | bytes 1843208 | tf_op jit(solution)/shard_map/ppermute | solution.py:40
  31.6 10.8 %collective-permute-done.6.refs_1_ = bf16[160,1920]{1,0:T(8,128)(2,1)S(1)} collective-permute-done((bf16[160,1920]{1,0:T(8,128)(2,1)S(1)}, bf16[160,1920]{1,0:T(8,128)(2,1)S(1)}, u32[]{:S(2)}, u32[]{:S(2)}) %collective-permute-start.6) | collective-permute-done | bytes 614432 | tf_op jit(solution)/shard_map/ppermute | solution.py:40
  42.3 1.9 collective-permute-start.8
  44.3 4.6 %collective-permute-start.9 = (bf16[160,1920]{1,0:T(8,128)(2,1)S(1)}, bf16[160,1920]{1,0:T(8,128)(2,1)}, u32[]{:S(2)}, u32[]{:S(2)}) collective-permute-start(bf16[160,1920]{1,0:T(8,128)(2,1)S(1)} %collective-permute-done.7.refs_2_), channel_id=1, source_target_pairs={{0,56},{8,0},{16,8},{24,16},{32,24},{40,32},{48,40},{56,48},{1,57}... | collective-permute-start | bytes 1843208 | tf_op jit(solution)/shard_map/ppermute | solution.py:40
  49.7 4.6 %collective-permute-start.15 = (bf16[128,1920]{1,0:T(8,128)(2,1)}, bf16[128,1920]{1,0:T(8,128)(2,1)}, u32[]{:S(2)}, u32[]{:S(2)}) collective-permute-start(bf16[128,1920]{1,0:T(8,128)(2,1)} %dynamic-slice_bitcast_fusion), channel_id=1, source_target_pairs={{0,1},{1,0},{2,3},{3,2},{4,5},{5,4},{6,7},{7,6},{8,9},{9,8},{10,11... | collective-permute-start | bytes 1474568 | tf_op jit(solution)/shard_map/ppermute | solution.py:19
  54.3 1.9 collective-permute-start
  56.2 2.4 collective-permute-start.1
  58.8 1.9 collective-permute-start.10
  60.7 4.6 %collective-permute-start.11 = (bf16[160,1920]{1,0:T(8,128)(2,1)}, bf16[160,1920]{1,0:T(8,128)(2,1)S(1)}, u32[]{:S(2)}, u32[]{:S(2)}) collective-permute-start(bf16[160,1920]{1,0:T(8,128)(2,1)} %collective-permute-done.9.refs_4_), channel_id=1, source_target_pairs={{0,56},{8,0},{16,8},{24,16},{32,24},{40,32},{48,40},{56,48},{1,57}... | collective-permute-start | bytes 1843208 | tf_op jit(solution)/shard_map/ppermute | solution.py:40
  67.5 4.7 %all-to-all-start = ((bf16[32,8,640]{2,1,0:T(8,128)(2,1)}), bf16[32,8,640]{2,1,0:T(8,128)(2,1)}, u32[]{:S(2)}, u32[]{:S(2)}) async-start(bf16[32,8,640]{2,1,0:T(8,128)(2,1)} %reshape.72), calls=%async_computation | async-start | bytes 655360 | tf_op jit(solution)/shard_map/all_to_all | solution.py:213
  72.2 2.2 collective-permute-done.10.refs_5_
  75.2 1.9 collective-permute-start.12
  77.8 4.6 %collective-permute-start.13 = (bf16[80,1920]{1,0:T(8,128)(2,1)}, bf16[80,1920]{1,0:T(8,128)(2,1)}, u32[]{:S(2)}, u32[]{:S(2)}) collective-permute-start(bf16[80,1920]{1,0:T(8,128)(2,1)} %slice.31), channel_id=1, source_target_pairs={{0,56},{8,0},{16,8},{24,16},{32,24},{40,32},{48,40},{56,48},{1,57}... | collective-permute-start | bytes 921608 | tf_op jit(solution)/shard_map/ppermute | solution.py:40
  82.4 1.2 bitcast_select_fusion.1
  83.7 2.0 shard_map.85.cells_ref
  85.7 2.7 %collective-permute-done.12.refs_7_ = bf16[80,1920]{1,0:T(8,128)(2,1)S(1)} collective-permute-done((bf16[80,1920]{1,0:T(8,128)(2,1)}, bf16[80,1920]{1,0:T(8,128)(2,1)S(1)}, u32[]{:S(2)}, u32[]{:S(2)}) %collective-permute-start.12) | collective-permute-done | bytes 307232 | tf_op jit(solution)/shard_map/ppermute | solution.py:40
  88.4 1.2 collective-permute-done.13.refs_8_
  89.6 1.1 copy-done.3
  90.7 1.1 copy-done.6
  91.7 5.0 %shard_map.88 = (f32[256,640]{1,0:T(8,128)S(1)}, f32[256,640]{1,0:T(8,128)}) custom-call(s32[2]{0:T(128)S(1)} %pad_add_fusion.1.where_ref, bf16[256,1920]{1,0:T(8,128)(2,1)S(1)} %pad_maximum_fusion.rows_ref, bf16[160,1920]{1,0:T(8,128)(2,1)S(1)} %bitcast.52, bf16[160,1920]{1,0:T(8,128)(2,1)S(1)} %copy-done.3, bf16[160,1920]{1,0:T(8,128)(2,1)S(1)} %copy-done.6, ...), custom_call_target="tpu_custom_call" | custom-call | flops 1258291200 | bytes 8000000 | tf_op jit(solution)/shard_map/pallas_call | solution.py:257
  96.7 0.8 copy-done.8
  97.6 7.9 %collective-permute-start.16 = (f32[256,640]{1,0:T(8,128)}, f32[256,640]{1,0:T(8,128)}, u32[]{:S(2)}, u32[]{:S(2)}) collective-permute-start(f32[256,640]{1,0:T(8,128)} %get-tuple-element.6), channel_id=1, source_target_pairs={{0,1},{1,0},{2,3},{3,2},{4,5},{5,4},{6,7},{7,6},{8,9},{9,8},{10,11... | collective-permute-start | bytes 1966088 | tf_op jit(solution)/shard_map/ppermute | solution.py:19
  105.5 2.1 collective-permute-start.2
  107.6 1.3 collective-permute-start.3
  110.3 2.9 %collective-permute-done.3.after_ref = bf16[64,640]{1,0:T(8,128)(2,1)S(1)} collective-permute-done((bf16[64,640]{1,0:T(8,128)(2,1)S(1)}, bf16[64,640]{1,0:T(8,128)(2,1)S(1)}, u32[]{:S(2)}, u32[]{:S(2)}) %collective-permute-start.3) | collective-permute-done | bytes 81952 | tf_op jit(solution)/shard_map/ppermute | solution.py:226
  113.9 4.8 %shard_map.86 = bf16[256,640]{1,0:T(8,128)(2,1)} custom-call(s32[256,1]{1,0:T(8,128)} %broadcast_in_dim_reshape.8.cell_ref, f32[27,640]{1,0:T(8,128)} %constant_dynamic-slice_fusion.1.kernel_ref, bf16[64,640]{1,0:T(8,128)(2,1)} %copy-done.16, bf16[256,640]{1,0:T(8,128)(2,1)} %shard_map.85.cells_ref, bf16[64,640]{1,0:T(8,128)(2,1)} %copy-done.17), custom_call_target="tpu_custom_call" | custom-call | tf_op jit(solution)/shard_map/pallas_call | solution.py:169
  118.7 10.3 %all-to-all-start.1 = ((bf16[32,8,640]{2,1,0:T(8,128)(2,1)}), bf16[32,8,640]{2,1,0:T(8,128)(2,1)S(1)}, u32[]{:S(2)}, u32[]{:S(2)}) async-start(bf16[32,8,640]{2,1,0:T(8,128)(2,1)} %bitcast.59), calls=%async_computation.1 | async-start | bytes 655360 | tf_op jit(solution)/shard_map/all_to_all | solution.py:218
  129.0 1.9 add_convert_fusion
  131.0 1.1 reshape_reshape.3
  133.0 8.2 %all-to-all-done.1 = bf16[32,8,640]{2,1,0:T(8,128)(2,1)S(1)} async-done(((bf16[32,8,640]{2,1,0:T(8,128)(2,1)}), bf16[32,8,640]{2,1,0:T(8,128)(2,1)S(1)}, u32[]{:S(2)}, u32[]{:S(2)}) %all-to-all-start.1) | async-done | bytes 327712 | tf_op jit(solution)/shard_map/all_to_all | solution.py:218
  141.1 5.1 %all-to-all-start.3 = ((bf16[32,8,640]{2,1,0:T(8,128)(2,1)}), bf16[32,8,640]{2,1,0:T(8,128)(2,1)S(1)}, u32[]{:S(2)}, u32[]{:S(2)}) async-start(bf16[32,8,640]{2,1,0:T(8,128)(2,1)} %reshape.80), calls=%async_computation.3 | async-start | bytes 655360 | tf_op jit(solution)/shard_map/all_to_all | solution.py:213
  147.3 3.8 %collective-permute-start.4 = (bf16[2,128,640]{2,1,0:T(8,128)(2,1)}, bf16[2,128,640]{2,1,0:T(8,128)(2,1)}, u32[]{:S(2)}, u32[]{:S(2)}) collective-permute-start(bf16[2,128,640]{2,1,0:T(8,128)(2,1)} %reshape.76), channel_id=1, source_target_pairs={{0,1},{1,0},{2,3},{3,2},{4,5},{5,4},{6,7},{7,6},{8,9},{9,8},{10,11... | collective-permute-start | bytes 983048 | tf_op jit(solution)/shard_map/ppermute | solution.py:19
  151.1 1.6 collective-permute-done.4
  152.7 1.1 broadcast_select_fusion.1
  153.8 3.3 %all-to-all-done.3 = bf16[32,8,640]{2,1,0:T(8,128)(2,1)S(1)} async-done(((bf16[32,8,640]{2,1,0:T(8,128)(2,1)}), bf16[32,8,640]{2,1,0:T(8,128)(2,1)S(1)}, u32[]{:S(2)}, u32[]{:S(2)}) %all-to-all-start.3) | async-done | bytes 327712 | tf_op jit(solution)/shard_map/all_to_all | solution.py:213
  157.8 2.0 shard_map.89.cells_ref.grad_ref
  159.8 4.2 %shard_map.91 = f32[32,640]{1,0:T(8,128)} custom-call(bf16[256,640]{1,0:T(8,128)(2,1)} %shard_map.89.cells_ref.grad_ref, bf16[64,640]{1,0:T(8,128)(2,1)} %copy-done.16, bf16[256,640]{1,0:T(8,128)(2,1)} %shard_map.85.cells_ref, bf16[64,640]{1,0:T(8,128)(2,1)} %copy-done.17), custom_call_target="tpu_custom_call" | custom-call | tf_op jit(solution)/shard_map/pallas_call | solution.py:200
  164.0 3.9 %all-to-all-start.5 = ((f32[4,5,8,128]{3,2,1,0:T(8,128)}), f32[4,5,8,128]{3,2,1,0:T(8,128)S(1)}, u32[]{:S(2)}, u32[]{:S(2)}) async-start(f32[4,5,8,128]{3,2,1,0:T(8,128)} %bitcast.65), calls=%async_computation.5 | async-start | bytes 163840 | tf_op jit(solution)/shard_map/all_to_all | solution.py:269
  167.9 0.9 pad_maximum_fusion.1
  168.8 3.7 %all-to-all-done.5 = f32[4,5,8,128]{3,2,1,0:T(8,128)S(1)} async-done(((f32[4,5,8,128]{3,2,1,0:T(8,128)}), f32[4,5,8,128]{3,2,1,0:T(8,128)S(1)}, u32[]{:S(2)}, u32[]{:S(2)}) %all-to-all-start.5) | async-done | bytes 81952 | tf_op jit(solution)/shard_map/all_to_all | solution.py:269
  173.2 3.5 %all-to-all-start.6 = ((f32[8,5,8,128]{3,2,1,0:T(8,128)}), f32[8,5,8,128]{3,2,1,0:T(8,128)S(1)}, u32[]{:S(2)}, u32[]{:S(2)}) async-start(f32[8,5,8,128]{3,2,1,0:T(8,128)} %broadcast_in_dim.18), calls=%async_computation.6 | async-start | bytes 327680 | tf_op jit(solution)/shard_map/all_to_all | solution.py:34
  176.7 1.1 copy-done.1
  177.8 1.1 copy-done.4
  178.8 1.1 copy-done.7
  179.9 4.4 %shard_map.87 = bf16[256,1920]{1,0:T(8,128)(2,1)S(1)} custom-call(s32[2]{0:T(128)S(1)} %pad_add_fusion.1.where_ref, bf16[256,1280]{1,0:T(8,128)(2,1)S(1)} %bitcast.56, bf16[160,1920]{1,0:T(8,128)(2,1)S(1)} %bitcast.53, bf16[160,1920]{1,0:T(8,128)(2,1)S(1)} %copy-done.4, bf16[160,1920]{1,0:T(8,128)(2,1)S(1)} %copy-done.7, ...), custom_call_target="tpu_custom_call" | custom-call | flops 1258291200 | bytes 8000000 | tf_op jit(solution)/shard_map/pallas_call | solution.py:278
  184.4 6.9 %collective-permute-start.14 = (bf16[128,1920]{1,0:T(8,128)(2,1)S(1)}, bf16[128,1920]{1,0:T(8,128)(2,1)S(1)}, u32[]{:S(2)}, u32[]{:S(2)}) collective-permute-start(bf16[128,1920]{1,0:T(8,128)(2,1)S(1)} %dynamic-slice_bitcast_fusion.1), channel_id=1, source_target_pairs={{0,1},{1,0},{2,3},{3,2},{4,5},{5,4},{6,7},{7,6},{8,9},{9,8},{10,11... | collective-permute-start | bytes 1474568 | tf_op jit(solution)/shard_map/ppermute | solution.py:19
  192.1 8.0 %all-to-all-start.7 = ((f32[8,5,8,128]{3,2,1,0:T(8,128)}), f32[8,5,8,128]{3,2,1,0:T(8,128)S(1)}, u32[]{:S(2)}, u32[]{:S(2)}) async-start(f32[8,5,8,128]{3,2,1,0:T(8,128)} %broadcast_in_dim.19), calls=%async_computation.7 | async-start | bytes 327680 | tf_op jit(solution)/shard_map/all_to_all | solution.py:34
  200.1 2.2 collective-permute-start.17
  202.3 1.3 collective-permute-start.18
  203.6 1.9 rev.3.kernel_ref
  205.4 2.0 collective-permute-done.18.after_ref
  208.1 4.8 %shard_map.90 = bf16[256,640]{1,0:T(8,128)(2,1)} custom-call(s32[256,1]{1,0:T(8,128)} %broadcast_in_dim_reshape.8.cell_ref, f32[27,640]{1,0:T(8,128)} %rev.3.kernel_ref, bf16[64,640]{1,0:T(8,128)(2,1)} %copy-done.19, bf16[256,640]{1,0:T(8,128)(2,1)} %shard_map.89.cells_ref.grad_ref, bf16[64,640]{1,0:T(8,128)(2,1)} %copy-done.20), custom_call_target="tpu_custom_call" | custom-call | tf_op jit(solution)/shard_map/pallas_call | solution.py:169
  212.9 12.7 %all-to-all-start.4 = ((bf16[32,8,640]{2,1,0:T(8,128)(2,1)}), bf16[32,8,640]{2,1,0:T(8,128)(2,1)S(1)}, u32[]{:S(2)}, u32[]{:S(2)}) async-start(bf16[32,8,640]{2,1,0:T(8,128)(2,1)} %bitcast.58), calls=%async_computation.4 | async-start | bytes 655360 | tf_op jit(solution)/shard_map/all_to_all | solution.py:218
  225.7 10.6 %all-to-all-done.4 = bf16[32,8,640]{2,1,0:T(8,128)(2,1)S(1)} async-done(((bf16[32,8,640]{2,1,0:T(8,128)(2,1)}), bf16[32,8,640]{2,1,0:T(8,128)(2,1)S(1)}, u32[]{:S(2)}, u32[]{:S(2)}) %all-to-all-start.4) | async-done | bytes 327712 | tf_op jit(solution)/shard_map/all_to_all | solution.py:218
  237.0 7.9 %all-to-all-start.8 = ((f32[8,5,8,128]{3,2,1,0:T(8,128)}), f32[8,5,8,128]{3,2,1,0:T(8,128)S(1)}, u32[]{:S(2)}, u32[]{:S(2)}) async-start(f32[8,5,8,128]{3,2,1,0:T(8,128)} %broadcast_in_dim.20), calls=%async_computation.8 | async-start | bytes 327680 | tf_op jit(solution)/shard_map/all_to_all | solution.py:34
  245.2 2.0 collective-permute-start.19
  247.2 1.0 maximum_bitcast_fusion
  248.2 2.2 all-to-all-done.8
  (97 shorter events, 14.2 us)
Async XLA Ops:
  0.6 108.3 %copy-start = (f32[27,1280]{1,0:T(8,128)S(1)}, f32[27,1280]{1,0:T(8,128)}, u32[]{:S(2)}) copy-start(f32[27,1280]{1,0:T(8,128)} %param.8) | copy-start | bytes 414724
  1.6 9.7 %collective-permute-start.5 = (bf16[20,1920]{1,0:T(8,128)(2,1)S(1)}, bf16[20,1920]{1,0:T(8,128)(2,1)S(1)}, u32[]{:S(2)}, u32[]{:S(2)}) collective-permute-start(bf16[20,1920]{1,0:T(8,128)(2,1)S(1)} %constant_dynamic-slice_fusion), channel_id=1, source_target_pairs={{0,1},{1,0},{2,3},{3,2},{4,5},{5,4},{6,7},{7,6},{8,9},{9,8},{10,11... | collective-permute-start | bytes 230408 | tf_op jit(solution)/shard_map/ppermute | solution.py:19
  12.3 36.6 %copy-start.13 = (bf16[1,128,3840]{2,1,0:T(8,128)(2,1)S(1)}, bf16[1,128,3840]{2,1,0:T(8,128)(2,1)}, u32[]{:S(2)}) copy-start(bf16[1,128,3840]{2,1,0:T(8,128)(2,1)} %param.10) | copy-start | bytes 2949124
  12.3 41.9 %copy-start.21 = (s32[1,128]{1,0:T(1,128)S(1)}, s32[1,128]{1,0:T(1,128)}, u32[]{:S(2)}) copy-start(s32[1,128]{1,0:T(1,128)} %param.7) | copy-start | bytes 1540
  12.3 43.9 %copy-start.18 = (bf16[1,128,1280]{2,1,0:T(8,128)(2,1)S(1)}, bf16[1,128,1280]{2,1,0:T(8,128)(2,1)}, u32[]{:S(2)}) copy-start(bf16[1,128,1280]{2,1,0:T(8,128)(2,1)} %param.6) | copy-start | bytes 983044
  25.1 17.3 %collective-permute-start.6 = (bf16[160,1920]{1,0:T(8,128)(2,1)S(1)}, bf16[160,1920]{1,0:T(8,128)(2,1)S(1)}, u32[]{:S(2)}, u32[]{:S(2)}) collective-permute-start(bf16[160,1920]{1,0:T(8,128)(2,1)S(1)} %bitcast.50), channel_id=1, source_target_pairs={{0,8},{8,16},{16,24},{24,32},{32,40},{40,48},{48,56},{56,0},{1,9},... | collective-permute-start | bytes 1843208 | tf_op jit(solution)/shard_map/ppermute | solution.py:40
  27.0 17.3 %collective-permute-start.7 = (bf16[160,1920]{1,0:T(8,128)(2,1)S(1)}, bf16[160,1920]{1,0:T(8,128)(2,1)S(1)}, u32[]{:S(2)}, u32[]{:S(2)}) collective-permute-start(bf16[160,1920]{1,0:T(8,128)(2,1)S(1)} %bitcast.51), channel_id=1, source_target_pairs={{0,56},{8,0},{16,8},{24,16},{32,24},{40,32},{48,40},{56,48},{1,57}... | collective-permute-start | bytes 1843208 | tf_op jit(solution)/shard_map/ppermute | solution.py:40
  42.3 24.1 %copy-start.2 = (bf16[160,1920]{1,0:T(8,128)(2,1)}, bf16[160,1920]{1,0:T(8,128)(2,1)S(1)}, u32[]{:S(2)}) copy-start(bf16[160,1920]{1,0:T(8,128)(2,1)S(1)} %collective-permute-done.6.refs_1_) | copy-start | bytes 1843204
  42.3 16.4 %collective-permute-start.8 = (bf16[160,1920]{1,0:T(8,128)(2,1)S(1)}, bf16[160,1920]{1,0:T(8,128)(2,1)}, u32[]{:S(2)}, u32[]{:S(2)}) collective-permute-start(bf16[160,1920]{1,0:T(8,128)(2,1)S(1)} %collective-permute-done.6.refs_1_), channel_id=1, source_target_pairs={{0,8},{8,16},{16,24},{24,32},{32,40},{40,48},{48,56},{56,0},{1,9},... | collective-permute-start | bytes 1843208 | tf_op jit(solution)/shard_map/ppermute | solution.py:40
  44.3 16.4 %copy-start.5 = (bf16[160,1920]{1,0:T(8,128)(2,1)}, bf16[160,1920]{1,0:T(8,128)(2,1)S(1)}, u32[]{:S(2)}) copy-start(bf16[160,1920]{1,0:T(8,128)(2,1)S(1)} %collective-permute-done.7.refs_2_) | copy-start | bytes 1843204
  44.3 16.4 %collective-permute-start.9 = (bf16[160,1920]{1,0:T(8,128)(2,1)S(1)}, bf16[160,1920]{1,0:T(8,128)(2,1)}, u32[]{:S(2)}, u32[]{:S(2)}) collective-permute-start(bf16[160,1920]{1,0:T(8,128)(2,1)S(1)} %collective-permute-done.7.refs_2_), channel_id=1, source_target_pairs={{0,56},{8,0},{16,8},{24,16},{32,24},{40,32},{48,40},{56,48},{1,57}... | collective-permute-start | bytes 1843208 | tf_op jit(solution)/shard_map/ppermute | solution.py:40
  49.7 32.7 %collective-permute-start.15 = (bf16[128,1920]{1,0:T(8,128)(2,1)}, bf16[128,1920]{1,0:T(8,128)(2,1)}, u32[]{:S(2)}, u32[]{:S(2)}) collective-permute-start(bf16[128,1920]{1,0:T(8,128)(2,1)} %dynamic-slice_bitcast_fusion), channel_id=1, source_target_pairs={{0,1},{1,0},{2,3},{3,2},{4,5},{5,4},{6,7},{7,6},{8,9},{9,8},{10,11... | collective-permute-start | bytes 1474568 | tf_op jit(solution)/shard_map/ppermute | solution.py:19
  54.3 4.5 %collective-permute-start = (s32[1,128]{1,0:T(1,128)S(1)}, s32[1,128]{1,0:T(1,128)S(1)}, u32[]{:S(2)}, u32[]{:S(2)}) collective-permute-start(s32[1,128]{1,0:T(1,128)S(1)} %copy-done.21), channel_id=1, source_target_pairs={{0,1},{1,0},{2,3},{3,2},{4,5},{5,4},{6,7},{7,6},{8,9},{9,8},{10,11... | collective-permute-start | bytes 1544 | tf_op jit(solution)/shard_map/ppermute | solution.py:19
  56.2 10.1 %collective-permute-start.1 = (bf16[128,640]{1,0:T(8,128)(2,1)S(1)}, bf16[128,640]{1,0:T(8,128)(2,1)S(1)}, u32[]{:S(2)}, u32[]{:S(2)}) collective-permute-start(bf16[128,640]{1,0:T(8,128)(2,1)S(1)} %dynamic-slice_bitcast_fusion.3), channel_id=1, source_target_pairs={{0,1},{1,0},{2,3},{3,2},{4,5},{5,4},{6,7},{7,6},{8,9},{9,8},{10,11... | collective-permute-start | bytes 491528 | tf_op jit(solution)/shard_map/ppermute | solution.py:19
  58.8 15.6 %collective-permute-start.10 = (bf16[160,1920]{1,0:T(8,128)(2,1)}, bf16[160,1920]{1,0:T(8,128)(2,1)S(1)}, u32[]{:S(2)}, u32[]{:S(2)}) collective-permute-start(bf16[160,1920]{1,0:T(8,128)(2,1)} %collective-permute-done.8.refs_3_), channel_id=1, source_target_pairs={{0,8},{8,16},{16,24},{24,32},{32,40},{40,48},{48,56},{56,0},{1,9},... | collective-permute-start | bytes 1843208 | tf_op jit(solution)/shard_map/ppermute | solution.py:40
  60.7 16.4 %collective-permute-start.11 = (bf16[160,1920]{1,0:T(8,128)(2,1)}, bf16[160,1920]{1,0:T(8,128)(2,1)S(1)}, u32[]{:S(2)}, u32[]{:S(2)}) collective-permute-start(bf16[160,1920]{1,0:T(8,128)(2,1)} %collective-permute-done.9.refs_4_), channel_id=1, source_target_pairs={{0,56},{8,0},{16,8},{24,16},{32,24},{40,32},{48,40},{56,48},{1,57}... | collective-permute-start | bytes 1843208 | tf_op jit(solution)/shard_map/ppermute | solution.py:40
  67.5 14.9 %copy-start.14 = (bf16[1,128,3840]{2,1,0:T(8,128)(2,1)S(1)}, bf16[1,128,3840]{2,1,0:T(8,128)(2,1)}, u32[]{:S(2)}) copy-start(bf16[1,128,3840]{2,1,0:T(8,128)(2,1)} %param.10) | copy-start | bytes 2949124
  67.5 16.2 %all-to-all-start = ((bf16[32,8,640]{2,1,0:T(8,128)(2,1)}), bf16[32,8,640]{2,1,0:T(8,128)(2,1)}, u32[]{:S(2)}, u32[]{:S(2)}) async-start(bf16[32,8,640]{2,1,0:T(8,128)(2,1)} %reshape.72), calls=%async_computation | async-start | bytes 655360 | tf_op jit(solution)/shard_map/all_to_all | solution.py:213
  75.2 13.2 %collective-permute-start.12 = (bf16[80,1920]{1,0:T(8,128)(2,1)}, bf16[80,1920]{1,0:T(8,128)(2,1)S(1)}, u32[]{:S(2)}, u32[]{:S(2)}) collective-permute-start(bf16[80,1920]{1,0:T(8,128)(2,1)} %slice.30), channel_id=1, source_target_pairs={{0,8},{8,16},{16,24},{24,32},{32,40},{40,48},{48,56},{56,0},{1,9},... | collective-permute-start | bytes 921608 | tf_op jit(solution)/shard_map/ppermute | solution.py:40
  77.8 11.8 %collective-permute-start.13 = (bf16[80,1920]{1,0:T(8,128)(2,1)}, bf16[80,1920]{1,0:T(8,128)(2,1)}, u32[]{:S(2)}, u32[]{:S(2)}) collective-permute-start(bf16[80,1920]{1,0:T(8,128)(2,1)} %slice.31), channel_id=1, source_target_pairs={{0,56},{8,0},{16,8},{24,16},{32,24},{40,32},{48,40},{56,48},{1,57}... | collective-permute-start | bytes 921608 | tf_op jit(solution)/shard_map/ppermute | solution.py:40
  89.6 1.1 copy-start.3
  90.7 1.1 copy-start.6
  91.7 13.7 %copy-start.10 = (bf16[256,640]{1,0:T(8,128)(2,1)S(1)}, bf16[256,640]{1,0:T(8,128)(2,1)}, u32[]{:S(2)}) copy-start(bf16[256,640]{1,0:T(8,128)(2,1)} %shard_map.85.cells_ref) | copy-start | bytes 983044
  96.7 0.8 copy-start.8
  97.6 31.5 %collective-permute-start.16 = (f32[256,640]{1,0:T(8,128)}, f32[256,640]{1,0:T(8,128)}, u32[]{:S(2)}, u32[]{:S(2)}) collective-permute-start(f32[256,640]{1,0:T(8,128)} %get-tuple-element.6), channel_id=1, source_target_pairs={{0,1},{1,0},{2,3},{3,2},{4,5},{5,4},{6,7},{7,6},{8,9},{9,8},{10,11... | collective-permute-start | bytes 1966088 | tf_op jit(solution)/shard_map/ppermute | solution.py:19
  105.5 4.8 %collective-permute-start.2 = (bf16[64,640]{1,0:T(8,128)(2,1)S(1)}, bf16[64,640]{1,0:T(8,128)(2,1)S(1)}, u32[]{:S(2)}, u32[]{:S(2)}) collective-permute-start(bf16[64,640]{1,0:T(8,128)(2,1)S(1)} %get-tuple-element.20), channel_id=1, source_target_pairs={{0,2},{2,4},{4,6},{6,8},{8,10},{10,12},{12,14},{14,16},{16,18},{18... | collective-permute-start | bytes 245768 | tf_op jit(solution)/shard_map/ppermute | solution.py:225
  107.6 5.6 %collective-permute-start.3 = (bf16[64,640]{1,0:T(8,128)(2,1)S(1)}, bf16[64,640]{1,0:T(8,128)(2,1)S(1)}, u32[]{:S(2)}, u32[]{:S(2)}) collective-permute-start(bf16[64,640]{1,0:T(8,128)(2,1)S(1)} %get-tuple-element.19), channel_id=1, source_target_pairs={{2,0},{4,2},{6,4},{8,6},{10,8},{12,10},{14,12},{16,14},{18,16},{20... | collective-permute-start | bytes 245768 | tf_op jit(solution)/shard_map/ppermute | solution.py:226
  109.6 19.5 %copy-start.9 = (f32[256,640]{1,0:T(8,128)S(1)}, f32[256,640]{1,0:T(8,128)}, u32[]{:S(2)}) copy-start(f32[256,640]{1,0:T(8,128)} %copy-done.8) | copy-start | bytes 1966084
  110.3 2.9 %copy-start.16 = (bf16[64,640]{1,0:T(8,128)(2,1)}, bf16[64,640]{1,0:T(8,128)(2,1)S(1)}, u32[]{:S(2)}) copy-start(bf16[64,640]{1,0:T(8,128)(2,1)S(1)} %collective-permute-done.2.before_ref) | copy-start | bytes 245764
  113.2 0.6 copy-start.17
  118.7 22.4 %all-to-all-start.1 = ((bf16[32,8,640]{2,1,0:T(8,128)(2,1)}), bf16[32,8,640]{2,1,0:T(8,128)(2,1)S(1)}, u32[]{:S(2)}, u32[]{:S(2)}) async-start(bf16[32,8,640]{2,1,0:T(8,128)(2,1)} %bitcast.59), calls=%async_computation.1 | async-start | bytes 655360 | tf_op jit(solution)/shard_map/all_to_all | solution.py:218
  141.1 15.9 %all-to-all-start.3 = ((bf16[32,8,640]{2,1,0:T(8,128)(2,1)}), bf16[32,8,640]{2,1,0:T(8,128)(2,1)S(1)}, u32[]{:S(2)}, u32[]{:S(2)}) async-start(bf16[32,8,640]{2,1,0:T(8,128)(2,1)} %reshape.80), calls=%async_computation.3 | async-start | bytes 655360 | tf_op jit(solution)/shard_map/all_to_all | solution.py:213
  147.3 5.4 %collective-permute-start.4 = (bf16[2,128,640]{2,1,0:T(8,128)(2,1)}, bf16[2,128,640]{2,1,0:T(8,128)(2,1)}, u32[]{:S(2)}, u32[]{:S(2)}) collective-permute-start(bf16[2,128,640]{2,1,0:T(8,128)(2,1)} %reshape.76), channel_id=1, source_target_pairs={{0,1},{1,0},{2,3},{3,2},{4,5},{5,4},{6,7},{7,6},{8,9},{9,8},{10,11... | collective-permute-start | bytes 983048 | tf_op jit(solution)/shard_map/ppermute | solution.py:19
  157.1 0.7 copy-start.12
  164.0 8.5 %all-to-all-start.5 = ((f32[4,5,8,128]{3,2,1,0:T(8,128)}), f32[4,5,8,128]{3,2,1,0:T(8,128)S(1)}, u32[]{:S(2)}, u32[]{:S(2)}) async-start(f32[4,5,8,128]{3,2,1,0:T(8,128)} %bitcast.65), calls=%async_computation.5 | async-start | bytes 163840 | tf_op jit(solution)/shard_map/all_to_all | solution.py:269
  173.2 18.2 %all-to-all-start.6 = ((f32[8,5,8,128]{3,2,1,0:T(8,128)}), f32[8,5,8,128]{3,2,1,0:T(8,128)S(1)}, u32[]{:S(2)}, u32[]{:S(2)}) async-start(f32[8,5,8,128]{3,2,1,0:T(8,128)} %broadcast_in_dim.18), calls=%async_computation.6 | async-start | bytes 327680 | tf_op jit(solution)/shard_map/all_to_all | solution.py:34
  176.7 1.1 copy-start.1
  177.8 1.1 copy-start.4
  178.8 1.1 copy-start.7
  184.3 15.7 %copy-start.11 = (bf16[256,640]{1,0:T(8,128)(2,1)S(1)}, bf16[256,640]{1,0:T(8,128)(2,1)}, u32[]{:S(2)}) copy-start(bf16[256,640]{1,0:T(8,128)(2,1)} %shard_map.89.cells_ref.grad_ref) | copy-start | bytes 983044
  184.4 19.2 %copy-start.15 = (f32[27,640]{1,0:T(8,128)S(1)}, f32[27,640]{1,0:T(8,128)}, u32[]{:S(2)}) copy-start(f32[27,640]{1,0:T(8,128)} %constant_dynamic-slice_fusion.1.kernel_ref) | copy-start | bytes 207364
  184.4 41.2 %collective-permute-start.14 = (bf16[128,1920]{1,0:T(8,128)(2,1)S(1)}, bf16[128,1920]{1,0:T(8,128)(2,1)S(1)}, u32[]{:S(2)}, u32[]{:S(2)}) collective-permute-start(bf16[128,1920]{1,0:T(8,128)(2,1)S(1)} %dynamic-slice_bitcast_fusion.1), channel_id=1, source_target_pairs={{0,1},{1,0},{2,3},{3,2},{4,5},{5,4},{6,7},{7,6},{8,9},{9,8},{10,11... | collective-permute-start | bytes 1474568 | tf_op jit(solution)/shard_map/ppermute | solution.py:19
  192.1 20.8 %all-to-all-start.7 = ((f32[8,5,8,128]{3,2,1,0:T(8,128)}), f32[8,5,8,128]{3,2,1,0:T(8,128)S(1)}, u32[]{:S(2)}, u32[]{:S(2)}) async-start(f32[8,5,8,128]{3,2,1,0:T(8,128)} %broadcast_in_dim.19), calls=%async_computation.7 | async-start | bytes 327680 | tf_op jit(solution)/shard_map/all_to_all | solution.py:34
  200.1 5.4 %collective-permute-start.17 = (bf16[64,640]{1,0:T(8,128)(2,1)S(1)}, bf16[64,640]{1,0:T(8,128)(2,1)S(1)}, u32[]{:S(2)}, u32[]{:S(2)}) collective-permute-start(bf16[64,640]{1,0:T(8,128)(2,1)S(1)} %get-tuple-element.18), channel_id=1, source_target_pairs={{0,2},{2,4},{4,6},{6,8},{8,10},{10,12},{12,14},{14,16},{16,18},{18... | collective-permute-start | bytes 245768 | tf_op jit(solution)/shard_map/ppermute | solution.py:225
  202.3 5.2 %collective-permute-start.18 = (bf16[64,640]{1,0:T(8,128)(2,1)S(1)}, bf16[64,640]{1,0:T(8,128)(2,1)S(1)}, u32[]{:S(2)}, u32[]{:S(2)}) collective-permute-start(bf16[64,640]{1,0:T(8,128)(2,1)S(1)} %get-tuple-element.17), channel_id=1, source_target_pairs={{2,0},{4,2},{6,4},{8,6},{10,8},{12,10},{14,12},{16,14},{18,16},{20... | collective-permute-start | bytes 245768 | tf_op jit(solution)/shard_map/ppermute | solution.py:226
  205.4 2.0 copy-start.19
  207.5 0.6 copy-start.20
  212.9 23.4 %all-to-all-start.4 = ((bf16[32,8,640]{2,1,0:T(8,128)(2,1)}), bf16[32,8,640]{2,1,0:T(8,128)(2,1)S(1)}, u32[]{:S(2)}, u32[]{:S(2)}) async-start(bf16[32,8,640]{2,1,0:T(8,128)(2,1)} %bitcast.58), calls=%async_computation.4 | async-start | bytes 655360 | tf_op jit(solution)/shard_map/all_to_all | solution.py:218
  237.0 13.5 %all-to-all-start.8 = ((f32[8,5,8,128]{3,2,1,0:T(8,128)}), f32[8,5,8,128]{3,2,1,0:T(8,128)S(1)}, u32[]{:S(2)}, u32[]{:S(2)}) async-start(f32[8,5,8,128]{3,2,1,0:T(8,128)} %broadcast_in_dim.20), calls=%async_computation.8 | async-start | bytes 327680 | tf_op jit(solution)/shard_map/all_to_all | solution.py:34
  245.2 5.3 %collective-permute-start.19 = (bf16[128,640]{1,0:T(8,128)(2,1)S(1)}, bf16[128,640]{1,0:T(8,128)(2,1)S(1)}, u32[]{:S(2)}, u32[]{:S(2)}) collective-permute-start(bf16[128,640]{1,0:T(8,128)(2,1)S(1)} %dynamic-slice_bitcast_fusion.2), channel_id=1, source_target_pairs={{0,1},{1,0},{2,3},{3,2},{4,5},{5,4},{6,7},{7,6},{8,9},{9,8},{10,11... | collective-permute-start | bytes 491528 | tf_op jit(solution)/shard_map/ppermute | solution.py:19

commit v2 on v0

v2 whole, which is shorter than its diff:
```python
import functools

import jax
import jax.numpy as jnp
import numpy as np
from jax import lax
from jax.experimental import pallas as pl
from jax.experimental.pallas import tpu as pltpu
from jax.sharding import Mesh
from jax.sharding import PartitionSpec as P

NY, NX, NC = 8, 4, 2
CHIPS = NY * NX
TOK = 128
LAYER = 64
GROUP = 20
BF16, F32 = jnp.bfloat16, jnp.float32
VMEM = pl.BlockSpec(memory_space=pltpu.VMEM)
SMEM = pl.BlockSpec(memory_space=pltpu.SMEM)
AWAY = pl.BlockSpec(memory_space=pltpu.HBM)


def swap(value):
    return lax.ppermute(value, "c", [(0, 1), (1, 0)])


def spread(value, axis, size):
    return lax.all_to_all(
        jnp.broadcast_to(value[None], (size, *value.shape)), axis, 0, 0, tiled=True
    )


def shift(value, axis, size, step):
    return lax.ppermute(value, axis, [(i, (i + step) % size) for i in range(size)])


def after(value, *others):
    return lax.optimization_barrier((value, *others))[0]


def params(vmem=None):
    return pltpu.CompilerParams(vmem_limit_bytes=vmem)


ROWS = NX * GROUP
CUT = 48
PIECES = [(s, 0, ROWS) for s in (0, -1, 1, -2, 2, -3, 3)] + [(4, 0, CUT), (4, CUT, ROWS - CUT)]


def ring(up, down):
    return shift(up, "y", NY, 1), shift(down, "y", NY, -1)


def assemble(where_ref, arrays, weight, sems, more):
    copies = [
        pltpu.make_async_copy(source, target, sems.at[len(PIECES) + i])
        for i, (source, target) in enumerate(more)
    ]
    for i, (step, skip, rows) in enumerate(PIECES):
        row = pl.multiple_of(lax.rem(where_ref[0] + step + NY, NY) * ROWS + skip, 16)
        copies.append(
            pltpu.make_async_copy(arrays[i], weight.at[pl.ds(row, rows)], sems.at[i])
        )
    for copy in copies:
        copy.start()
    for copy in copies:
        copy.wait()


def one_hot(hit):
    return jnp.where(hit, 1.0, 0.0).astype(BF16)


def pick_rows(source, count, value):
    shape = (count, value.shape[0])
    hit = lax.broadcasted_iota(jnp.int32, shape, 1) == source(
        lax.broadcasted_iota(jnp.int32, shape, 0)
    )
    return jnp.dot(one_hot(hit), value, preferred_element_type=F32).astype(BF16)


def stacked_row(core):
    def source(row):
        block = lax.shift_right_logical(row, 2) & 1
        at = lax.shift_left(lax.shift_right_logical(row, 3), 2) + (row & 3)
        return at + jnp.where(block == core, 0, TOK)

    return source


def landed_row(block):
    def source(row):
        return lax.shift_left(lax.shift_right_logical(row, 2), 3) + (row & 3) + block * 4

    return source


def both_rows(core):
    def source(row):
        block = jnp.where(row < TOK, core, 1 - core)
        return landed_row(block)(row & (TOK - 1))

    return source


def back_kernel(where_ref, y_ref, own_ref, other_ref, *refs):
    arrays, (out_ref, whole_ref, weight, sems, rows) = refs[: len(PIECES)], refs[len(PIECES) :]
    more = [(own_ref, rows.at[0:TOK]), (other_ref, rows.at[TOK:])]
    assemble(where_ref, arrays, weight, sems, more)
    whole = pltpu.make_async_copy(weight, whole_ref, sems.at[len(PIECES) + 2])
    whole.start()
    width = y_ref.shape[1]
    out_ref[:, 0:width] = y_ref[...]
    for at, size in ((0, 256), (256, 256), (512, 128)):
        part = lax.dot_general(
            rows[...],
            weight[at : at + size, :],
            (((1,), (1,)), ((), ())),
            preferred_element_type=F32,
        ).astype(BF16)
        out_ref[:, width + at : width + at + size] = pick_rows(
            stacked_row(where_ref[1]), part.shape[0], part
        )
    whole.wait()


def back_rows(where, rows_y, own, other, arrays):
    columns = own.shape[1]
    return pl.pallas_call(
        back_kernel,
        out_shape=(
            jax.ShapeDtypeStruct((2 * TOK, 2 * NY * ROWS), BF16),
            jax.ShapeDtypeStruct((NY * ROWS, columns), BF16),
        ),
        in_specs=[SMEM, VMEM] + [AWAY] * (2 + len(arrays)),
        out_specs=(VMEM, AWAY),
        scratch_shapes=[
            pltpu.VMEM((NY * ROWS, columns), BF16),
            pltpu.SemaphoreType.DMA((len(PIECES) + 3,)),
            pltpu.VMEM((2 * TOK, columns), BF16),
        ],
        compiler_params=params(60 << 20),
    )(where, rows_y, own, other, *arrays)


def project_kernel(where_ref, landed_ref, whole_ref, keep_ref, send_ref, weight, sem):
    copy = pltpu.make_async_copy(whole_ref, weight, sem)
    copy.start()
    landed = landed_ref[:, 0 : weight.shape[0]]
    rows = pick_rows(both_rows(where_ref[1]), landed.shape[0], landed)
    copy.wait()
    for at in range(0, weight.shape[1], 768):
        part = jnp.dot(rows, weight[:, at : at + 768], preferred_element_type=F32)
        keep_ref[:, at : at + 768] = part[0:TOK]
        send_ref[:, at : at + 768] = part[TOK:]


def project(where, landed, whole):
    out = jax.ShapeDtypeStruct((TOK, whole.shape[1]), F32)
    return pl.pallas_call(
        project_kernel,
        out_shape=(out, out),
        in_specs=[SMEM, VMEM, AWAY],
        out_specs=(VMEM, VMEM),
        scratch_shapes=[pltpu.VMEM(whole.shape, BF16), pltpu.SemaphoreType.DMA],
        compiler_params=params(60 << 20),
        cost_estimate=pl.CostEstimate(
            flops=4 * TOK * whole.size, bytes_accessed=20_000_000, transcendentals=0
        ),
    )(where, landed, whole)


def chosen(channel_ref, width, dtype=BF16):
    shape = (width, channel_ref.shape[1])
    hit = lax.broadcasted_iota(jnp.int32, shape, 0) == channel_ref[...]
    return jnp.where(hit, 1.0, 0.0).astype(dtype)


def select_kernel(own_ref, other_ref, rows_ref, place_ref, kernel_ref, x_ref, send_ref, kern_ref):
    width = rows_ref.shape[1]
    mine = chosen(own_ref, width)
    x_ref[...] = jnp.dot(rows_ref[...], mine, preferred_element_type=F32).astype(BF16)
    theirs = chosen(other_ref, width)
    send_ref[0:TOK] = jnp.dot(rows_ref[...], theirs, preferred_element_type=F32).astype(BF16)
    send_ref[TOK:] = jnp.zeros((16, send_ref.shape[1]), BF16)
    place = jnp.broadcast_to(place_ref[...].astype(F32), (16, TOK)).astype(BF16)
    send_ref[TOK:, 0:TOK] = place
    kern_ref[...] = jnp.dot(
        kernel_ref[...],
        chosen(own_ref, width, F32),
        precision=lax.Precision.HIGHEST,
        preferred_element_type=F32,
    )


def put_cells(cell_ref, rows, out_ref, first_ref, last_ref):
    count = out_ref.shape[0]
    hit = lax.broadcasted_iota(jnp.int32, (count, count), 0) == cell_ref[...]
    cells = jnp.dot(one_hot(hit), rows, preferred_element_type=F32).astype(BF16)
    out_ref[...] = cells
    first_ref[...] = cells[0:LAYER]
    last_ref[...] = cells[count - LAYER :]


def join_kernel(cell_ref, own_ref, other_ref, *outs):
    put_cells(cell_ref, jnp.concatenate([own_ref[...], other_ref[0:TOK, :]], axis=0), *outs)


def cells_kernel(cell_ref, rows_ref, *outs):
    put_cells(cell_ref, rows_ref[:, rows_ref.shape[1] - outs[0].shape[1] :], *outs)


def in_vmem(body, out_shape, *operands, vmem=None, scalars=0):
    return pl.pallas_call(
        body,
        out_shape=out_shape,
        in_specs=[SMEM] * scalars + [VMEM] * (len(operands) - scalars),
        out_specs=jax.tree.map(lambda _: VMEM, out_shape),
        compiler_params=params(vmem),
    )(*operands)


def fill(before_ref, cells_ref, after_ref, field):
    parts = (before_ref[...], cells_ref[...], after_ref[...])
    lanes = cells_ref.shape[1]
    wide = jnp.concatenate([p.astype(F32) for p in parts], axis=0)
    wide = wide.reshape(6 * 8, 8, lanes)
    column = lax.broadcasted_iota(jnp.int32, wide.shape, 1)
    lower = jnp.where(column == 0, 0.0, jnp.roll(wide, 1, axis=1))
    upper = jnp.where(column == 7, 0.0, jnp.roll(wide, -1, axis=1))
    zero = jnp.zeros((6, 1, 8, lanes), F32)
    for s, value in enumerate((lower, wide, upper)):
        field[s, :, 0:1] = zero
        field[s, :, 9:10] = zero
        field[s, :, 1:9] = value.reshape(6, 8, 8, lanes)


def conv_body(flip, index_ref, kernel_ref, before_ref, cells_ref, after_ref, out_ref, field):
    fill(before_ref, cells_ref, after_ref, field)
    count, lanes = cells_ref.shape
    layers = []
    for z in range(4):
        total = jnp.zeros((8, 8, lanes), F32)
        for o in range(27):
            dz, di, dc = o // 9, o // 3 % 3, o % 3
            row = 26 - o if flip else o
            total = total + kernel_ref[row : row + 1, :][None] * field[dc, z + dz, di : di + 8]
        layers.append(total)
    conv = jnp.stack(layers).reshape(count, lanes)
    result = (cells_ref[...].astype(F32) + conv).astype(BF16)
    hit = lax.broadcasted_iota(jnp.int32, (count, count), 1) == index_ref[...]
    out_ref[...] = jnp.dot(one_hot(hit), result, preferred_element_type=F32).astype(BF16)


def high_part(value):
    return value.astype(BF16)


def rest_part(value):
    return (value - value.astype(BF16).astype(F32)).astype(BF16)


def back_conv_body(index_ref, kernel_ref, before_ref, cells_ref, after_ref, sums_ref, out_ref, field):
    step = pl.program_id(0)
    last = pl.num_programs(0) - 2

    @pl.when(step < last)
    def _():
        conv_body(True, index_ref, kernel_ref, before_ref, cells_ref, after_ref, out_ref, field)

    @pl.when(step == last)
    def _():
        out_ref[...] = high_part(sums_ref[...])

    @pl.when(step == last + 1)
    def _():
        out_ref[...] = rest_part(sums_ref[...])


def tall(rows, steps, lanes=128):
    return pl.BlockSpec((rows, lanes), lambda t: (0, jnp.minimum(t, steps - 1)))


def conv_rows(cells, before, after, kernel, cell_column, sums=None):
    count, width = cells.shape
    steps = width // 128
    specs = [
        pl.BlockSpec((count, 1), lambda t: (0, 0)),
        tall(kernel.shape[0], steps),
        tall(LAYER, steps),
        tall(count, steps),
        tall(LAYER, steps),
    ]
    operands = (cell_column, kernel, before, cells, after)
    if sums is not None:
        specs.append(pl.BlockSpec(sums.shape, lambda t: (0, 0)))
        operands += (sums,)
    wide = steps if sums is None else steps + 2
    return pl.pallas_call(
        functools.partial(conv_body, False) if sums is None else back_conv_body,
        out_shape=jax.ShapeDtypeStruct((count, wide * 128), BF16),
        grid=(wide,),
        in_specs=specs,
        out_specs=pl.BlockSpec((count, 128), lambda t: (0, t)),
        scratch_shapes=[pltpu.VMEM((3, 6, 10, 8, 128), F32)],
    )(*operands)


def grad_body(steps, grad_ref, before_ref, cells_ref, after_ref, out_ref, field):
    @pl.when(pl.program_id(0) >= steps)
    def _():
        out_ref[...] = jnp.zeros_like(out_ref)

    @pl.when(pl.program_id(0) < steps)
    def _():
        fill(before_ref, cells_ref, after_ref, field)
        lanes = cells_ref.shape[1]
        grad = grad_ref[...].astype(F32).reshape(4, 8, 8, lanes)
        sums = []
        for o in range(27):
            dz, di, dc = o // 9, o // 3 % 3, o % 3
            part = grad * field[dc, dz : dz + 4, di : di + 8]
            sums.append(jnp.sum(part.reshape(32, 8, lanes), axis=0))
        sums += [jnp.zeros((8, lanes), F32)] * 5
        out_ref[...] = jnp.sum(jnp.stack(sums), axis=1)


def kernel_grad(grad, cells, before, after):
    count, width = cells.shape
    steps = width // 128
    return pl.pallas_call(
        functools.partial(grad_body, steps),
        out_shape=jax.ShapeDtypeStruct((count, 128), F32),
        grid=(count // 32,),
        in_specs=[tall(count, steps), tall(LAYER, steps), tall(count, steps), tall(LAYER, steps)],
        out_specs=pl.BlockSpec((32, 128), lambda t: (t, 0)),
        scratch_shapes=[pltpu.VMEM((3, 6, 10, 8, 128), F32)],
    )(grad, before, cells, after)


def in_three(value):
    high = value.astype(BF16)
    rest = value - high.astype(F32)
    middle = rest.astype(BF16)
    low = (rest - middle.astype(F32)).astype(BF16)
    return jnp.concatenate([high, middle, low], axis=0)


def pack_rows(block, landed_ref, tiles_ref):
    steps = NY * ROWS // 128
    rows = pick_rows(landed_row(block), TOK, landed_ref[:, 0 : NY * ROWS])
    tiles = [tiles_ref[4 * t : 4 * t + 4].reshape(32, 128) for t in range(steps)]
    return jnp.concatenate([rows, in_three(jnp.concatenate(tiles, axis=1))], axis=0)


def pack_kernel(where_ref, landed_ref, tiles_ref, out_ref):
    out_ref[...] = pack_rows(1 - where_ref[1], landed_ref, tiles_ref)


def last_kernel(where_ref, own_ch, other_ch, landed_ref, tiles_ref, other_ref, out_ref, grad_ref):
    width = out_ref.shape[1]
    contract = (((1,), (1,)), ((), ()))
    own = pack_rows(where_ref[1], landed_ref, tiles_ref)
    total = lax.dot_general(own, chosen(own_ch, width), contract, preferred_element_type=F32)
    total = total + lax.dot_general(
        other_ref[...], chosen(other_ch, width), contract, preferred_element_type=F32
    )
    out_ref[...] = total[0:TOK].astype(BF16)
    grad = total[TOK : TOK + 32] + total[TOK + 32 : TOK + 64] + total[TOK + 64 : TOK + 96]
    grad_ref[...] = grad[0 : grad_ref.shape[0]]


def landed_sum_kernel(landed_ref, out_ref):
    at = NY * ROWS
    parts = landed_ref[:, at : at + 128].astype(F32) + landed_ref[:, at + 128 : at + 256].astype(F32)
    total = jnp.sum(parts.reshape(CHIPS, 8, 128), axis=0)
    for i in range(out_ref.shape[0]):
        out_ref[i] = total


def sum_kernel(count, parts_ref, out_ref):
    total = parts_ref[0]
    for i in range(1, parts_ref.shape[0]):
        total = total + parts_ref[i]
    for i in range(count):
        out_ref[i] = total


def sum_spread(parts, axis, size):
    shape = jax.ShapeDtypeStruct((size, *parts.shape[1:]), F32)
    sent = in_vmem(functools.partial(sum_kernel, size), shape, parts)
    return lax.all_to_all(sent, axis, 0, 0, tiled=True)


def exchange(rows):
    count, width = rows.shape
    sent = rows.reshape(CHIPS, count // CHIPS, width)
    return lax.all_to_all(sent, ("y", "x"), 0, 0, tiled=True).reshape(count, width)


def faces(first, last):
    up = [(i, i + 1) for i in range(CHIPS - 1)]
    down = [(j, i) for i, j in up]
    return lax.ppermute(last, ("y", "x"), up), lax.ppermute(first, ("y", "x"), down)


def shards(planes, tokens, place, kernel, proj_weight, d_projected):
    core = lax.axis_index("c")
    where = jnp.stack([lax.axis_index("y"), core]).astype(jnp.int32)
    rows_x, rows_d = tokens[0], d_projected[0]
    width = rows_x.shape[1]
    local = width // NC

    other_d = swap(rows_d)
    block = after(spread(proj_weight, "x", NX), other_d).reshape(ROWS, proj_weight.shape[1])
    landed_x = exchange(after(rows_x, block))
    near = ring(block, block)
    second_near = ring(*near)

    steps = jnp.arange(local, dtype=jnp.int32)
    first = (steps // GROUP * (NC * GROUP) + steps % GROUP)[None]
    second = first + GROUP
    own_ch = jnp.where(core == 0, first, second)
    other_ch = jnp.where(core == 0, second, first)
    own_x, send_x, kern = in_vmem(
        select_kernel,
        (
            jax.ShapeDtypeStruct((TOK, local), BF16),
            jax.ShapeDtypeStruct((TOK + 16, local), BF16),
            jax.ShapeDtypeStruct((kernel.shape[0], local), F32),
        ),
        own_ch,
        other_ch,
        after(landed_x, *near),
        place,
        kernel,
        vmem=16 << 20,
    )
    other_x = swap(send_x)

    theirs = other_x[TOK, 0:TOK].astype(jnp.int32)
    places = jnp.stack([jnp.where(core == 0, place[0], theirs), jnp.where(core == 0, theirs, place[0])])
    cell = places.reshape(2, CHIPS, 2, 2) + jnp.array([0, TOK], jnp.int32)[:, None, None, None]
    by_block = cell.transpose(2, 1, 0, 3).reshape(2, TOK)
    stacked = jnp.where(core == 0, by_block, by_block[::-1]).reshape(1, 2 * TOK)
    cell = cell.transpose(1, 2, 0, 3).reshape(2 * TOK)
    cell_row, cell_column = cell[None, :], cell[:, None]

    layer = jax.ShapeDtypeStruct((LAYER, local), BF16)
    pair = (jax.ShapeDtypeStruct((2 * TOK, local), BF16), layer, layer)
    third_near = ring(*lax.optimization_barrier((*second_near, own_x))[:2])
    cells_x, first_x, last_x = in_vmem(join_kernel, pair, stacked, own_x, other_x)
    before_x, after_x = faces(first_x, last_x)
    up, down, before_x, after_x = lax.optimization_barrier((*third_near, before_x, after_x))
    far = (shift(up[:CUT], "y", NY, 1), shift(down[CUT:], "y", NY, -1))
    rows_y = conv_rows(cells_x, before_x, after_x, kern, cell_column)

    arrays = (block, *near, *second_near, *third_near, *far)
    sent, whole = back_rows(where, rows_y, rows_d, other_d, arrays)
    landed = exchange(sent)
    cells_d, first_d, last_d = in_vmem(cells_kernel, pair, cell_row, landed)
    before_d, after_d = faces(first_d, last_d)
    sums = kernel_grad(cells_d, cells_x, before_x, after_x)
    back = conv_rows(cells_d, before_d, after_d, kern, cell_column, sums)
    landed = after(landed, back)
    keep, send = project(where, landed, whole)
    landed_d = exchange(back)
    tile = jax.ShapeDtypeStruct((planes, 8, 128), F32)
    tiles = lax.all_to_all(in_vmem(landed_sum_kernel, tile, landed_d), "z", 0, 0, tiled=True)
    tiles = sum_spread(tiles, ("y", "x"), CHIPS)
    packed = jax.ShapeDtypeStruct((TOK + 96, local), BF16)
    d_other = swap(in_vmem(pack_kernel, packed, where, landed_d, tiles, scalars=1))

    projected = (keep + swap(after(send, landed_d))).astype(BF16)
    projected, d_other = lax.optimization_barrier((projected, d_other))
    d_tokens, d_kernel = in_vmem(
        last_kernel,
        (
            jax.ShapeDtypeStruct((TOK, width), BF16),
            jax.ShapeDtypeStruct(kernel.shape, F32),
        ),
        where,
        own_ch,
        other_ch,
        landed_d,
        tiles,
        d_other,
        vmem=16 << 20,
        scalars=1,
    )
    return projected[None], d_tokens[None], d_kernel


def solution(mesh):
    planes = mesh.shape["dp"]
    devices = np.asarray(mesh.devices).reshape(planes, NY, NX, NC)
    grid = Mesh(devices, ("z", "y", "x", "c"))
    seq = ("y", "x", "c")
    return jax.shard_map(
        functools.partial(shards, planes),
        mesh=grid,
        in_specs=(P("z", seq, None), P(seq, None), P(), P(seq, None), P("z", seq, None)),
        out_specs=(P("z", seq, None), P("z", seq, None), P()),
        check_vma=False,
    )
```

time: 493 us -> 224 us (0.45)
  waiting for transfers between devices: 362 us -> 33 us
  blocking collectives: 0 us -> 45.3 us
  Pallas kernels: 0 us -> 45.1 us
  starting transfers between devices: 42.8 us -> 83.1 us
  local copies, waits for them, and re-layouts: 39.6 us -> 9.98 us
  other arithmetic: 19.6 us -> 4 us
  between operations: 14.6 us -> 1.11 us
  matrix products: 13.3 us -> 0 us
    psum x1 -> x0, waiting for transfers between devices: 256 us -> none  [shards(): d_kernel = lax.psum(partial_value, ('dp', 'seq'))]
    all_gather x1 -> x0, waiting for transfers between devices: 83.8 us -> none  [shards(): lax.all_gather(proj_weight, 'seq', axis=0, tiled=True)]
    ppermute x4 -> x16, starting transfers between devices: 10.5 us -> 62.3 us  [the longest x4 31.2 us: swap(): return lax.ppermute(value, 'c', [(0, 1), (1, 0)])]
    all_to_all x0 -> x3, blocking collectives: none -> 45.3 us  [the longest x1 17.2 us: shards(): lax.all_to_all(in_vmem(landed_sum_kernel, tile, landed_d), 'z', 0, 0, til...]
    pallas_call x0 -> x12, Pallas kernels: none -> 45.1 us  [the longest x7 14.5 us: in_vmem(): pl.pallas_call(body, out_shape=out_shape, in_specs=[SMEM] * scalars + [VM...]
    ppermute x4 -> x16, waiting for transfers between devices: 0.01 us -> 13.5 us  [the longest x8 9.14 us: shift(): lax.ppermute(value, axis, [(i, (i + step) % size) for i in range(size)])]
    dot_general x2 -> x0, matrix products: 13.3 us -> none  [the longest x1 7.08 us: shards(): lax.dot_general(d_rows, lax.all_gather(proj_weight, 'seq', axis=0, tiled=...]
    all_to_all x4 -> x3, starting transfers between devices: 32.2 us -> 20.8 us  [exchange(): lax.all_to_all(sent, ('y', 'x'), 0, 0, tiled=True).reshape(count, width)]
  transfers between devices with their start and end apart: 10 -> 19, of which waited for: 4 -> 6; matrix products, arithmetic and copies ran while one was open for 12% -> 4% of each run, Pallas kernels for 0% -> 12%
where the time goes in v2:
time: 224 us; the launch traced here: 222 us
  starting transfers between devices  83.1 us (37%)
  blocking collectives  45.3 us (20%)
  Pallas kernels  45.1 us (20%)
  waiting for transfers between devices  33 us (15%)
  local copies, waits for them, and re-layouts  9.98 us (4%)
  other arithmetic  4 us (2%)
    ppermute x4, starting transfers between devices, swap(): return lax.ppermute(value, 'c', [(0, 1), (1, 0)])  31.2 us
    ppermute x8, starting transfers between devices, shift(): lax.ppermute(value, axis, [(i, (i + step) % size) for i in range(size)])  23.7 us
    all_to_all x3, starting transfers between devices, exchange(): lax.all_to_all(sent, ('y', 'x'), 0, 0, tiled=True).reshape(count, width)  20.8 us
    all_to_all x3, waiting for transfers between devices, exchange(): lax.all_to_all(sent, ('y', 'x'), 0, 0, tiled=True).reshape(count, width)  19.5 us
    all_to_all x1, blocking collectives, shards(): lax.all_to_all(in_vmem(landed_sum_kernel, tile, landed_d), 'z', 0, 0, til...  17.2 us
    pallas_call x7, Pallas kernels, in_vmem(): pl.pallas_call(body, out_shape=out_shape, in_specs=[SMEM] * scalars + [VM...  14.5 us
    all_to_all x1, blocking collectives, spread(): lax.all_to_all(jnp.broadcast_to(value[None], (size, *value.shape)), axis,...  14.2 us
    all_to_all x1, blocking collectives, sum_spread(): return lax.all_to_all(sent, axis, 0, 0, tiled=True)  13.9 us
  transfers between devices with their start and end apart: 19, of which 6 were waited for; matrix products, arithmetic and copies ran while one was open for 4% of the time, Pallas kernels for 12%

profile of v2, /device:TPU:1, one launch (start us, length us, event | category | flops | bytes accessed | tf_op | source)
XLA Modules:
  0.0 221.7 jit_solution(4504859712745478427)
XLA Ops:
  0.6 8.9 %collective-permute-start = (bf16[128,3840]{1,0:T(8,128)(2,1)}, bf16[128,3840]{1,0:T(8,128)(2,1)S(1)}, u32[]{:S(2)}, u32[]{:S(2)}) collective-permute-start(bf16[128,3840]{1,0:T(8,128)(2,1)} %bitcast.21), channel_id=1, source_target_pairs={{0,1},{1,0},{2,3},{3,2},{4,5},{5,4},{6,7},{7,6},{8,9},{9,8},{10,11... | collective-permute-start | bytes 2949128 | tf_op jit(solution)/shard_map/ppermute | solution.py:24
  9.6 1.0 broadcast_in_dim.6
  10.5 14.2 %all_to_all.30 = bf16[4,20,3840]{2,1,0:T(8,128)(2,1)S(1)} all-to-all(bf16[4,20,3840]{2,1,0:T(8,128)(2,1)S(1)} %broadcast_in_dim.6), channel_id=1, replica_groups=mesh['z'=8,'y'=8,'x'=4,'c'=2] {'x'}, dimensions={0} | all-to-all | bytes 1228800 | tf_op jit(solution)/shard_map/all_to_all | solution.py:28
  24.8 0.1 reshape.103.refs_0_
  24.9 2.1 collective-permute-start.2
  27.0 3.4 %collective-permute-start.1 = (bf16[80,3840]{1,0:T(8,128)(2,1)S(1)}, bf16[80,3840]{1,0:T(8,128)(2,1)}, u32[]{:S(2)}, u32[]{:S(2)}) collective-permute-start(bf16[80,3840]{1,0:T(8,128)(2,1)S(1)} %reshape.103.refs_0_), channel_id=1, source_target_pairs={{0,8},{8,16},{16,24},{24,32},{32,40},{40,48},{48,56},{56,0},{1,9},... | collective-permute-start | bytes 1843208 | tf_op jit(solution)/shard_map/ppermute | solution.py:34
  30.4 0.8 reshape.104
  31.2 3.9 %all-to-all-start.1 = ((bf16[32,4,1280]{2,1,0:T(4,128)(2,1)}), bf16[32,4,1280]{2,1,0:T(4,128)(2,1)S(1)}, u32[]{:S(2)}, u32[]{:S(2)}) async-start(bf16[32,4,1280]{2,1,0:T(4,128)(2,1)} %reshape.104), calls=%async_computation.1 | async-start | bytes 655360 | tf_op jit(solution)/shard_map/all_to_all | solution.py:398
  35.1 9.1 %collective-permute-done.2.refs_2_ = bf16[80,3840]{1,0:T(8,128)(2,1)S(1)} collective-permute-done((bf16[80,3840]{1,0:T(8,128)(2,1)S(1)}, bf16[80,3840]{1,0:T(8,128)(2,1)S(1)}, u32[]{:S(2)}, u32[]{:S(2)}) %collective-permute-start.2) | collective-permute-done | bytes 614432 | tf_op jit(solution)/shard_map/ppermute | solution.py:34
  44.2 1.9 collective-permute-start.5
  46.1 3.4 %collective-permute-start.4 = (bf16[80,3840]{1,0:T(8,128)(2,1)}, bf16[80,3840]{1,0:T(8,128)(2,1)}, u32[]{:S(2)}, u32[]{:S(2)}) collective-permute-start(bf16[80,3840]{1,0:T(8,128)(2,1)} %collective-permute-done.1.refs_1_), channel_id=1, source_target_pairs={{0,8},{8,16},{16,24},{24,32},{32,40},{40,48},{48,56},{56,0},{1,9},... | collective-permute-start | bytes 1843208 | tf_op jit(solution)/shard_map/ppermute | solution.py:34
  49.5 1.5 all-to-all-done.1
  51.1 0.1 reshape.105.rows_ref
  51.2 2.7 %shard_map.85 = (bf16[128,640]{1,0:T(8,128)(2,1)S(1)}, bf16[144,640]{1,0:T(8,128)(2,1)S(1)}, f32[27,640]{1,0:T(8,128)S(1)}) custom-call(s32[1,640]{1,0:T(1,128)S(1)} %get-tuple-element.64.own_ref.own_ch, s32[1,640]{1,0:T(1,128)S(1)} %get-tuple-element.63.other_ref.other_ch, bf16[128,1280]{1,0:T(8,128)(2,1)S(1)} %reshape.105.rows_ref, ...), custom_call_target="tpu_custom_call" | custom-call | tf_op jit(solution)/shard_map/pallas_call | solution.py:214
  53.9 0.6 copy-done.3
  54.5 0.7 copy-done.5
  55.2 6.0 %collective-permute-start.3 = (bf16[144,640]{1,0:T(8,128)(2,1)S(1)}, bf16[144,640]{1,0:T(8,128)(2,1)S(1)}, u32[]{:S(2)}, u32[]{:S(2)}) collective-permute-start(bf16[144,640]{1,0:T(8,128)(2,1)S(1)} %get-tuple-element.34), channel_id=1, source_target_pairs={{0,1},{1,0},{2,3},{3,2},{4,5},{5,4},{6,7},{7,6},{8,9},{9,8},{10,11... | collective-permute-start | bytes 552968 | tf_op jit(solution)/shard_map/ppermute | solution.py:24
  61.2 3.3 %collective-permute-start.6 = (bf16[80,3840]{1,0:T(8,128)(2,1)}, bf16[80,3840]{1,0:T(8,128)(2,1)S(1)}, u32[]{:S(2)}, u32[]{:S(2)}) collective-permute-start(bf16[80,3840]{1,0:T(8,128)(2,1)} %collective-permute-done.4.refs_3_), channel_id=1, source_target_pairs={{0,8},{8,16},{16,24},{24,32},{32,40},{40,48},{48,56},{56,0},{1,9},... | collective-permute-start | bytes 1843208 | tf_op jit(solution)/shard_map/ppermute | solution.py:34
  64.6 3.1 %collective-permute-start.7 = (bf16[80,3840]{1,0:T(8,128)(2,1)}, bf16[80,3840]{1,0:T(8,128)(2,1)S(1)}, u32[]{:S(2)}, u32[]{:S(2)}) collective-permute-start(bf16[80,3840]{1,0:T(8,128)(2,1)} %collective-permute-done.5.refs_4_), channel_id=1, source_target_pairs={{0,56},{8,0},{16,8},{24,16},{32,24},{40,32},{48,40},{56,48},{1,57}... | collective-permute-start | bytes 1843208 | tf_op jit(solution)/shard_map/ppermute | solution.py:34
  67.8 0.6 copy-done.18
  68.4 0.2 stack.21
  68.6 0.1 copy.16
  68.7 0.2 stack.22
  68.9 0.1 copy.17
  69.0 0.1 copy.19
  69.2 0.2 reshape.106
  69.3 0.5 broadcast_select_fusion.2
  69.9 2.0 shard_map.86
  71.9 2.3 %collective-permute-start.8 = (bf16[64,640]{1,0:T(8,128)(2,1)}, bf16[64,640]{1,0:T(8,128)(2,1)S(1)}, u32[]{:S(2)}, u32[]{:S(2)}) collective-permute-start(bf16[64,640]{1,0:T(8,128)(2,1)} %get-tuple-element.39), channel_id=1, source_target_pairs={{0,2},{2,4},{4,6},{6,8},{8,10},{10,12},{12,14},{14,16},{16,18},{18... | collective-permute-start | bytes 245768 | tf_op jit(solution)/shard_map/ppermute | solution.py:404
  74.2 1.3 collective-permute-start.9
  75.5 0.5 collective-permute-done.8.before_ref
  76.0 3.9 %collective-permute-done.9.after_ref = bf16[64,640]{1,0:T(8,128)(2,1)S(1)} collective-permute-done((bf16[64,640]{1,0:T(8,128)(2,1)}, bf16[64,640]{1,0:T(8,128)(2,1)S(1)}, u32[]{:S(2)}, u32[]{:S(2)}) %collective-permute-start.9) | collective-permute-done | bytes 81952 | tf_op jit(solution)/shard_map/ppermute | solution.py:404
  80.0 4.1 %collective-permute-start.10 = (bf16[48,3840]{1,0:T(8,128)(2,1)S(1)}, bf16[48,3840]{1,0:T(8,128)(2,1)S(1)}, u32[]{:S(2)}, u32[]{:S(2)}) collective-permute-start(bf16[48,3840]{1,0:T(8,128)(2,1)S(1)} %slice.10), channel_id=1, source_target_pairs={{0,8},{8,16},{16,24},{24,32},{32,40},{40,48},{48,56},{56,0},{1,9},... | collective-permute-start | bytes 1105928 | tf_op jit(solution)/shard_map/ppermute | solution.py:34
  84.1 0.7 slice.11
  84.8 2.4 %collective-permute-start.11 = (bf16[32,3840]{1,0:T(8,128)(2,1)}, bf16[32,3840]{1,0:T(8,128)(2,1)}, u32[]{:S(2)}, u32[]{:S(2)}) collective-permute-start(bf16[32,3840]{1,0:T(8,128)(2,1)} %slice.11), channel_id=1, source_target_pairs={{0,56},{8,0},{16,8},{24,16},{32,24},{40,32},{48,40},{56,48},{1,57}... | collective-permute-start | bytes 737288 | tf_op jit(solution)/shard_map/ppermute | solution.py:34
  87.2 0.6 pad_add_fusion.where_ref
  87.8 0.1 copy.18
  88.0 0.8 broadcast_in_dim_reshape.8.index_ref
  88.7 4.8 %shard_map.87.y_ref = bf16[256,640]{1,0:T(8,128)(2,1)} custom-call(s32[256,1]{1,0:T(8,128)} %broadcast_in_dim_reshape.8.index_ref, f32[27,640]{1,0:T(8,128)} %copy-done.3, bf16[64,640]{1,0:T(8,128)(2,1)} %copy-done.15, bf16[256,640]{1,0:T(8,128)(2,1)} %get-tuple-element.42.cells_ref, bf16[64,640]{1,0:T(8,128)(2,1)} %copy-done.16), custom_call_target="tpu_custom_call" | custom-call | tf_op jit(solution)/shard_map/pallas_call | solution.py:299
  93.6 0.7 copy-done.14
  94.4 8.0 %shard_map.88 = (bf16[256,1280]{1,0:T(8,128)(2,1)}, bf16[640,3840]{1,0:T(8,128)(2,1)}) custom-call(s32[2]{0:T(128)} %pad_add_fusion.where_ref, bf16[256,640]{1,0:T(8,128)(2,1)} %shard_map.87.y_ref, bf16[128,3840]{1,0:T(8,128)(2,1)} %bitcast.22, bf16[128,3840]{1,0:T(8,128)(2,1)} %copy-done.12, bf16[80,3840]{1,0:T(8,128)(2,1)} %copy-done.9, ...), custom_call_target="tpu_custom_call" | custom-call | tf_op jit(solution)/shard_map/pallas_call | solution.py:129
  102.4 8.6 %all-to-all-start.2 = ((bf16[32,8,1280]{2,1,0:T(8,128)(2,1)}), bf16[32,8,1280]{2,1,0:T(8,128)(2,1)S(1)}, u32[]{:S(2)}, u32[]{:S(2)}) async-start(bf16[32,8,1280]{2,1,0:T(8,128)(2,1)} %bitcast.24), calls=%async_computation.2 | async-start | bytes 1310720 | tf_op jit(solution)/shard_map/all_to_all | solution.py:398
  111.0 0.7 broadcast_in_dim_reshape.7.cell_ref
  111.7 13.1 %all-to-all-done.2 = bf16[32,8,1280]{2,1,0:T(8,128)(2,1)S(1)} async-done(((bf16[32,8,1280]{2,1,0:T(8,128)(2,1)}), bf16[32,8,1280]{2,1,0:T(8,128)(2,1)S(1)}, u32[]{:S(2)}, u32[]{:S(2)}) %all-to-all-start.2) | async-done | bytes 655392 | tf_op jit(solution)/shard_map/all_to_all | solution.py:398
  124.8 0.8 copy-done.8
  125.6 2.1 shard_map.89
  127.7 2.5 %collective-permute-start.12 = (bf16[64,640]{1,0:T(8,128)(2,1)}, bf16[64,640]{1,0:T(8,128)(2,1)S(1)}, u32[]{:S(2)}, u32[]{:S(2)}) collective-permute-start(bf16[64,640]{1,0:T(8,128)(2,1)} %get-tuple-element.47), channel_id=1, source_target_pairs={{0,2},{2,4},{4,6},{6,8},{8,10},{10,12},{12,14},{14,16},{16,18},{18... | collective-permute-start | bytes 245768 | tf_op jit(solution)/shard_map/ppermute | solution.py:404
  130.3 1.3 collective-permute-start.13
  131.6 4.9 %shard_map.90.sums_ref = f32[256,128]{1,0:T(8,128)} custom-call(bf16[256,640]{1,0:T(8,128)(2,1)} %get-tuple-element.48.grad_ref.cells_ref, bf16[64,640]{1,0:T(8,128)(2,1)} %copy-done.15, bf16[256,640]{1,0:T(8,128)(2,1)} %get-tuple-element.42.cells_ref, bf16[64,640]{1,0:T(8,128)(2,1)} %copy-done.16), custom_call_target="tpu_custom_call" | custom-call | tf_op jit(solution)/shard_map/pallas_call | solution.py:331
  136.5 0.6 copy-done.19
  137.1 0.6 copy-done.20
  137.8 5.5 %shard_map.91 = bf16[256,896]{1,0:T(8,128)(2,1)} custom-call(s32[256,1]{1,0:T(8,128)} %broadcast_in_dim_reshape.8.index_ref, f32[27,640]{1,0:T(8,128)} %copy-done.3, bf16[64,640]{1,0:T(8,128)(2,1)} %copy-done.19, bf16[256,640]{1,0:T(8,128)(2,1)} %get-tuple-element.48.grad_ref.cells_ref, bf16[64,640]{1,0:T(8,128)(2,1)} %copy-done.20, ...), custom_call_target="tpu_custom_call" | custom-call | tf_op jit(solution)/shard_map/pallas_call | solution.py:299
  143.3 8.4 %all-to-all-start.3 = ((bf16[32,8,896]{2,1,0:T(8,128)(2,1)}), bf16[32,8,896]{2,1,0:T(8,128)(2,1)S(1)}, u32[]{:S(2)}, u32[]{:S(2)}) async-start(bf16[32,8,896]{2,1,0:T(8,128)(2,1)} %bitcast.20), calls=%async_computation.3 | async-start | bytes 917504 | tf_op jit(solution)/shard_map/all_to_all | solution.py:398
  151.7 7.2 %shard_map.92 = (f32[128,3840]{1,0:T(8,128)}, f32[128,3840]{1,0:T(8,128)}) custom-call(s32[2]{0:T(128)} %pad_add_fusion.where_ref, bf16[256,1280]{1,0:T(8,128)(2,1)} %bitcast.19, bf16[640,3840]{1,0:T(8,128)(2,1)} %get-tuple-element.51.whole_ref), custom_call_target="tpu_custom_call" | custom-call | flops 1258291200 | bytes 20000000 | tf_op jit(solution)/shard_map/pallas_call | solution.py:160
  158.9 4.9 %all-to-all-done.3 = bf16[32,8,896]{2,1,0:T(8,128)(2,1)S(1)} async-done(((bf16[32,8,896]{2,1,0:T(8,128)(2,1)}), bf16[32,8,896]{2,1,0:T(8,128)(2,1)S(1)}, u32[]{:S(2)}, u32[]{:S(2)}) %all-to-all-start.3) | async-done | bytes 458784 | tf_op jit(solution)/shard_map/all_to_all | solution.py:398
  163.8 11.8 %collective-permute-start.14 = (f32[128,3840]{1,0:T(8,128)}, f32[128,3840]{1,0:T(8,128)S(1)}, u32[]{:S(2)}, u32[]{:S(2)}) collective-permute-start(f32[128,3840]{1,0:T(8,128)} %get-tuple-element.54), channel_id=1, source_target_pairs={{0,1},{1,0},{2,3},{3,2},{4,5},{5,4},{6,7},{7,6},{8,9},{9,8},{10,11... | collective-permute-start | bytes 5898248 | tf_op jit(solution)/shard_map/ppermute | solution.py:24
  175.6 1.7 shard_map.93
  177.3 17.2 %all_to_all.31.parts_ref = f32[8,8,128]{2,1,0:T(8,128)} all-to-all(f32[8,8,128]{2,1,0:T(8,128)} %shard_map.93), channel_id=1, replica_groups=mesh['z'=8,'y'=8,'x'=4,'c'=2] {'z'}, dimensions={0} | all-to-all | bytes 65536 | tf_op jit(solution)/shard_map/all_to_all | solution.py:469
  194.5 1.4 shard_map.94
  195.9 13.9 %all_to_all.32.tiles_ref = f32[32,8,128]{2,1,0:T(8,128)} all-to-all(f32[32,8,128]{2,1,0:T(8,128)} %shard_map.94), channel_id=1, replica_groups=mesh['z'=8,'y'=8,'x'=4,'c'=2] {'y','x'}, dimensions={0} | all-to-all | bytes 262144 | tf_op jit(solution)/shard_map/all_to_all | solution.py:392
  209.8 2.0 shard_map.95
  211.8 4.5 %collective-permute-start.15 = (bf16[224,640]{1,0:T(8,128)(2,1)}, bf16[224,640]{1,0:T(8,128)(2,1)S(1)}, u32[]{:S(2)}, u32[]{:S(2)}) collective-permute-start(bf16[224,640]{1,0:T(8,128)(2,1)} %shard_map.95), channel_id=1, source_target_pairs={{0,1},{1,0},{2,3},{3,2},{4,5},{5,4},{6,7},{7,6},{8,9},{9,8},{10,11... | collective-permute-start | bytes 860168 | tf_op jit(solution)/shard_map/ppermute | solution.py:24
  216.4 2.7 %add_convert_fusion = bf16[128,3840]{1,0:T(8,128)(2,1)} fusion(f32[128,3840]{1,0:T(8,128)} %get-tuple-element.52, f32[128,3840]{1,0:T(8,128)S(1)} %collective-permute-done.14), kind=kLoop, calls=%fused_computation | loop fusion | flops 983040 | bytes 4915200 | tf_op jit(solution)/shard_map/convert_element_type | solution.py:474
  219.1 2.6 %shard_map.96 = (bf16[128,1280]{1,0:T(8,128)(2,1)}, f32[27,1280]{1,0:T(8,128)}) custom-call(s32[2]{0:T(128)S(1)} %copy-done.6, s32[1,640]{1,0:T(1,128)S(1)} %get-tuple-element.64.own_ref.own_ch, s32[1,640]{1,0:T(1,128)S(1)} %get-tuple-element.63.other_ref.other_ch, bf16[256,896]{1,0:T(8,128)(2,1)S(1)} %bitcast.17, f32[32,8,128]{2,1,0:T(8,128)S(1)} %copy-done.2, ...), custom_call_target="tpu_custom_call" | custom-call | tf_op jit(solution)/shard_map/pallas_call | solution.py:214
  (54 shorter events, 0.3 us)
Async XLA Ops:
  0.6 29.7 %copy-start.17 = (bf16[1,128,1280]{2,1,0:T(8,128)(2,1)S(1)}, bf16[1,128,1280]{2,1,0:T(8,128)(2,1)}, u32[]{:S(2)}) copy-start(bf16[1,128,1280]{2,1,0:T(8,128)(2,1)} %param.6) | copy-start | bytes 983044
  0.6 24.1 %collective-permute-start = (bf16[128,3840]{1,0:T(8,128)(2,1)}, bf16[128,3840]{1,0:T(8,128)(2,1)S(1)}, u32[]{:S(2)}, u32[]{:S(2)}) collective-permute-start(bf16[128,3840]{1,0:T(8,128)(2,1)} %bitcast.21), channel_id=1, source_target_pairs={{0,1},{1,0},{2,3},{3,2},{4,5},{5,4},{6,7},{7,6},{8,9},{9,8},{10,11... | collective-permute-start | bytes 2949128 | tf_op jit(solution)/shard_map/ppermute | solution.py:24
  24.8 26.4 %copy-start.4 = (f32[27,1280]{1,0:T(8,128)S(1)}, f32[27,1280]{1,0:T(8,128)}, u32[]{:S(2)}) copy-start(f32[27,1280]{1,0:T(8,128)} %kernel_ref.1) | copy-start | bytes 414724
  24.8 26.4 %copy-start.7 = (s32[1,128]{1,0:T(1,128)S(1)}, s32[1,128]{1,0:T(1,128)}, u32[]{:S(2)}) copy-start(s32[1,128]{1,0:T(1,128)} %place_ref.1) | copy-start | bytes 1540
  24.8 44.1 %copy-start.12 = (bf16[128,3840]{1,0:T(8,128)(2,1)}, bf16[128,3840]{1,0:T(8,128)(2,1)S(1)}, u32[]{:S(2)}) copy-start(bf16[128,3840]{1,0:T(8,128)(2,1)S(1)} %collective-permute-done.other_ref) | copy-start | bytes 2949124
  24.9 59.9 %copy-start.9 = (bf16[80,3840]{1,0:T(8,128)(2,1)}, bf16[80,3840]{1,0:T(8,128)(2,1)S(1)}, u32[]{:S(2)}) copy-start(bf16[80,3840]{1,0:T(8,128)(2,1)S(1)} %reshape.103.refs_0_) | copy-start | bytes 1843204
  24.9 19.3 %collective-permute-start.2 = (bf16[80,3840]{1,0:T(8,128)(2,1)S(1)}, bf16[80,3840]{1,0:T(8,128)(2,1)S(1)}, u32[]{:S(2)}, u32[]{:S(2)}) collective-permute-start(bf16[80,3840]{1,0:T(8,128)(2,1)S(1)} %reshape.103.refs_0_), channel_id=1, source_target_pairs={{0,56},{8,0},{16,8},{24,16},{32,24},{40,32},{48,40},{56,48},{1,57}... | collective-permute-start | bytes 1843208 | tf_op jit(solution)/shard_map/ppermute | solution.py:34
  27.0 19.1 %collective-permute-start.1 = (bf16[80,3840]{1,0:T(8,128)(2,1)S(1)}, bf16[80,3840]{1,0:T(8,128)(2,1)}, u32[]{:S(2)}, u32[]{:S(2)}) collective-permute-start(bf16[80,3840]{1,0:T(8,128)(2,1)S(1)} %reshape.103.refs_0_), channel_id=1, source_target_pairs={{0,8},{8,16},{16,24},{24,32},{32,40},{40,48},{48,56},{56,0},{1,9},... | collective-permute-start | bytes 1843208 | tf_op jit(solution)/shard_map/ppermute | solution.py:34
  31.2 19.9 %all-to-all-start.1 = ((bf16[32,4,1280]{2,1,0:T(4,128)(2,1)}), bf16[32,4,1280]{2,1,0:T(4,128)(2,1)S(1)}, u32[]{:S(2)}, u32[]{:S(2)}) async-start(bf16[32,4,1280]{2,1,0:T(4,128)(2,1)} %reshape.104), calls=%async_computation.1 | async-start | bytes 655360 | tf_op jit(solution)/shard_map/all_to_all | solution.py:398
  44.2 49.4 %copy-start.13 = (bf16[80,3840]{1,0:T(8,128)(2,1)}, bf16[80,3840]{1,0:T(8,128)(2,1)S(1)}, u32[]{:S(2)}) copy-start(bf16[80,3840]{1,0:T(8,128)(2,1)S(1)} %collective-permute-done.2.refs_2_) | copy-start | bytes 1843204
  44.2 17.0 %collective-permute-start.5 = (bf16[80,3840]{1,0:T(8,128)(2,1)S(1)}, bf16[80,3840]{1,0:T(8,128)(2,1)}, u32[]{:S(2)}, u32[]{:S(2)}) collective-permute-start(bf16[80,3840]{1,0:T(8,128)(2,1)S(1)} %collective-permute-done.2.refs_2_), channel_id=1, source_target_pairs={{0,56},{8,0},{16,8},{24,16},{32,24},{40,32},{48,40},{56,48},{1,57}... | collective-permute-start | bytes 1843208 | tf_op jit(solution)/shard_map/ppermute | solution.py:34
  46.1 15.1 %collective-permute-start.4 = (bf16[80,3840]{1,0:T(8,128)(2,1)}, bf16[80,3840]{1,0:T(8,128)(2,1)}, u32[]{:S(2)}, u32[]{:S(2)}) collective-permute-start(bf16[80,3840]{1,0:T(8,128)(2,1)} %collective-permute-done.1.refs_1_), channel_id=1, source_target_pairs={{0,8},{8,16},{16,24},{24,32},{32,40},{40,48},{48,56},{56,0},{1,9},... | collective-permute-start | bytes 1843208 | tf_op jit(solution)/shard_map/ppermute | solution.py:34
  53.9 0.6 copy-start.3
  54.5 0.7 copy-start.5
  55.2 12.5 %collective-permute-start.3 = (bf16[144,640]{1,0:T(8,128)(2,1)S(1)}, bf16[144,640]{1,0:T(8,128)(2,1)S(1)}, u32[]{:S(2)}, u32[]{:S(2)}) collective-permute-start(bf16[144,640]{1,0:T(8,128)(2,1)S(1)} %get-tuple-element.34), channel_id=1, source_target_pairs={{0,1},{1,0},{2,3},{3,2},{4,5},{5,4},{6,7},{7,6},{8,9},{9,8},{10,11... | collective-permute-start | bytes 552968 | tf_op jit(solution)/shard_map/ppermute | solution.py:24
  61.2 18.7 %collective-permute-start.6 = (bf16[80,3840]{1,0:T(8,128)(2,1)}, bf16[80,3840]{1,0:T(8,128)(2,1)S(1)}, u32[]{:S(2)}, u32[]{:S(2)}) collective-permute-start(bf16[80,3840]{1,0:T(8,128)(2,1)} %collective-permute-done.4.refs_3_), channel_id=1, source_target_pairs={{0,8},{8,16},{16,24},{24,32},{32,40},{40,48},{48,56},{56,0},{1,9},... | collective-permute-start | bytes 1843208 | tf_op jit(solution)/shard_map/ppermute | solution.py:34
  64.6 15.4 %collective-permute-start.7 = (bf16[80,3840]{1,0:T(8,128)(2,1)}, bf16[80,3840]{1,0:T(8,128)(2,1)S(1)}, u32[]{:S(2)}, u32[]{:S(2)}) collective-permute-start(bf16[80,3840]{1,0:T(8,128)(2,1)} %collective-permute-done.5.refs_4_), channel_id=1, source_target_pairs={{0,56},{8,0},{16,8},{24,16},{32,24},{40,32},{48,40},{56,48},{1,57}... | collective-permute-start | bytes 1843208 | tf_op jit(solution)/shard_map/ppermute | solution.py:34
  67.8 0.7 copy-start.18
  71.9 4.1 %collective-permute-start.8 = (bf16[64,640]{1,0:T(8,128)(2,1)}, bf16[64,640]{1,0:T(8,128)(2,1)S(1)}, u32[]{:S(2)}, u32[]{:S(2)}) collective-permute-start(bf16[64,640]{1,0:T(8,128)(2,1)} %get-tuple-element.39), channel_id=1, source_target_pairs={{0,2},{2,4},{4,6},{6,8},{8,10},{10,12},{12,14},{14,16},{16,18},{18... | collective-permute-start | bytes 245768 | tf_op jit(solution)/shard_map/ppermute | solution.py:404
  74.2 5.7 %collective-permute-start.9 = (bf16[64,640]{1,0:T(8,128)(2,1)}, bf16[64,640]{1,0:T(8,128)(2,1)S(1)}, u32[]{:S(2)}, u32[]{:S(2)}) collective-permute-start(bf16[64,640]{1,0:T(8,128)(2,1)} %get-tuple-element.40), channel_id=1, source_target_pairs={{2,0},{4,2},{6,4},{8,6},{10,8},{12,10},{14,12},{16,14},{18,16},{20... | collective-permute-start | bytes 245768 | tf_op jit(solution)/shard_map/ppermute | solution.py:404
  76.0 12.7 %copy-start.15 = (bf16[64,640]{1,0:T(8,128)(2,1)}, bf16[64,640]{1,0:T(8,128)(2,1)S(1)}, u32[]{:S(2)}) copy-start(bf16[64,640]{1,0:T(8,128)(2,1)S(1)} %collective-permute-done.8.before_ref) | copy-start | bytes 245764
  79.9 8.8 %copy-start.16 = (bf16[64,640]{1,0:T(8,128)(2,1)}, bf16[64,640]{1,0:T(8,128)(2,1)S(1)}, u32[]{:S(2)}) copy-start(bf16[64,640]{1,0:T(8,128)(2,1)S(1)} %collective-permute-done.9.after_ref) | copy-start | bytes 245764
  79.9 13.7 %copy-start.10 = (bf16[80,3840]{1,0:T(8,128)(2,1)}, bf16[80,3840]{1,0:T(8,128)(2,1)S(1)}, u32[]{:S(2)}) copy-start(bf16[80,3840]{1,0:T(8,128)(2,1)S(1)} %collective-permute-done.6.refs_5_) | copy-start | bytes 1843204
  80.0 13.7 %copy-start.11 = (bf16[80,3840]{1,0:T(8,128)(2,1)}, bf16[80,3840]{1,0:T(8,128)(2,1)S(1)}, u32[]{:S(2)}) copy-start(bf16[80,3840]{1,0:T(8,128)(2,1)S(1)} %collective-permute-done.7.refs_6_) | copy-start | bytes 1843204
  80.0 13.6 %collective-permute-start.10 = (bf16[48,3840]{1,0:T(8,128)(2,1)S(1)}, bf16[48,3840]{1,0:T(8,128)(2,1)S(1)}, u32[]{:S(2)}, u32[]{:S(2)}) collective-permute-start(bf16[48,3840]{1,0:T(8,128)(2,1)S(1)} %slice.10), channel_id=1, source_target_pairs={{0,8},{8,16},{16,24},{24,32},{32,40},{40,48},{48,56},{56,0},{1,9},... | collective-permute-start | bytes 1105928 | tf_op jit(solution)/shard_map/ppermute | solution.py:34
  84.8 8.8 %collective-permute-start.11 = (bf16[32,3840]{1,0:T(8,128)(2,1)}, bf16[32,3840]{1,0:T(8,128)(2,1)}, u32[]{:S(2)}, u32[]{:S(2)}) collective-permute-start(bf16[32,3840]{1,0:T(8,128)(2,1)} %slice.11), channel_id=1, source_target_pairs={{0,56},{8,0},{16,8},{24,16},{32,24},{40,32},{48,40},{56,48},{1,57}... | collective-permute-start | bytes 737288 | tf_op jit(solution)/shard_map/ppermute | solution.py:34
  93.6 0.8 copy-start.14
  102.4 22.4 %all-to-all-start.2 = ((bf16[32,8,1280]{2,1,0:T(8,128)(2,1)}), bf16[32,8,1280]{2,1,0:T(8,128)(2,1)S(1)}, u32[]{:S(2)}, u32[]{:S(2)}) async-start(bf16[32,8,1280]{2,1,0:T(8,128)(2,1)} %bitcast.24), calls=%async_computation.2 | async-start | bytes 1310720 | tf_op jit(solution)/shard_map/all_to_all | solution.py:398
  124.8 0.8 copy-start.8
  127.7 8.8 %collective-permute-start.12 = (bf16[64,640]{1,0:T(8,128)(2,1)}, bf16[64,640]{1,0:T(8,128)(2,1)S(1)}, u32[]{:S(2)}, u32[]{:S(2)}) collective-permute-start(bf16[64,640]{1,0:T(8,128)(2,1)} %get-tuple-element.47), channel_id=1, source_target_pairs={{0,2},{2,4},{4,6},{6,8},{8,10},{10,12},{12,14},{14,16},{16,18},{18... | collective-permute-start | bytes 245768 | tf_op jit(solution)/shard_map/ppermute | solution.py:404
  130.3 6.2 %collective-permute-start.13 = (bf16[64,640]{1,0:T(8,128)(2,1)}, bf16[64,640]{1,0:T(8,128)(2,1)S(1)}, u32[]{:S(2)}, u32[]{:S(2)}) collective-permute-start(bf16[64,640]{1,0:T(8,128)(2,1)} %get-tuple-element.49), channel_id=1, source_target_pairs={{2,0},{4,2},{6,4},{8,6},{10,8},{12,10},{14,12},{16,14},{18,16},{20... | collective-permute-start | bytes 245768 | tf_op jit(solution)/shard_map/ppermute | solution.py:404
  136.5 0.6 copy-start.19
  137.1 0.6 copy-start.20
  143.3 20.5 %all-to-all-start.3 = ((bf16[32,8,896]{2,1,0:T(8,128)(2,1)}), bf16[32,8,896]{2,1,0:T(8,128)(2,1)S(1)}, u32[]{:S(2)}, u32[]{:S(2)}) async-start(bf16[32,8,896]{2,1,0:T(8,128)(2,1)} %bitcast.20), calls=%async_computation.3 | async-start | bytes 917504 | tf_op jit(solution)/shard_map/all_to_all | solution.py:398
  163.8 11.8 %copy-start = (bf16[32,8,896]{2,1,0:T(8,128)(2,1)}, bf16[32,8,896]{2,1,0:T(8,128)(2,1)S(1)}, u32[]{:S(2)}) copy-start(bf16[32,8,896]{2,1,0:T(8,128)(2,1)S(1)} %all-to-all-done.3) | copy-start | bytes 1376260
  163.8 52.5 %collective-permute-start.14 = (f32[128,3840]{1,0:T(8,128)}, f32[128,3840]{1,0:T(8,128)S(1)}, u32[]{:S(2)}, u32[]{:S(2)}) collective-permute-start(f32[128,3840]{1,0:T(8,128)} %get-tuple-element.54), channel_id=1, source_target_pairs={{0,1},{1,0},{2,3},{3,2},{4,5},{5,4},{6,7},{7,6},{8,9},{9,8},{10,11... | collective-permute-start | bytes 5898248 | tf_op jit(solution)/shard_map/ppermute | solution.py:24
  211.8 7.3 %collective-permute-start.15 = (bf16[224,640]{1,0:T(8,128)(2,1)}, bf16[224,640]{1,0:T(8,128)(2,1)S(1)}, u32[]{:S(2)}, u32[]{:S(2)}) collective-permute-start(bf16[224,640]{1,0:T(8,128)(2,1)} %shard_map.95), channel_id=1, source_target_pairs={{0,1},{1,0},{2,3},{3,2},{4,5},{5,4},{6,7},{7,6},{8,9},{9,8},{10,11... | collective-permute-start | bytes 860168 | tf_op jit(solution)/shard_map/ppermute | solution.py:24
  216.3 2.8 %copy-start.1 = (bf16[32,8,896]{2,1,0:T(8,128)(2,1)S(1)}, bf16[32,8,896]{2,1,0:T(8,128)(2,1)}, u32[]{:S(2)}) copy-start(bf16[32,8,896]{2,1,0:T(8,128)(2,1)} %copy-done) | copy-start | bytes 1376260
  216.3 2.7 %copy-start.2 = (f32[32,8,128]{2,1,0:T(8,128)S(1)}, f32[32,8,128]{2,1,0:T(8,128)}, u32[]{:S(2)}) copy-start(f32[32,8,128]{2,1,0:T(8,128)} %all_to_all.32.tiles_ref) | copy-start | bytes 393220
  216.4 2.7 %copy-start.6 = (s32[2]{0:T(128)S(1)}, s32[2]{0:T(128)}, u32[]{:S(2)}) copy-start(s32[2]{0:T(128)} %pad_add_fusion.where_ref) | copy-start | bytes 28

commit v3 on v2

--- a/solution.py
+++ b/solution.py
@@ -468,11 +468,11 @@
     tile = jax.ShapeDtypeStruct((planes, 8, 128), F32)
     tiles = lax.all_to_all(in_vmem(landed_sum_kernel, tile, landed_d), "z", 0, 0, tiled=True)
     tiles = sum_spread(tiles, ("y", "x"), CHIPS)
+    projected = (keep + swap(after(send, landed_d))).astype(BF16)
+    tiles, projected = lax.optimization_barrier((tiles, projected))
     packed = jax.ShapeDtypeStruct((TOK + 96, local), BF16)
     d_other = swap(in_vmem(pack_kernel, packed, where, landed_d, tiles, scalars=1))
 
-    projected = (keep + swap(after(send, landed_d))).astype(BF16)
-    projected, d_other = lax.optimization_barrier((projected, d_other))
     d_tokens, d_kernel = in_vmem(
         last_kernel,
         (

time: 224 us -> 223 us (level)
  blocking collectives: 45.3 us -> 31.4 us
  waiting for transfers between devices: 33 us -> 41 us
  starting transfers between devices: 83.1 us -> 87.4 us
    all_to_all x1 -> x0, blocking collectives: 13.9 us -> none  [sum_spread(): return lax.all_to_all(sent, axis, 0, 0, tiled=True)]
    all_to_all x0 -> x1, waiting for transfers between devices: none -> 6.6 us  [sum_spread(): return lax.all_to_all(sent, axis, 0, 0, tiled=True)]
    all_to_all x0 -> x1, starting transfers between devices: none -> 3.93 us  [sum_spread(): return lax.all_to_all(sent, axis, 0, 0, tiled=True)]
    unnamed x42 -> x44, local copies, waits for them, and re-layouts: 4.81 us -> 6.38 us
  transfers between devices with their start and end apart: 19 -> 20, of which waited for: 6 -> 8; matrix products, arithmetic and copies ran while one was open for 4% -> 4% of each run, Pallas kernels for 12% -> 11%
where the time goes in v3:
time: 223 us; the launch traced here: 222 us
  starting transfers between devices  87.4 us (39%)
  Pallas kernels  45.1 us (20%)
  waiting for transfers between devices  41 us (18%)
  blocking collectives  31.4 us (14%)
  local copies, waits for them, and re-layouts  11.6 us (5%)
  other arithmetic  4.01 us (2%)
    ppermute x4, starting transfers between devices, swap(): return lax.ppermute(value, 'c', [(0, 1), (1, 0)])  31.5 us
    ppermute x8, starting transfers between devices, shift(): lax.ppermute(value, axis, [(i, (i + step) % size) for i in range(size)])  23.7 us
    all_to_all x3, starting transfers between devices, exchange(): lax.all_to_all(sent, ('y', 'x'), 0, 0, tiled=True).reshape(count, width)  20.8 us
    all_to_all x3, waiting for transfers between devices, exchange(): lax.all_to_all(sent, ('y', 'x'), 0, 0, tiled=True).reshape(count, width)  19.5 us
    all_to_all x1, blocking collectives, shards(): lax.all_to_all(in_vmem(landed_sum_kernel, tile, landed_d), 'z', 0, 0, til...  17.2 us
    pallas_call x7, Pallas kernels, in_vmem(): pl.pallas_call(body, out_shape=out_shape, in_specs=[SMEM] * scalars + [VM...  14.5 us
    all_to_all x1, blocking collectives, spread(): lax.all_to_all(jnp.broadcast_to(value[None], (size, *value.shape)), axis,...  14.2 us
    pallas_call x2, Pallas kernels, conv_rows(): pl.pallas_call(functools.partial(conv_body, False) if sums is None else b...  10.4 us
  transfers between devices with their start and end apart: 20, of which 8 were waited for; matrix products, arithmetic and copies ran while one was open for 4% of the time, Pallas kernels for 11%

profile of v3, /device:TPU:1, one launch (start us, length us, event | category | flops | bytes accessed | tf_op | source)
XLA Modules:
  0.0 221.5 jit_solution(3291941451383103500)
XLA Ops:
  0.6 8.9 %collective-permute-start = (bf16[128,3840]{1,0:T(8,128)(2,1)}, bf16[128,3840]{1,0:T(8,128)(2,1)S(1)}, u32[]{:S(2)}, u32[]{:S(2)}) collective-permute-start(bf16[128,3840]{1,0:T(8,128)(2,1)} %bitcast.21), channel_id=1, source_target_pairs={{0,1},{1,0},{2,3},{3,2},{4,5},{5,4},{6,7},{7,6},{8,9},{9,8},{10,11... | collective-permute-start | bytes 2949128 | tf_op jit(solution)/shard_map/ppermute | solution.py:24
  9.6 1.0 broadcast_in_dim.6
  10.5 14.2 %all_to_all.30 = bf16[4,20,3840]{2,1,0:T(8,128)(2,1)S(1)} all-to-all(bf16[4,20,3840]{2,1,0:T(8,128)(2,1)S(1)} %broadcast_in_dim.6), channel_id=1, replica_groups=mesh['z'=8,'y'=8,'x'=4,'c'=2] {'x'}, dimensions={0} | all-to-all | bytes 1228800 | tf_op jit(solution)/shard_map/all_to_all | solution.py:28
  24.8 0.1 reshape.103.refs_0_
  24.9 2.1 collective-permute-start.2
  27.0 3.4 %collective-permute-start.1 = (bf16[80,3840]{1,0:T(8,128)(2,1)S(1)}, bf16[80,3840]{1,0:T(8,128)(2,1)}, u32[]{:S(2)}, u32[]{:S(2)}) collective-permute-start(bf16[80,3840]{1,0:T(8,128)(2,1)S(1)} %reshape.103.refs_0_), channel_id=1, source_target_pairs={{0,8},{8,16},{16,24},{24,32},{32,40},{40,48},{48,56},{56,0},{1,9},... | collective-permute-start | bytes 1843208 | tf_op jit(solution)/shard_map/ppermute | solution.py:34
  30.4 0.8 reshape.104
  31.2 3.9 %all-to-all-start.1 = ((bf16[32,4,1280]{2,1,0:T(4,128)(2,1)}), bf16[32,4,1280]{2,1,0:T(4,128)(2,1)S(1)}, u32[]{:S(2)}, u32[]{:S(2)}) async-start(bf16[32,4,1280]{2,1,0:T(4,128)(2,1)} %reshape.104), calls=%async_computation.1 | async-start | bytes 655360 | tf_op jit(solution)/shard_map/all_to_all | solution.py:398
  35.1 9.1 %collective-permute-done.2.refs_2_ = bf16[80,3840]{1,0:T(8,128)(2,1)S(1)} collective-permute-done((bf16[80,3840]{1,0:T(8,128)(2,1)S(1)}, bf16[80,3840]{1,0:T(8,128)(2,1)S(1)}, u32[]{:S(2)}, u32[]{:S(2)}) %collective-permute-start.2) | collective-permute-done | bytes 614432 | tf_op jit(solution)/shard_map/ppermute | solution.py:34
  44.2 1.9 collective-permute-start.5
  46.1 3.4 %collective-permute-start.4 = (bf16[80,3840]{1,0:T(8,128)(2,1)}, bf16[80,3840]{1,0:T(8,128)(2,1)}, u32[]{:S(2)}, u32[]{:S(2)}) collective-permute-start(bf16[80,3840]{1,0:T(8,128)(2,1)} %collective-permute-done.1.refs_1_), channel_id=1, source_target_pairs={{0,8},{8,16},{16,24},{24,32},{32,40},{40,48},{48,56},{56,0},{1,9},... | collective-permute-start | bytes 1843208 | tf_op jit(solution)/shard_map/ppermute | solution.py:34
  49.5 1.5 all-to-all-done.1
  51.2 2.7 %shard_map.85 = (bf16[128,640]{1,0:T(8,128)(2,1)S(1)}, bf16[144,640]{1,0:T(8,128)(2,1)S(1)}, f32[27,640]{1,0:T(8,128)S(1)}) custom-call(s32[1,640]{1,0:T(1,128)S(1)} %get-tuple-element.64.own_ref.own_ch, s32[1,640]{1,0:T(1,128)S(1)} %get-tuple-element.63.other_ref.other_ch, bf16[128,1280]{1,0:T(8,128)(2,1)S(1)} %reshape.105.rows_ref, ...), custom_call_target="tpu_custom_call" | custom-call | tf_op jit(solution)/shard_map/pallas_call | solution.py:214
  53.9 0.6 copy-done.4
  54.5 0.7 copy-done.6
  55.2 6.0 %collective-permute-start.3 = (bf16[144,640]{1,0:T(8,128)(2,1)S(1)}, bf16[144,640]{1,0:T(8,128)(2,1)S(1)}, u32[]{:S(2)}, u32[]{:S(2)}) collective-permute-start(bf16[144,640]{1,0:T(8,128)(2,1)S(1)} %get-tuple-element.34), channel_id=1, source_target_pairs={{0,1},{1,0},{2,3},{3,2},{4,5},{5,4},{6,7},{7,6},{8,9},{9,8},{10,11... | collective-permute-start | bytes 552968 | tf_op jit(solution)/shard_map/ppermute | solution.py:24
  61.2 3.3 %collective-permute-start.6 = (bf16[80,3840]{1,0:T(8,128)(2,1)}, bf16[80,3840]{1,0:T(8,128)(2,1)S(1)}, u32[]{:S(2)}, u32[]{:S(2)}) collective-permute-start(bf16[80,3840]{1,0:T(8,128)(2,1)} %collective-permute-done.4.refs_3_), channel_id=1, source_target_pairs={{0,8},{8,16},{16,24},{24,32},{32,40},{40,48},{48,56},{56,0},{1,9},... | collective-permute-start | bytes 1843208 | tf_op jit(solution)/shard_map/ppermute | solution.py:34
  64.6 3.1 %collective-permute-start.7 = (bf16[80,3840]{1,0:T(8,128)(2,1)}, bf16[80,3840]{1,0:T(8,128)(2,1)S(1)}, u32[]{:S(2)}, u32[]{:S(2)}) collective-permute-start(bf16[80,3840]{1,0:T(8,128)(2,1)} %collective-permute-done.5.refs_4_), channel_id=1, source_target_pairs={{0,56},{8,0},{16,8},{24,16},{32,24},{40,32},{48,40},{56,48},{1,57}... | collective-permute-start | bytes 1843208 | tf_op jit(solution)/shard_map/ppermute | solution.py:34
  67.8 0.6 copy-done.19
  68.4 0.2 stack.18
  68.7 0.2 stack.19
  69.1 0.2 reshape.106
  69.3 0.6 broadcast_select_fusion.2
  69.9 2.0 shard_map.86
  71.9 2.3 %collective-permute-start.8 = (bf16[64,640]{1,0:T(8,128)(2,1)}, bf16[64,640]{1,0:T(8,128)(2,1)S(1)}, u32[]{:S(2)}, u32[]{:S(2)}) collective-permute-start(bf16[64,640]{1,0:T(8,128)(2,1)} %get-tuple-element.39), channel_id=1, source_target_pairs={{0,2},{2,4},{4,6},{6,8},{8,10},{10,12},{12,14},{14,16},{16,18},{18... | collective-permute-start | bytes 245768 | tf_op jit(solution)/shard_map/ppermute | solution.py:404
  74.3 1.3 collective-permute-start.9
  75.6 0.5 collective-permute-done.8.before_ref
  76.0 3.9 %collective-permute-done.9.after_ref = bf16[64,640]{1,0:T(8,128)(2,1)S(1)} collective-permute-done((bf16[64,640]{1,0:T(8,128)(2,1)}, bf16[64,640]{1,0:T(8,128)(2,1)S(1)}, u32[]{:S(2)}, u32[]{:S(2)}) %collective-permute-start.9) | collective-permute-done | bytes 81952 | tf_op jit(solution)/shard_map/ppermute | solution.py:404
  80.0 4.1 %collective-permute-start.10 = (bf16[48,3840]{1,0:T(8,128)(2,1)S(1)}, bf16[48,3840]{1,0:T(8,128)(2,1)S(1)}, u32[]{:S(2)}, u32[]{:S(2)}) collective-permute-start(bf16[48,3840]{1,0:T(8,128)(2,1)S(1)} %slice.10), channel_id=1, source_target_pairs={{0,8},{8,16},{16,24},{24,32},{32,40},{40,48},{48,56},{56,0},{1,9},... | collective-permute-start | bytes 1105928 | tf_op jit(solution)/shard_map/ppermute | solution.py:34
  84.1 0.7 slice.11
  84.9 2.4 %collective-permute-start.11 = (bf16[32,3840]{1,0:T(8,128)(2,1)}, bf16[32,3840]{1,0:T(8,128)(2,1)}, u32[]{:S(2)}, u32[]{:S(2)}) collective-permute-start(bf16[32,3840]{1,0:T(8,128)(2,1)} %slice.11), channel_id=1, source_target_pairs={{0,56},{8,0},{16,8},{24,16},{32,24},{40,32},{48,40},{56,48},{1,57}... | collective-permute-start | bytes 737288 | tf_op jit(solution)/shard_map/ppermute | solution.py:34
  87.2 0.6 pad_add_fusion.where_ref
  87.8 0.1 copy.18
  88.0 0.8 broadcast_in_dim_reshape.8.index_ref
  88.8 4.9 %shard_map.87.y_ref = bf16[256,640]{1,0:T(8,128)(2,1)} custom-call(s32[256,1]{1,0:T(8,128)} %broadcast_in_dim_reshape.8.index_ref, f32[27,640]{1,0:T(8,128)} %copy-done.4, bf16[64,640]{1,0:T(8,128)(2,1)} %copy-done.16, bf16[256,640]{1,0:T(8,128)(2,1)} %get-tuple-element.42.cells_ref, bf16[64,640]{1,0:T(8,128)(2,1)} %copy-done.17), custom_call_target="tpu_custom_call" | custom-call | tf_op jit(solution)/shard_map/pallas_call | solution.py:299
  93.7 0.8 copy-done.15
  94.4 8.0 %shard_map.88 = (bf16[256,1280]{1,0:T(8,128)(2,1)}, bf16[640,3840]{1,0:T(8,128)(2,1)}) custom-call(s32[2]{0:T(128)} %pad_add_fusion.where_ref, bf16[256,640]{1,0:T(8,128)(2,1)} %shard_map.87.y_ref, bf16[128,3840]{1,0:T(8,128)(2,1)} %bitcast.22, bf16[128,3840]{1,0:T(8,128)(2,1)} %copy-done.13, bf16[80,3840]{1,0:T(8,128)(2,1)} %copy-done.10, ...), custom_call_target="tpu_custom_call" | custom-call | tf_op jit(solution)/shard_map/pallas_call | solution.py:129
  102.5 8.6 %all-to-all-start.2 = ((bf16[32,8,1280]{2,1,0:T(8,128)(2,1)}), bf16[32,8,1280]{2,1,0:T(8,128)(2,1)S(1)}, u32[]{:S(2)}, u32[]{:S(2)}) async-start(bf16[32,8,1280]{2,1,0:T(8,128)(2,1)} %bitcast.24), calls=%async_computation.2 | async-start | bytes 1310720 | tf_op jit(solution)/shard_map/all_to_all | solution.py:398
  111.0 0.7 broadcast_in_dim_reshape.7.cell_ref
  111.7 13.1 %all-to-all-done.2 = bf16[32,8,1280]{2,1,0:T(8,128)(2,1)S(1)} async-done(((bf16[32,8,1280]{2,1,0:T(8,128)(2,1)}), bf16[32,8,1280]{2,1,0:T(8,128)(2,1)S(1)}, u32[]{:S(2)}, u32[]{:S(2)}) %all-to-all-start.2) | async-done | bytes 655392 | tf_op jit(solution)/shard_map/all_to_all | solution.py:398
  124.8 0.8 copy-done.9
  125.6 2.1 shard_map.89
  127.8 2.5 %collective-permute-start.12 = (bf16[64,640]{1,0:T(8,128)(2,1)}, bf16[64,640]{1,0:T(8,128)(2,1)S(1)}, u32[]{:S(2)}, u32[]{:S(2)}) collective-permute-start(bf16[64,640]{1,0:T(8,128)(2,1)} %get-tuple-element.47), channel_id=1, source_target_pairs={{0,2},{2,4},{4,6},{6,8},{8,10},{10,12},{12,14},{14,16},{16,18},{18... | collective-permute-start | bytes 245768 | tf_op jit(solution)/shard_map/ppermute | solution.py:404
  130.3 1.3 collective-permute-start.13
  131.6 4.9 %shard_map.90.sums_ref = f32[256,128]{1,0:T(8,128)} custom-call(bf16[256,640]{1,0:T(8,128)(2,1)} %get-tuple-element.48.grad_ref.cells_ref, bf16[64,640]{1,0:T(8,128)(2,1)} %copy-done.16, bf16[256,640]{1,0:T(8,128)(2,1)} %get-tuple-element.42.cells_ref, bf16[64,640]{1,0:T(8,128)(2,1)} %copy-done.17), custom_call_target="tpu_custom_call" | custom-call | tf_op jit(solution)/shard_map/pallas_call | solution.py:331
  136.5 0.6 copy-done.20
  137.2 0.6 copy-done.21
  137.8 5.5 %shard_map.91 = bf16[256,896]{1,0:T(8,128)(2,1)} custom-call(s32[256,1]{1,0:T(8,128)} %broadcast_in_dim_reshape.8.index_ref, f32[27,640]{1,0:T(8,128)} %copy-done.4, bf16[64,640]{1,0:T(8,128)(2,1)} %copy-done.20, bf16[256,640]{1,0:T(8,128)(2,1)} %get-tuple-element.48.grad_ref.cells_ref, bf16[64,640]{1,0:T(8,128)(2,1)} %copy-done.21, ...), custom_call_target="tpu_custom_call" | custom-call | tf_op jit(solution)/shard_map/pallas_call | solution.py:299
  143.3 8.4 %all-to-all-start.3 = ((bf16[32,8,896]{2,1,0:T(8,128)(2,1)}), bf16[32,8,896]{2,1,0:T(8,128)(2,1)S(1)}, u32[]{:S(2)}, u32[]{:S(2)}) async-start(bf16[32,8,896]{2,1,0:T(8,128)(2,1)} %bitcast.20), calls=%async_computation.3 | async-start | bytes 917504 | tf_op jit(solution)/shard_map/all_to_all | solution.py:398
  151.7 7.2 %shard_map.94 = (f32[128,3840]{1,0:T(8,128)}, f32[128,3840]{1,0:T(8,128)}) custom-call(s32[2]{0:T(128)} %pad_add_fusion.where_ref, bf16[256,1280]{1,0:T(8,128)(2,1)} %bitcast.19, bf16[640,3840]{1,0:T(8,128)(2,1)} %get-tuple-element.51.whole_ref), custom_call_target="tpu_custom_call" | custom-call | flops 1258291200 | bytes 20000000 | tf_op jit(solution)/shard_map/pallas_call | solution.py:160
  159.0 4.9 %all-to-all-done.3 = bf16[32,8,896]{2,1,0:T(8,128)(2,1)S(1)} async-done(((bf16[32,8,896]{2,1,0:T(8,128)(2,1)}), bf16[32,8,896]{2,1,0:T(8,128)(2,1)S(1)}, u32[]{:S(2)}, u32[]{:S(2)}) %all-to-all-start.3) | async-done | bytes 458784 | tf_op jit(solution)/shard_map/all_to_all | solution.py:398
  163.9 11.8 %collective-permute-start.14 = (f32[128,3840]{1,0:T(8,128)}, f32[128,3840]{1,0:T(8,128)S(1)}, u32[]{:S(2)}, u32[]{:S(2)}) collective-permute-start(f32[128,3840]{1,0:T(8,128)} %get-tuple-element.54), channel_id=1, source_target_pairs={{0,1},{1,0},{2,3},{3,2},{4,5},{5,4},{6,7},{7,6},{8,9},{9,8},{10,11... | collective-permute-start | bytes 5898248 | tf_op jit(solution)/shard_map/ppermute | solution.py:24
  175.7 1.7 shard_map.92
  177.3 17.2 %all_to_all.31.parts_ref = f32[8,8,128]{2,1,0:T(8,128)} all-to-all(f32[8,8,128]{2,1,0:T(8,128)} %shard_map.92), channel_id=1, replica_groups=mesh['z'=8,'y'=8,'x'=4,'c'=2] {'z'}, dimensions={0} | all-to-all | bytes 65536 | tf_op jit(solution)/shard_map/all_to_all | solution.py:469
  194.5 1.4 shard_map.93
  195.9 3.9 %all-to-all-start.5 = ((f32[32,8,128]{2,1,0:T(8,128)}), f32[32,8,128]{2,1,0:T(8,128)S(1)}, u32[]{:S(2)}, u32[]{:S(2)}) async-start(f32[32,8,128]{2,1,0:T(8,128)} %shard_map.93), calls=%async_computation.5 | async-start | bytes 262144 | tf_op jit(solution)/shard_map/all_to_all | solution.py:392
  199.9 2.7 %add_convert_fusion = bf16[128,3840]{1,0:T(8,128)(2,1)} fusion(f32[128,3840]{1,0:T(8,128)} %get-tuple-element.52, f32[128,3840]{1,0:T(8,128)S(1)} %collective-permute-done.14), kind=kLoop, calls=%fused_computation | loop fusion | flops 983040 | bytes 4915200 | tf_op jit(solution)/shard_map/convert_element_type | solution.py:471
  202.6 6.6 %all-to-all-done.5.tiles_ref = f32[32,8,128]{2,1,0:T(8,128)S(1)} async-done(((f32[32,8,128]{2,1,0:T(8,128)}), f32[32,8,128]{2,1,0:T(8,128)S(1)}, u32[]{:S(2)}, u32[]{:S(2)}) %all-to-all-start.5) | async-done | bytes 131104 | tf_op jit(solution)/shard_map/all_to_all | solution.py:392
  209.2 0.7 copy-done.2
  209.9 2.0 shard_map.95
  211.8 4.8 %collective-permute-start.15 = (bf16[224,640]{1,0:T(8,128)(2,1)}, bf16[224,640]{1,0:T(8,128)(2,1)S(1)}, u32[]{:S(2)}, u32[]{:S(2)}) collective-permute-start(bf16[224,640]{1,0:T(8,128)(2,1)} %shard_map.95), channel_id=1, source_target_pairs={{0,1},{1,0},{2,3},{3,2},{4,5},{5,4},{6,7},{7,6},{8,9},{9,8},{10,11... | collective-permute-start | bytes 860168 | tf_op jit(solution)/shard_map/ppermute | solution.py:24
  216.7 1.4 collective-permute-done.15.other_ref
  218.1 0.9 copy-done.3
  219.0 2.6 %shard_map.96 = (bf16[128,1280]{1,0:T(8,128)(2,1)}, f32[27,1280]{1,0:T(8,128)}) custom-call(s32[2]{0:T(128)S(1)} %copy-done.7, s32[1,640]{1,0:T(1,128)S(1)} %get-tuple-element.64.own_ref.own_ch, s32[1,640]{1,0:T(1,128)S(1)} %get-tuple-element.63.other_ref.other_ch, bf16[256,896]{1,0:T(8,128)(2,1)S(1)} %bitcast.17, f32[32,8,128]{2,1,0:T(8,128)S(1)} %copy-done.3, ...), custom_call_target="tpu_custom_call" | custom-call | tf_op jit(solution)/shard_map/pallas_call | solution.py:214
  (57 shorter events, 0.6 us)
Async XLA Ops:
  0.6 29.7 %copy-start.18 = (bf16[1,128,1280]{2,1,0:T(8,128)(2,1)S(1)}, bf16[1,128,1280]{2,1,0:T(8,128)(2,1)}, u32[]{:S(2)}) copy-start(bf16[1,128,1280]{2,1,0:T(8,128)(2,1)} %param.6) | copy-start | bytes 983044
  0.6 24.1 %collective-permute-start = (bf16[128,3840]{1,0:T(8,128)(2,1)}, bf16[128,3840]{1,0:T(8,128)(2,1)S(1)}, u32[]{:S(2)}, u32[]{:S(2)}) collective-permute-start(bf16[128,3840]{1,0:T(8,128)(2,1)} %bitcast.21), channel_id=1, source_target_pairs={{0,1},{1,0},{2,3},{3,2},{4,5},{5,4},{6,7},{7,6},{8,9},{9,8},{10,11... | collective-permute-start | bytes 2949128 | tf_op jit(solution)/shard_map/ppermute | solution.py:24
  24.8 26.4 %copy-start.5 = (f32[27,1280]{1,0:T(8,128)S(1)}, f32[27,1280]{1,0:T(8,128)}, u32[]{:S(2)}) copy-start(f32[27,1280]{1,0:T(8,128)} %kernel_ref.1) | copy-start | bytes 414724
  24.8 26.4 %copy-start.8 = (s32[1,128]{1,0:T(1,128)S(1)}, s32[1,128]{1,0:T(1,128)}, u32[]{:S(2)}) copy-start(s32[1,128]{1,0:T(1,128)} %place_ref.1) | copy-start | bytes 1540
  24.8 44.1 %copy-start.13 = (bf16[128,3840]{1,0:T(8,128)(2,1)}, bf16[128,3840]{1,0:T(8,128)(2,1)S(1)}, u32[]{:S(2)}) copy-start(bf16[128,3840]{1,0:T(8,128)(2,1)S(1)} %collective-permute-done.other_ref) | copy-start | bytes 2949124
  24.9 59.9 %copy-start.10 = (bf16[80,3840]{1,0:T(8,128)(2,1)}, bf16[80,3840]{1,0:T(8,128)(2,1)S(1)}, u32[]{:S(2)}) copy-start(bf16[80,3840]{1,0:T(8,128)(2,1)S(1)} %reshape.103.refs_0_) | copy-start | bytes 1843204
  24.9 19.3 %collective-permute-start.2 = (bf16[80,3840]{1,0:T(8,128)(2,1)S(1)}, bf16[80,3840]{1,0:T(8,128)(2,1)S(1)}, u32[]{:S(2)}, u32[]{:S(2)}) collective-permute-start(bf16[80,3840]{1,0:T(8,128)(2,1)S(1)} %reshape.103.refs_0_), channel_id=1, source_target_pairs={{0,56},{8,0},{16,8},{24,16},{32,24},{40,32},{48,40},{56,48},{1,57}... | collective-permute-start | bytes 1843208 | tf_op jit(solution)/shard_map/ppermute | solution.py:34
  27.0 19.1 %collective-permute-start.1 = (bf16[80,3840]{1,0:T(8,128)(2,1)S(1)}, bf16[80,3840]{1,0:T(8,128)(2,1)}, u32[]{:S(2)}, u32[]{:S(2)}) collective-permute-start(bf16[80,3840]{1,0:T(8,128)(2,1)S(1)} %reshape.103.refs_0_), channel_id=1, source_target_pairs={{0,8},{8,16},{16,24},{24,32},{32,40},{40,48},{48,56},{56,0},{1,9},... | collective-permute-start | bytes 1843208 | tf_op jit(solution)/shard_map/ppermute | solution.py:34
  31.2 19.9 %all-to-all-start.1 = ((bf16[32,4,1280]{2,1,0:T(4,128)(2,1)}), bf16[32,4,1280]{2,1,0:T(4,128)(2,1)S(1)}, u32[]{:S(2)}, u32[]{:S(2)}) async-start(bf16[32,4,1280]{2,1,0:T(4,128)(2,1)} %reshape.104), calls=%async_computation.1 | async-start | bytes 655360 | tf_op jit(solution)/shard_map/all_to_all | solution.py:398
  44.2 49.4 %copy-start.14 = (bf16[80,3840]{1,0:T(8,128)(2,1)}, bf16[80,3840]{1,0:T(8,128)(2,1)S(1)}, u32[]{:S(2)}) copy-start(bf16[80,3840]{1,0:T(8,128)(2,1)S(1)} %collective-permute-done.2.refs_2_) | copy-start | bytes 1843204
  44.2 17.0 %collective-permute-start.5 = (bf16[80,3840]{1,0:T(8,128)(2,1)S(1)}, bf16[80,3840]{1,0:T(8,128)(2,1)}, u32[]{:S(2)}, u32[]{:S(2)}) collective-permute-start(bf16[80,3840]{1,0:T(8,128)(2,1)S(1)} %collective-permute-done.2.refs_2_), channel_id=1, source_target_pairs={{0,56},{8,0},{16,8},{24,16},{32,24},{40,32},{48,40},{56,48},{1,57}... | collective-permute-start | bytes 1843208 | tf_op jit(solution)/shard_map/ppermute | solution.py:34
  46.1 15.1 %collective-permute-start.4 = (bf16[80,3840]{1,0:T(8,128)(2,1)}, bf16[80,3840]{1,0:T(8,128)(2,1)}, u32[]{:S(2)}, u32[]{:S(2)}) collective-permute-start(bf16[80,3840]{1,0:T(8,128)(2,1)} %collective-permute-done.1.refs_1_), channel_id=1, source_target_pairs={{0,8},{8,16},{16,24},{24,32},{32,40},{40,48},{48,56},{56,0},{1,9},... | collective-permute-start | bytes 1843208 | tf_op jit(solution)/shard_map/ppermute | solution.py:34
  53.9 0.6 copy-start.4
  54.5 0.7 copy-start.6
  55.2 12.5 %collective-permute-start.3 = (bf16[144,640]{1,0:T(8,128)(2,1)S(1)}, bf16[144,640]{1,0:T(8,128)(2,1)S(1)}, u32[]{:S(2)}, u32[]{:S(2)}) collective-permute-start(bf16[144,640]{1,0:T(8,128)(2,1)S(1)} %get-tuple-element.34), channel_id=1, source_target_pairs={{0,1},{1,0},{2,3},{3,2},{4,5},{5,4},{6,7},{7,6},{8,9},{9,8},{10,11... | collective-permute-start | bytes 552968 | tf_op jit(solution)/shard_map/ppermute | solution.py:24
  61.2 18.7 %collective-permute-start.6 = (bf16[80,3840]{1,0:T(8,128)(2,1)}, bf16[80,3840]{1,0:T(8,128)(2,1)S(1)}, u32[]{:S(2)}, u32[]{:S(2)}) collective-permute-start(bf16[80,3840]{1,0:T(8,128)(2,1)} %collective-permute-done.4.refs_3_), channel_id=1, source_target_pairs={{0,8},{8,16},{16,24},{24,32},{32,40},{40,48},{48,56},{56,0},{1,9},... | collective-permute-start | bytes 1843208 | tf_op jit(solution)/shard_map/ppermute | solution.py:34
  64.6 15.4 %collective-permute-start.7 = (bf16[80,3840]{1,0:T(8,128)(2,1)}, bf16[80,3840]{1,0:T(8,128)(2,1)S(1)}, u32[]{:S(2)}, u32[]{:S(2)}) collective-permute-start(bf16[80,3840]{1,0:T(8,128)(2,1)} %collective-permute-done.5.refs_4_), channel_id=1, source_target_pairs={{0,56},{8,0},{16,8},{24,16},{32,24},{40,32},{48,40},{56,48},{1,57}... | collective-permute-start | bytes 1843208 | tf_op jit(solution)/shard_map/ppermute | solution.py:34
  67.8 0.7 copy-start.19
  71.9 4.1 %collective-permute-start.8 = (bf16[64,640]{1,0:T(8,128)(2,1)}, bf16[64,640]{1,0:T(8,128)(2,1)S(1)}, u32[]{:S(2)}, u32[]{:S(2)}) collective-permute-start(bf16[64,640]{1,0:T(8,128)(2,1)} %get-tuple-element.39), channel_id=1, source_target_pairs={{0,2},{2,4},{4,6},{6,8},{8,10},{10,12},{12,14},{14,16},{16,18},{18... | collective-permute-start | bytes 245768 | tf_op jit(solution)/shard_map/ppermute | solution.py:404
  74.3 5.7 %collective-permute-start.9 = (bf16[64,640]{1,0:T(8,128)(2,1)}, bf16[64,640]{1,0:T(8,128)(2,1)S(1)}, u32[]{:S(2)}, u32[]{:S(2)}) collective-permute-start(bf16[64,640]{1,0:T(8,128)(2,1)} %get-tuple-element.40), channel_id=1, source_target_pairs={{2,0},{4,2},{6,4},{8,6},{10,8},{12,10},{14,12},{16,14},{18,16},{20... | collective-permute-start | bytes 245768 | tf_op jit(solution)/shard_map/ppermute | solution.py:404
  76.0 12.7 %copy-start.16 = (bf16[64,640]{1,0:T(8,128)(2,1)}, bf16[64,640]{1,0:T(8,128)(2,1)S(1)}, u32[]{:S(2)}) copy-start(bf16[64,640]{1,0:T(8,128)(2,1)S(1)} %collective-permute-done.8.before_ref) | copy-start | bytes 245764
  79.9 8.8 %copy-start.17 = (bf16[64,640]{1,0:T(8,128)(2,1)}, bf16[64,640]{1,0:T(8,128)(2,1)S(1)}, u32[]{:S(2)}) copy-start(bf16[64,640]{1,0:T(8,128)(2,1)S(1)} %collective-permute-done.9.after_ref) | copy-start | bytes 245764
  79.9 13.7 %copy-start.11 = (bf16[80,3840]{1,0:T(8,128)(2,1)}, bf16[80,3840]{1,0:T(8,128)(2,1)S(1)}, u32[]{:S(2)}) copy-start(bf16[80,3840]{1,0:T(8,128)(2,1)S(1)} %collective-permute-done.6.refs_5_) | copy-start | bytes 1843204
  80.0 13.7 %copy-start.12 = (bf16[80,3840]{1,0:T(8,128)(2,1)}, bf16[80,3840]{1,0:T(8,128)(2,1)S(1)}, u32[]{:S(2)}) copy-start(bf16[80,3840]{1,0:T(8,128)(2,1)S(1)} %collective-permute-done.7.refs_6_) | copy-start | bytes 1843204
  80.0 13.6 %collective-permute-start.10 = (bf16[48,3840]{1,0:T(8,128)(2,1)S(1)}, bf16[48,3840]{1,0:T(8,128)(2,1)S(1)}, u32[]{:S(2)}, u32[]{:S(2)}) collective-permute-start(bf16[48,3840]{1,0:T(8,128)(2,1)S(1)} %slice.10), channel_id=1, source_target_pairs={{0,8},{8,16},{16,24},{24,32},{32,40},{40,48},{48,56},{56,0},{1,9},... | collective-permute-start | bytes 1105928 | tf_op jit(solution)/shard_map/ppermute | solution.py:34
  84.9 8.8 %collective-permute-start.11 = (bf16[32,3840]{1,0:T(8,128)(2,1)}, bf16[32,3840]{1,0:T(8,128)(2,1)}, u32[]{:S(2)}, u32[]{:S(2)}) collective-permute-start(bf16[32,3840]{1,0:T(8,128)(2,1)} %slice.11), channel_id=1, source_target_pairs={{0,56},{8,0},{16,8},{24,16},{32,24},{40,32},{48,40},{56,48},{1,57}... | collective-permute-start | bytes 737288 | tf_op jit(solution)/shard_map/ppermute | solution.py:34
  93.7 0.8 copy-start.15
  102.5 22.4 %all-to-all-start.2 = ((bf16[32,8,1280]{2,1,0:T(8,128)(2,1)}), bf16[32,8,1280]{2,1,0:T(8,128)(2,1)S(1)}, u32[]{:S(2)}, u32[]{:S(2)}) async-start(bf16[32,8,1280]{2,1,0:T(8,128)(2,1)} %bitcast.24), calls=%async_computation.2 | async-start | bytes 1310720 | tf_op jit(solution)/shard_map/all_to_all | solution.py:398
  124.8 0.8 copy-start.9
  127.8 8.8 %collective-permute-start.12 = (bf16[64,640]{1,0:T(8,128)(2,1)}, bf16[64,640]{1,0:T(8,128)(2,1)S(1)}, u32[]{:S(2)}, u32[]{:S(2)}) collective-permute-start(bf16[64,640]{1,0:T(8,128)(2,1)} %get-tuple-element.47), channel_id=1, source_target_pairs={{0,2},{2,4},{4,6},{6,8},{8,10},{10,12},{12,14},{14,16},{16,18},{18... | collective-permute-start | bytes 245768 | tf_op jit(solution)/shard_map/ppermute | solution.py:404
  130.3 6.2 %collective-permute-start.13 = (bf16[64,640]{1,0:T(8,128)(2,1)}, bf16[64,640]{1,0:T(8,128)(2,1)S(1)}, u32[]{:S(2)}, u32[]{:S(2)}) collective-permute-start(bf16[64,640]{1,0:T(8,128)(2,1)} %get-tuple-element.49), channel_id=1, source_target_pairs={{2,0},{4,2},{6,4},{8,6},{10,8},{12,10},{14,12},{16,14},{18,16},{20... | collective-permute-start | bytes 245768 | tf_op jit(solution)/shard_map/ppermute | solution.py:404
  136.5 0.6 copy-start.20
  137.2 0.6 copy-start.21
  143.3 20.5 %all-to-all-start.3 = ((bf16[32,8,896]{2,1,0:T(8,128)(2,1)}), bf16[32,8,896]{2,1,0:T(8,128)(2,1)S(1)}, u32[]{:S(2)}, u32[]{:S(2)}) async-start(bf16[32,8,896]{2,1,0:T(8,128)(2,1)} %bitcast.20), calls=%async_computation.3 | async-start | bytes 917504 | tf_op jit(solution)/shard_map/all_to_all | solution.py:398
  163.9 11.8 %copy-start = (bf16[32,8,896]{2,1,0:T(8,128)(2,1)}, bf16[32,8,896]{2,1,0:T(8,128)(2,1)S(1)}, u32[]{:S(2)}) copy-start(bf16[32,8,896]{2,1,0:T(8,128)(2,1)S(1)} %all-to-all-done.3) | copy-start | bytes 1376260
  163.9 36.0 %collective-permute-start.14 = (f32[128,3840]{1,0:T(8,128)}, f32[128,3840]{1,0:T(8,128)S(1)}, u32[]{:S(2)}, u32[]{:S(2)}) collective-permute-start(f32[128,3840]{1,0:T(8,128)} %get-tuple-element.54), channel_id=1, source_target_pairs={{0,1},{1,0},{2,3},{3,2},{4,5},{5,4},{6,7},{7,6},{8,9},{9,8},{10,11... | collective-permute-start | bytes 5898248 | tf_op jit(solution)/shard_map/ppermute | solution.py:24
  195.9 13.3 %all-to-all-start.5 = ((f32[32,8,128]{2,1,0:T(8,128)}), f32[32,8,128]{2,1,0:T(8,128)S(1)}, u32[]{:S(2)}, u32[]{:S(2)}) async-start(f32[32,8,128]{2,1,0:T(8,128)} %shard_map.93), calls=%async_computation.5 | async-start | bytes 262144 | tf_op jit(solution)/shard_map/all_to_all | solution.py:392
  199.9 18.2 %copy-start.1 = (bf16[32,8,896]{2,1,0:T(8,128)(2,1)S(1)}, bf16[32,8,896]{2,1,0:T(8,128)(2,1)}, u32[]{:S(2)}) copy-start(bf16[32,8,896]{2,1,0:T(8,128)(2,1)} %copy-done) | copy-start | bytes 1376260
  199.9 18.2 %copy-start.7 = (s32[2]{0:T(128)S(1)}, s32[2]{0:T(128)}, u32[]{:S(2)}) copy-start(s32[2]{0:T(128)} %pad_add_fusion.where_ref) | copy-start | bytes 28
  209.2 0.7 copy-start.2
  211.8 6.2 %collective-permute-start.15 = (bf16[224,640]{1,0:T(8,128)(2,1)}, bf16[224,640]{1,0:T(8,128)(2,1)S(1)}, u32[]{:S(2)}, u32[]{:S(2)}) collective-permute-start(bf16[224,640]{1,0:T(8,128)(2,1)} %shard_map.95), channel_id=1, source_target_pairs={{0,1},{1,0},{2,3},{3,2},{4,5},{5,4},{6,7},{7,6},{8,9},{9,8},{10,11... | collective-permute-start | bytes 860168 | tf_op jit(solution)/shard_map/ppermute | solution.py:24
  218.1 0.9 copy-start.3

commit v4 on v3

--- a/solution.py
+++ b/solution.py
@@ -221,18 +221,23 @@
 
 
 def fill(before_ref, cells_ref, after_ref, field):
-    parts = (before_ref[...], cells_ref[...], after_ref[...])
     lanes = cells_ref.shape[1]
-    wide = jnp.concatenate([p.astype(F32) for p in parts], axis=0)
-    wide = wide.reshape(6 * 8, 8, lanes)
-    column = lax.broadcasted_iota(jnp.int32, wide.shape, 1)
-    lower = jnp.where(column == 0, 0.0, jnp.roll(wide, 1, axis=1))
-    upper = jnp.where(column == 7, 0.0, jnp.roll(wide, -1, axis=1))
     zero = jnp.zeros((6, 1, 8, lanes), F32)
-    for s, value in enumerate((lower, wide, upper)):
-        field[s, :, 0:1] = zero
-        field[s, :, 9:10] = zero
-        field[s, :, 1:9] = value.reshape(6, 8, 8, lanes)
+    field[:, 0:1] = zero
+    field[:, 9:10] = zero
+    field[0:1, 1:9] = before_ref[...].astype(F32).reshape(1, 8, 8, lanes)
+    field[1:5, 1:9] = cells_ref[...].astype(F32).reshape(4, 8, 8, lanes)
+    field[5:6, 1:9] = after_ref[...].astype(F32).reshape(1, 8, 8, lanes)
+
+
+def from_lower(value):
+    column = lax.broadcasted_iota(jnp.int32, value.shape, value.ndim - 2)
+    return jnp.where(column == 0, 0.0, jnp.roll(value, 1, axis=value.ndim - 2))
+
+
+def from_upper(value):
+    column = lax.broadcasted_iota(jnp.int32, value.shape, value.ndim - 2)
+    return jnp.where(column == 7, 0.0, jnp.roll(value, -1, axis=value.ndim - 2))
 
 
 def conv_body(flip, index_ref, kernel_ref, before_ref, cells_ref, after_ref, out_ref, field):
@@ -240,12 +245,16 @@
     count, lanes = cells_ref.shape
     layers = []
     for z in range(4):
-        total = jnp.zeros((8, 8, lanes), F32)
-        for o in range(27):
-            dz, di, dc = o // 9, o // 3 % 3, o % 3
-            row = 26 - o if flip else o
-            total = total + kernel_ref[row : row + 1, :][None] * field[dc, z + dz, di : di + 8]
-        layers.append(total)
+        sums = []
+        for dc in range(3):
+            total = None
+            for o in range(dc, 27, 3):
+                dz, di = o // 9, o // 3 % 3
+                row = 26 - o if flip else o
+                term = kernel_ref[row : row + 1, :][None] * field[z + dz, di : di + 8]
+                total = term if total is None else total + term
+            sums.append(total)
+        layers.append(sums[1] + from_lower(sums[0]) + from_upper(sums[2]))
     conv = jnp.stack(layers).reshape(count, lanes)
     result = (cells_ref[...].astype(F32) + conv).astype(BF16)
     hit = lax.broadcasted_iota(jnp.int32, (count, count), 1) == index_ref[...]
@@ -302,7 +311,7 @@
         grid=(wide,),
         in_specs=specs,
         out_specs=pl.BlockSpec((count, 128), lambda t: (0, t)),
-        scratch_shapes=[pltpu.VMEM((3, 6, 10, 8, 128), F32)],
+        scratch_shapes=[pltpu.VMEM((6, 10, 8, 128), F32)],
     )(*operands)
 
 
@@ -316,10 +325,11 @@
         fill(before_ref, cells_ref, after_ref, field)
         lanes = cells_ref.shape[1]
         grad = grad_ref[...].astype(F32).reshape(4, 8, 8, lanes)
+        shifted = (from_upper(grad), grad, from_lower(grad))
         sums = []
         for o in range(27):
             dz, di, dc = o // 9, o // 3 % 3, o % 3
-            part = grad * field[dc, dz : dz + 4, di : di + 8]
+            part = shifted[dc] * field[dz : dz + 4, di : di + 8]
             sums.append(jnp.sum(part.reshape(32, 8, lanes), axis=0))
         sums += [jnp.zeros((8, lanes), F32)] * 5
         out_ref[...] = jnp.sum(jnp.stack(sums), axis=1)
@@ -334,7 +344,7 @@
         grid=(count // 32,),
         in_specs=[tall(count, steps), tall(LAYER, steps), tall(count, steps), tall(LAYER, steps)],
         out_specs=pl.BlockSpec((32, 128), lambda t: (t, 0)),
-        scratch_shapes=[pltpu.VMEM((3, 6, 10, 8, 128), F32)],
+        scratch_shapes=[pltpu.VMEM((6, 10, 8, 128), F32)],
     )(grad, before, cells, after)
 
 
@@ -346,24 +356,27 @@
     return jnp.concatenate([high, middle, low], axis=0)
 
 
-def pack_rows(block, landed_ref, tiles_ref):
+def stack_parts(rows, tiles_ref):
     steps = NY * ROWS // 128
-    rows = pick_rows(landed_row(block), TOK, landed_ref[:, 0 : NY * ROWS])
     tiles = [tiles_ref[4 * t : 4 * t + 4].reshape(32, 128) for t in range(steps)]
     return jnp.concatenate([rows, in_three(jnp.concatenate(tiles, axis=1))], axis=0)
 
 
-def pack_kernel(where_ref, landed_ref, tiles_ref, out_ref):
-    out_ref[...] = pack_rows(1 - where_ref[1], landed_ref, tiles_ref)
-
-
-def last_kernel(where_ref, own_ch, other_ch, landed_ref, tiles_ref, other_ref, out_ref, grad_ref):
+def other_kernel(where_ref, landed_ref, out_ref):
+    out_ref[...] = pick_rows(
+        landed_row(1 - where_ref[1]), TOK, landed_ref[:, 0 : NY * ROWS]
+    )
+
+
+def last_kernel(where_ref, own_ch, other_ch, landed_ref, tiles_ref, rows_ref, other_ref, out_ref, grad_ref):
     width = out_ref.shape[1]
     contract = (((1,), (1,)), ((), ()))
-    own = pack_rows(where_ref[1], landed_ref, tiles_ref)
+    rows = pick_rows(landed_row(where_ref[1]), TOK, landed_ref[:, 0 : NY * ROWS])
+    own = stack_parts(rows, tiles_ref)
+    other = stack_parts(rows_ref[...], other_ref)
     total = lax.dot_general(own, chosen(own_ch, width), contract, preferred_element_type=F32)
     total = total + lax.dot_general(
-        other_ref[...], chosen(other_ch, width), contract, preferred_element_type=F32
+        other, chosen(other_ch, width), contract, preferred_element_type=F32
     )
     out_ref[...] = total[0:TOK].astype(BF16)
     grad = total[TOK : TOK + 32] + total[TOK + 32 : TOK + 64] + total[TOK + 64 : TOK + 96]
@@ -467,11 +480,11 @@
     landed_d = exchange(back)
     tile = jax.ShapeDtypeStruct((planes, 8, 128), F32)
     tiles = lax.all_to_all(in_vmem(landed_sum_kernel, tile, landed_d), "z", 0, 0, tiled=True)
-    tiles = sum_spread(tiles, ("y", "x"), CHIPS)
+    other_rows = jax.ShapeDtypeStruct((TOK, local), BF16)
+    d_other = swap(in_vmem(other_kernel, other_rows, where, landed_d, scalars=1))
+    tiles = sum_spread(after(tiles, d_other), ("y", "x"), CHIPS)
     projected = (keep + swap(after(send, landed_d))).astype(BF16)
     tiles, projected = lax.optimization_barrier((tiles, projected))
-    packed = jax.ShapeDtypeStruct((TOK + 96, local), BF16)
-    d_other = swap(in_vmem(pack_kernel, packed, where, landed_d, tiles, scalars=1))
 
     d_tokens, d_kernel = in_vmem(
         last_kernel,
@@ -485,6 +498,7 @@
         landed_d,
         tiles,
         d_other,
+        swap(tiles),
         vmem=16 << 20,
         scalars=1,
     )

time: 223 us -> 224 us (level)
  starting transfers between devices: 87.4 us -> 89.9 us
    ppermute x4 -> x5, starting transfers between devices: 31.5 us -> 34.1 us  [swap(): return lax.ppermute(value, 'c', [(0, 1), (1, 0)])]
    unnamed x44 -> x40, local copies, waits for them, and re-layouts: 6.38 us -> 4.81 us
  transfers between devices with their start and end apart: 20 -> 21, of which waited for: 8 -> 8; matrix products, arithmetic and copies ran while one was open for 4% -> 4% of each run, Pallas kernels for 11% -> 12%
where the time goes in v4:
time: 224 us; the launch traced here: 222 us
  starting transfers between devices  89.9 us (40%)
  Pallas kernels  44.9 us (20%)
  waiting for transfers between devices  40.7 us (18%)
  blocking collectives  31.4 us (14%)
  local copies, waits for them, and re-layouts  10 us (4%)
  other arithmetic  4.07 us (2%)
    ppermute x5, starting transfers between devices, swap(): return lax.ppermute(value, 'c', [(0, 1), (1, 0)])  34.1 us
    ppermute x8, starting transfers between devices, shift(): lax.ppermute(value, axis, [(i, (i + step) % size) for i in range(size)])  23.7 us
    all_to_all x3, starting transfers between devices, exchange(): lax.all_to_all(sent, ('y', 'x'), 0, 0, tiled=True).reshape(count, width)  20.8 us
    all_to_all x3, waiting for transfers between devices, exchange(): lax.all_to_all(sent, ('y', 'x'), 0, 0, tiled=True).reshape(count, width)  19.5 us
    all_to_all x1, blocking collectives, shards(): lax.all_to_all(in_vmem(landed_sum_kernel, tile, landed_d), 'z', 0, 0, til...  17.2 us
    pallas_call x7, Pallas kernels, in_vmem(): pl.pallas_call(body, out_shape=out_shape, in_specs=[SMEM] * scalars + [VM...  14.4 us
    all_to_all x1, blocking collectives, spread(): lax.all_to_all(jnp.broadcast_to(value[None], (size, *value.shape)), axis,...  14.2 us
    pallas_call x2, Pallas kernels, conv_rows(): pl.pallas_call(functools.partial(conv_body, False) if sums is None else b...  10.3 us
  transfers between devices with their start and end apart: 21, of which 8 were waited for; matrix products, arithmetic and copies ran while one was open for 4% of the time, Pallas kernels for 12%

profile of v4, /device:TPU:1, one launch (start us, length us, event | category | flops | bytes accessed | tf_op | source)
XLA Modules:
  0.0 222.2 jit_solution(7765039887064049925)
XLA Ops:
  0.6 8.9 %collective-permute-start = (bf16[128,3840]{1,0:T(8,128)(2,1)}, bf16[128,3840]{1,0:T(8,128)(2,1)S(1)}, u32[]{:S(2)}, u32[]{:S(2)}) collective-permute-start(bf16[128,3840]{1,0:T(8,128)(2,1)} %bitcast.21), channel_id=1, source_target_pairs={{0,1},{1,0},{2,3},{3,2},{4,5},{5,4},{6,7},{7,6},{8,9},{9,8},{10,11... | collective-permute-start | bytes 2949128 | tf_op jit(solution)/shard_map/ppermute | solution.py:24
  9.6 1.0 broadcast_in_dim.6
  10.5 14.2 %all_to_all.30 = bf16[4,20,3840]{2,1,0:T(8,128)(2,1)S(1)} all-to-all(bf16[4,20,3840]{2,1,0:T(8,128)(2,1)S(1)} %broadcast_in_dim.6), channel_id=1, replica_groups=mesh['z'=8,'y'=8,'x'=4,'c'=2] {'x'}, dimensions={0} | all-to-all | bytes 1228800 | tf_op jit(solution)/shard_map/all_to_all | solution.py:28
  24.8 0.1 reshape.103.refs_0_
  24.9 2.1 collective-permute-start.2
  27.0 3.4 %collective-permute-start.1 = (bf16[80,3840]{1,0:T(8,128)(2,1)S(1)}, bf16[80,3840]{1,0:T(8,128)(2,1)}, u32[]{:S(2)}, u32[]{:S(2)}) collective-permute-start(bf16[80,3840]{1,0:T(8,128)(2,1)S(1)} %reshape.103.refs_0_), channel_id=1, source_target_pairs={{0,8},{8,16},{16,24},{24,32},{32,40},{40,48},{48,56},{56,0},{1,9},... | collective-permute-start | bytes 1843208 | tf_op jit(solution)/shard_map/ppermute | solution.py:34
  30.4 0.8 reshape.104
  31.2 3.9 %all-to-all-start.1 = ((bf16[32,4,1280]{2,1,0:T(4,128)(2,1)}), bf16[32,4,1280]{2,1,0:T(4,128)(2,1)S(1)}, u32[]{:S(2)}, u32[]{:S(2)}) async-start(bf16[32,4,1280]{2,1,0:T(4,128)(2,1)} %reshape.104), calls=%async_computation.1 | async-start | bytes 655360 | tf_op jit(solution)/shard_map/all_to_all | solution.py:411
  35.1 9.1 %collective-permute-done.2.refs_2_ = bf16[80,3840]{1,0:T(8,128)(2,1)S(1)} collective-permute-done((bf16[80,3840]{1,0:T(8,128)(2,1)S(1)}, bf16[80,3840]{1,0:T(8,128)(2,1)S(1)}, u32[]{:S(2)}, u32[]{:S(2)}) %collective-permute-start.2) | collective-permute-done | bytes 614432 | tf_op jit(solution)/shard_map/ppermute | solution.py:34
  44.2 1.9 collective-permute-start.5
  46.1 3.4 %collective-permute-start.4 = (bf16[80,3840]{1,0:T(8,128)(2,1)}, bf16[80,3840]{1,0:T(8,128)(2,1)}, u32[]{:S(2)}, u32[]{:S(2)}) collective-permute-start(bf16[80,3840]{1,0:T(8,128)(2,1)} %collective-permute-done.1.refs_1_), channel_id=1, source_target_pairs={{0,8},{8,16},{16,24},{24,32},{32,40},{40,48},{48,56},{56,0},{1,9},... | collective-permute-start | bytes 1843208 | tf_op jit(solution)/shard_map/ppermute | solution.py:34
  49.5 1.5 all-to-all-done.1
  51.2 2.7 %shard_map.85 = (bf16[128,640]{1,0:T(8,128)(2,1)S(1)}, bf16[144,640]{1,0:T(8,128)(2,1)S(1)}, f32[27,640]{1,0:T(8,128)S(1)}) custom-call(s32[1,640]{1,0:T(1,128)S(1)} %get-tuple-element.66.own_ref.own_ch, s32[1,640]{1,0:T(1,128)S(1)} %get-tuple-element.65.other_ref.other_ch, bf16[128,1280]{1,0:T(8,128)(2,1)S(1)} %reshape.105.rows_ref, ...), custom_call_target="tpu_custom_call" | custom-call | tf_op jit(solution)/shard_map/pallas_call | solution.py:214
  53.9 0.6 copy-done.2
  54.5 0.7 copy-done.4
  55.2 6.0 %collective-permute-start.3 = (bf16[144,640]{1,0:T(8,128)(2,1)S(1)}, bf16[144,640]{1,0:T(8,128)(2,1)S(1)}, u32[]{:S(2)}, u32[]{:S(2)}) collective-permute-start(bf16[144,640]{1,0:T(8,128)(2,1)S(1)} %get-tuple-element.35), channel_id=1, source_target_pairs={{0,1},{1,0},{2,3},{3,2},{4,5},{5,4},{6,7},{7,6},{8,9},{9,8},{10,11... | collective-permute-start | bytes 552968 | tf_op jit(solution)/shard_map/ppermute | solution.py:24
  61.2 3.3 %collective-permute-start.6 = (bf16[80,3840]{1,0:T(8,128)(2,1)}, bf16[80,3840]{1,0:T(8,128)(2,1)S(1)}, u32[]{:S(2)}, u32[]{:S(2)}) collective-permute-start(bf16[80,3840]{1,0:T(8,128)(2,1)} %collective-permute-done.4.refs_3_), channel_id=1, source_target_pairs={{0,8},{8,16},{16,24},{24,32},{32,40},{40,48},{48,56},{56,0},{1,9},... | collective-permute-start | bytes 1843208 | tf_op jit(solution)/shard_map/ppermute | solution.py:34
  64.6 3.2 %collective-permute-start.7 = (bf16[80,3840]{1,0:T(8,128)(2,1)}, bf16[80,3840]{1,0:T(8,128)(2,1)S(1)}, u32[]{:S(2)}, u32[]{:S(2)}) collective-permute-start(bf16[80,3840]{1,0:T(8,128)(2,1)} %collective-permute-done.5.refs_4_), channel_id=1, source_target_pairs={{0,56},{8,0},{16,8},{24,16},{32,24},{40,32},{48,40},{56,48},{1,57}... | collective-permute-start | bytes 1843208 | tf_op jit(solution)/shard_map/ppermute | solution.py:34
  67.8 0.6 copy-done.17
  68.4 0.2 stack.18
  68.7 0.2 stack.19
  69.0 0.1 copy.20
  69.2 0.2 reshape.106
  69.3 0.6 broadcast_select_fusion.2
  69.9 2.0 shard_map.86
  71.9 2.3 %collective-permute-start.8 = (bf16[64,640]{1,0:T(8,128)(2,1)}, bf16[64,640]{1,0:T(8,128)(2,1)S(1)}, u32[]{:S(2)}, u32[]{:S(2)}) collective-permute-start(bf16[64,640]{1,0:T(8,128)(2,1)} %get-tuple-element.40), channel_id=1, source_target_pairs={{0,2},{2,4},{4,6},{6,8},{8,10},{10,12},{12,14},{14,16},{16,18},{18... | collective-permute-start | bytes 245768 | tf_op jit(solution)/shard_map/ppermute | solution.py:417
  74.3 1.3 collective-permute-start.9
  75.6 0.5 collective-permute-done.8.before_ref
  76.1 3.9 %collective-permute-done.9.after_ref = bf16[64,640]{1,0:T(8,128)(2,1)S(1)} collective-permute-done((bf16[64,640]{1,0:T(8,128)(2,1)}, bf16[64,640]{1,0:T(8,128)(2,1)S(1)}, u32[]{:S(2)}, u32[]{:S(2)}) %collective-permute-start.9) | collective-permute-done | bytes 81952 | tf_op jit(solution)/shard_map/ppermute | solution.py:417
  80.0 4.1 %collective-permute-start.10 = (bf16[48,3840]{1,0:T(8,128)(2,1)S(1)}, bf16[48,3840]{1,0:T(8,128)(2,1)S(1)}, u32[]{:S(2)}, u32[]{:S(2)}) collective-permute-start(bf16[48,3840]{1,0:T(8,128)(2,1)S(1)} %slice.10), channel_id=1, source_target_pairs={{0,8},{8,16},{16,24},{24,32},{32,40},{40,48},{48,56},{56,0},{1,9},... | collective-permute-start | bytes 1105928 | tf_op jit(solution)/shard_map/ppermute | solution.py:34
  84.1 0.7 slice.11
  84.9 2.4 %collective-permute-start.11 = (bf16[32,3840]{1,0:T(8,128)(2,1)}, bf16[32,3840]{1,0:T(8,128)(2,1)}, u32[]{:S(2)}, u32[]{:S(2)}) collective-permute-start(bf16[32,3840]{1,0:T(8,128)(2,1)} %slice.11), channel_id=1, source_target_pairs={{0,56},{8,0},{16,8},{24,16},{32,24},{40,32},{48,40},{56,48},{1,57}... | collective-permute-start | bytes 737288 | tf_op jit(solution)/shard_map/ppermute | solution.py:34
  87.3 0.6 pad_add_fusion.where_ref
  87.9 0.1 copy.18
  88.0 0.8 broadcast_in_dim_reshape.8.index_ref
  88.8 4.8 %shard_map.87.y_ref = bf16[256,640]{1,0:T(8,128)(2,1)} custom-call(s32[256,1]{1,0:T(8,128)} %broadcast_in_dim_reshape.8.index_ref, f32[27,640]{1,0:T(8,128)} %copy-done.2, bf16[64,640]{1,0:T(8,128)(2,1)} %copy-done.14, bf16[256,640]{1,0:T(8,128)(2,1)} %get-tuple-element.43.cells_ref, bf16[64,640]{1,0:T(8,128)(2,1)} %copy-done.15), custom_call_target="tpu_custom_call" | custom-call | tf_op jit(solution)/shard_map/pallas_call | solution.py:308
  93.7 0.7 copy-done.13
  94.4 8.0 %shard_map.88 = (bf16[256,1280]{1,0:T(8,128)(2,1)}, bf16[640,3840]{1,0:T(8,128)(2,1)}) custom-call(s32[2]{0:T(128)} %pad_add_fusion.where_ref, bf16[256,640]{1,0:T(8,128)(2,1)} %shard_map.87.y_ref, bf16[128,3840]{1,0:T(8,128)(2,1)} %bitcast.22, bf16[128,3840]{1,0:T(8,128)(2,1)} %copy-done.11, bf16[80,3840]{1,0:T(8,128)(2,1)} %copy-done.8, ...), custom_call_target="tpu_custom_call" | custom-call | tf_op jit(solution)/shard_map/pallas_call | solution.py:129
  102.5 8.5 %all-to-all-start.2 = ((bf16[32,8,1280]{2,1,0:T(8,128)(2,1)}), bf16[32,8,1280]{2,1,0:T(8,128)(2,1)S(1)}, u32[]{:S(2)}, u32[]{:S(2)}) async-start(bf16[32,8,1280]{2,1,0:T(8,128)(2,1)} %bitcast.24), calls=%async_computation.2 | async-start | bytes 1310720 | tf_op jit(solution)/shard_map/all_to_all | solution.py:411
  111.0 0.7 broadcast_in_dim_reshape.7.cell_ref
  111.7 13.0 %all-to-all-done.2 = bf16[32,8,1280]{2,1,0:T(8,128)(2,1)S(1)} async-done(((bf16[32,8,1280]{2,1,0:T(8,128)(2,1)}), bf16[32,8,1280]{2,1,0:T(8,128)(2,1)S(1)}, u32[]{:S(2)}, u32[]{:S(2)}) %all-to-all-start.2) | async-done | bytes 655392 | tf_op jit(solution)/shard_map/all_to_all | solution.py:411
  124.8 0.8 copy-done.7
  125.6 2.1 shard_map.89
  127.7 2.5 %collective-permute-start.12 = (bf16[64,640]{1,0:T(8,128)(2,1)}, bf16[64,640]{1,0:T(8,128)(2,1)S(1)}, u32[]{:S(2)}, u32[]{:S(2)}) collective-permute-start(bf16[64,640]{1,0:T(8,128)(2,1)} %get-tuple-element.48), channel_id=1, source_target_pairs={{0,2},{2,4},{4,6},{6,8},{8,10},{10,12},{12,14},{14,16},{16,18},{18... | collective-permute-start | bytes 245768 | tf_op jit(solution)/shard_map/ppermute | solution.py:417
  130.3 1.3 collective-permute-start.13
  131.6 4.9 %shard_map.90.sums_ref = f32[256,128]{1,0:T(8,128)} custom-call(bf16[256,640]{1,0:T(8,128)(2,1)} %get-tuple-element.49.grad_ref.cells_ref, bf16[64,640]{1,0:T(8,128)(2,1)} %copy-done.14, bf16[256,640]{1,0:T(8,128)(2,1)} %get-tuple-element.43.cells_ref, bf16[64,640]{1,0:T(8,128)(2,1)} %copy-done.15), custom_call_target="tpu_custom_call" | custom-call | tf_op jit(solution)/shard_map/pallas_call | solution.py:341
  136.5 0.6 copy-done.18
  137.1 0.6 copy-done.19
  137.8 5.5 %shard_map.91 = bf16[256,896]{1,0:T(8,128)(2,1)} custom-call(s32[256,1]{1,0:T(8,128)} %broadcast_in_dim_reshape.8.index_ref, f32[27,640]{1,0:T(8,128)} %copy-done.2, bf16[64,640]{1,0:T(8,128)(2,1)} %copy-done.18, bf16[256,640]{1,0:T(8,128)(2,1)} %get-tuple-element.49.grad_ref.cells_ref, bf16[64,640]{1,0:T(8,128)(2,1)} %copy-done.19, ...), custom_call_target="tpu_custom_call" | custom-call | tf_op jit(solution)/shard_map/pallas_call | solution.py:308
  143.3 8.4 %all-to-all-start.3 = ((bf16[32,8,896]{2,1,0:T(8,128)(2,1)}), bf16[32,8,896]{2,1,0:T(8,128)(2,1)S(1)}, u32[]{:S(2)}, u32[]{:S(2)}) async-start(bf16[32,8,896]{2,1,0:T(8,128)(2,1)} %bitcast.20), calls=%async_computation.3 | async-start | bytes 917504 | tf_op jit(solution)/shard_map/all_to_all | solution.py:411
  151.7 7.2 %shard_map.95 = (f32[128,3840]{1,0:T(8,128)}, f32[128,3840]{1,0:T(8,128)}) custom-call(s32[2]{0:T(128)} %pad_add_fusion.where_ref, bf16[256,1280]{1,0:T(8,128)(2,1)} %bitcast.19, bf16[640,3840]{1,0:T(8,128)(2,1)} %get-tuple-element.53.whole_ref), custom_call_target="tpu_custom_call" | custom-call | flops 1258291200 | bytes 20000000 | tf_op jit(solution)/shard_map/pallas_call | solution.py:160
  158.9 4.9 %all-to-all-done.3 = bf16[32,8,896]{2,1,0:T(8,128)(2,1)S(1)} async-done(((bf16[32,8,896]{2,1,0:T(8,128)(2,1)}), bf16[32,8,896]{2,1,0:T(8,128)(2,1)S(1)}, u32[]{:S(2)}, u32[]{:S(2)}) %all-to-all-start.3) | async-done | bytes 458784 | tf_op jit(solution)/shard_map/all_to_all | solution.py:411
  163.8 12.0 %collective-permute-start.15 = (f32[128,3840]{1,0:T(8,128)}, f32[128,3840]{1,0:T(8,128)S(1)}, u32[]{:S(2)}, u32[]{:S(2)}) collective-permute-start(f32[128,3840]{1,0:T(8,128)} %get-tuple-element.56), channel_id=1, source_target_pairs={{0,1},{1,0},{2,3},{3,2},{4,5},{5,4},{6,7},{7,6},{8,9},{9,8},{10,11... | collective-permute-start | bytes 5898248 | tf_op jit(solution)/shard_map/ppermute | solution.py:24
  175.8 1.9 shard_map.93
  177.7 1.9 collective-permute-start.14
  179.6 1.7 shard_map.92
  181.3 17.2 %all_to_all.31.parts_ref = f32[8,8,128]{2,1,0:T(8,128)} all-to-all(f32[8,8,128]{2,1,0:T(8,128)} %shard_map.92), channel_id=1, replica_groups=mesh['z'=8,'y'=8,'x'=4,'c'=2] {'z'}, dimensions={0} | all-to-all | bytes 65536 | tf_op jit(solution)/shard_map/all_to_all | solution.py:482
  198.5 1.4 shard_map.94
  199.9 3.9 %all-to-all-start.5 = ((f32[32,8,128]{2,1,0:T(8,128)}), f32[32,8,128]{2,1,0:T(8,128)S(1)}, u32[]{:S(2)}, u32[]{:S(2)}) async-start(f32[32,8,128]{2,1,0:T(8,128)} %shard_map.94), calls=%async_computation.5 | async-start | bytes 262144 | tf_op jit(solution)/shard_map/all_to_all | solution.py:405
  203.9 2.7 %add_convert_fusion = bf16[128,3840]{1,0:T(8,128)(2,1)} fusion(f32[128,3840]{1,0:T(8,128)} %get-tuple-element.54, f32[128,3840]{1,0:T(8,128)S(1)} %collective-permute-done.15), kind=kLoop, calls=%fused_computation | loop fusion | flops 983040 | bytes 4915200 | tf_op jit(solution)/shard_map/convert_element_type | solution.py:486
  206.6 6.7 %all-to-all-done.5.tiles_ref = f32[32,8,128]{2,1,0:T(8,128)S(1)} async-done(((f32[32,8,128]{2,1,0:T(8,128)}), f32[32,8,128]{2,1,0:T(8,128)S(1)}, u32[]{:S(2)}, u32[]{:S(2)}) %all-to-all-start.5) | async-done | bytes 131104 | tf_op jit(solution)/shard_map/all_to_all | solution.py:405
  213.3 5.3 %collective-permute-start.16 = (f32[32,8,128]{2,1,0:T(8,128)S(1)}, f32[32,8,128]{2,1,0:T(8,128)S(1)}, u32[]{:S(2)}, u32[]{:S(2)}) collective-permute-start(f32[32,8,128]{2,1,0:T(8,128)S(1)} %all-to-all-done.5.tiles_ref), channel_id=1, source_target_pairs={{0,1},{1,0},{2,3},{3,2},{4,5},{5,4},{6,7},{7,6},{8,9},{9,8},{10,11... | collective-permute-start | bytes 393224 | tf_op jit(solution)/shard_map/ppermute | solution.py:24
  218.6 1.0 collective-permute-done.16.other_ref
  219.6 2.6 %shard_map.96 = (bf16[128,1280]{1,0:T(8,128)(2,1)}, f32[27,1280]{1,0:T(8,128)}) custom-call(s32[2]{0:T(128)S(1)} %copy-done.5, s32[1,640]{1,0:T(1,128)S(1)} %get-tuple-element.66.own_ref.own_ch, s32[1,640]{1,0:T(1,128)S(1)} %get-tuple-element.65.other_ref.other_ch, bf16[256,896]{1,0:T(8,128)(2,1)S(1)} %bitcast.17, ...), custom_call_target="tpu_custom_call" | custom-call | tf_op jit(solution)/shard_map/pallas_call | solution.py:214
  (55 shorter events, 0.5 us)
Async XLA Ops:
  0.6 29.7 %copy-start.16 = (bf16[1,128,1280]{2,1,0:T(8,128)(2,1)S(1)}, bf16[1,128,1280]{2,1,0:T(8,128)(2,1)}, u32[]{:S(2)}) copy-start(bf16[1,128,1280]{2,1,0:T(8,128)(2,1)} %param.6) | copy-start | bytes 983044
  0.6 24.1 %collective-permute-start = (bf16[128,3840]{1,0:T(8,128)(2,1)}, bf16[128,3840]{1,0:T(8,128)(2,1)S(1)}, u32[]{:S(2)}, u32[]{:S(2)}) collective-permute-start(bf16[128,3840]{1,0:T(8,128)(2,1)} %bitcast.21), channel_id=1, source_target_pairs={{0,1},{1,0},{2,3},{3,2},{4,5},{5,4},{6,7},{7,6},{8,9},{9,8},{10,11... | collective-permute-start | bytes 2949128 | tf_op jit(solution)/shard_map/ppermute | solution.py:24
  24.8 26.4 %copy-start.3 = (f32[27,1280]{1,0:T(8,128)S(1)}, f32[27,1280]{1,0:T(8,128)}, u32[]{:S(2)}) copy-start(f32[27,1280]{1,0:T(8,128)} %kernel_ref.1) | copy-start | bytes 414724
  24.8 26.4 %copy-start.6 = (s32[1,128]{1,0:T(1,128)S(1)}, s32[1,128]{1,0:T(1,128)}, u32[]{:S(2)}) copy-start(s32[1,128]{1,0:T(1,128)} %place_ref.1) | copy-start | bytes 1540
  24.8 44.1 %copy-start.11 = (bf16[128,3840]{1,0:T(8,128)(2,1)}, bf16[128,3840]{1,0:T(8,128)(2,1)S(1)}, u32[]{:S(2)}) copy-start(bf16[128,3840]{1,0:T(8,128)(2,1)S(1)} %collective-permute-done.other_ref) | copy-start | bytes 2949124
  24.9 59.9 %copy-start.8 = (bf16[80,3840]{1,0:T(8,128)(2,1)}, bf16[80,3840]{1,0:T(8,128)(2,1)S(1)}, u32[]{:S(2)}) copy-start(bf16[80,3840]{1,0:T(8,128)(2,1)S(1)} %reshape.103.refs_0_) | copy-start | bytes 1843204
  24.9 19.3 %collective-permute-start.2 = (bf16[80,3840]{1,0:T(8,128)(2,1)S(1)}, bf16[80,3840]{1,0:T(8,128)(2,1)S(1)}, u32[]{:S(2)}, u32[]{:S(2)}) collective-permute-start(bf16[80,3840]{1,0:T(8,128)(2,1)S(1)} %reshape.103.refs_0_), channel_id=1, source_target_pairs={{0,56},{8,0},{16,8},{24,16},{32,24},{40,32},{48,40},{56,48},{1,57}... | collective-permute-start | bytes 1843208 | tf_op jit(solution)/shard_map/ppermute | solution.py:34
  27.0 19.1 %collective-permute-start.1 = (bf16[80,3840]{1,0:T(8,128)(2,1)S(1)}, bf16[80,3840]{1,0:T(8,128)(2,1)}, u32[]{:S(2)}, u32[]{:S(2)}) collective-permute-start(bf16[80,3840]{1,0:T(8,128)(2,1)S(1)} %reshape.103.refs_0_), channel_id=1, source_target_pairs={{0,8},{8,16},{16,24},{24,32},{32,40},{40,48},{48,56},{56,0},{1,9},... | collective-permute-start | bytes 1843208 | tf_op jit(solution)/shard_map/ppermute | solution.py:34
  31.2 19.9 %all-to-all-start.1 = ((bf16[32,4,1280]{2,1,0:T(4,128)(2,1)}), bf16[32,4,1280]{2,1,0:T(4,128)(2,1)S(1)}, u32[]{:S(2)}, u32[]{:S(2)}) async-start(bf16[32,4,1280]{2,1,0:T(4,128)(2,1)} %reshape.104), calls=%async_computation.1 | async-start | bytes 655360 | tf_op jit(solution)/shard_map/all_to_all | solution.py:411
  44.2 49.4 %copy-start.12 = (bf16[80,3840]{1,0:T(8,128)(2,1)}, bf16[80,3840]{1,0:T(8,128)(2,1)S(1)}, u32[]{:S(2)}) copy-start(bf16[80,3840]{1,0:T(8,128)(2,1)S(1)} %collective-permute-done.2.refs_2_) | copy-start | bytes 1843204
  44.2 17.0 %collective-permute-start.5 = (bf16[80,3840]{1,0:T(8,128)(2,1)S(1)}, bf16[80,3840]{1,0:T(8,128)(2,1)}, u32[]{:S(2)}, u32[]{:S(2)}) collective-permute-start(bf16[80,3840]{1,0:T(8,128)(2,1)S(1)} %collective-permute-done.2.refs_2_), channel_id=1, source_target_pairs={{0,56},{8,0},{16,8},{24,16},{32,24},{40,32},{48,40},{56,48},{1,57}... | collective-permute-start | bytes 1843208 | tf_op jit(solution)/shard_map/ppermute | solution.py:34
  46.1 15.1 %collective-permute-start.4 = (bf16[80,3840]{1,0:T(8,128)(2,1)}, bf16[80,3840]{1,0:T(8,128)(2,1)}, u32[]{:S(2)}, u32[]{:S(2)}) collective-permute-start(bf16[80,3840]{1,0:T(8,128)(2,1)} %collective-permute-done.1.refs_1_), channel_id=1, source_target_pairs={{0,8},{8,16},{16,24},{24,32},{32,40},{40,48},{48,56},{56,0},{1,9},... | collective-permute-start | bytes 1843208 | tf_op jit(solution)/shard_map/ppermute | solution.py:34
  53.9 0.6 copy-start.2
  54.5 0.7 copy-start.4
  55.2 12.5 %collective-permute-start.3 = (bf16[144,640]{1,0:T(8,128)(2,1)S(1)}, bf16[144,640]{1,0:T(8,128)(2,1)S(1)}, u32[]{:S(2)}, u32[]{:S(2)}) collective-permute-start(bf16[144,640]{1,0:T(8,128)(2,1)S(1)} %get-tuple-element.35), channel_id=1, source_target_pairs={{0,1},{1,0},{2,3},{3,2},{4,5},{5,4},{6,7},{7,6},{8,9},{9,8},{10,11... | collective-permute-start | bytes 552968 | tf_op jit(solution)/shard_map/ppermute | solution.py:24
  61.2 18.7 %collective-permute-start.6 = (bf16[80,3840]{1,0:T(8,128)(2,1)}, bf16[80,3840]{1,0:T(8,128)(2,1)S(1)}, u32[]{:S(2)}, u32[]{:S(2)}) collective-permute-start(bf16[80,3840]{1,0:T(8,128)(2,1)} %collective-permute-done.4.refs_3_), channel_id=1, source_target_pairs={{0,8},{8,16},{16,24},{24,32},{32,40},{40,48},{48,56},{56,0},{1,9},... | collective-permute-start | bytes 1843208 | tf_op jit(solution)/shard_map/ppermute | solution.py:34
  64.6 15.4 %collective-permute-start.7 = (bf16[80,3840]{1,0:T(8,128)(2,1)}, bf16[80,3840]{1,0:T(8,128)(2,1)S(1)}, u32[]{:S(2)}, u32[]{:S(2)}) collective-permute-start(bf16[80,3840]{1,0:T(8,128)(2,1)} %collective-permute-done.5.refs_4_), channel_id=1, source_target_pairs={{0,56},{8,0},{16,8},{24,16},{32,24},{40,32},{48,40},{56,48},{1,57}... | collective-permute-start | bytes 1843208 | tf_op jit(solution)/shard_map/ppermute | solution.py:34
  67.8 0.7 copy-start.17
  71.9 4.1 %collective-permute-start.8 = (bf16[64,640]{1,0:T(8,128)(2,1)}, bf16[64,640]{1,0:T(8,128)(2,1)S(1)}, u32[]{:S(2)}, u32[]{:S(2)}) collective-permute-start(bf16[64,640]{1,0:T(8,128)(2,1)} %get-tuple-element.40), channel_id=1, source_target_pairs={{0,2},{2,4},{4,6},{6,8},{8,10},{10,12},{12,14},{14,16},{16,18},{18... | collective-permute-start | bytes 245768 | tf_op jit(solution)/shard_map/ppermute | solution.py:417
  74.3 5.7 %collective-permute-start.9 = (bf16[64,640]{1,0:T(8,128)(2,1)}, bf16[64,640]{1,0:T(8,128)(2,1)S(1)}, u32[]{:S(2)}, u32[]{:S(2)}) collective-permute-start(bf16[64,640]{1,0:T(8,128)(2,1)} %get-tuple-element.41), channel_id=1, source_target_pairs={{2,0},{4,2},{6,4},{8,6},{10,8},{12,10},{14,12},{16,14},{18,16},{20... | collective-permute-start | bytes 245768 | tf_op jit(solution)/shard_map/ppermute | solution.py:417
  76.1 12.8 %copy-start.14 = (bf16[64,640]{1,0:T(8,128)(2,1)}, bf16[64,640]{1,0:T(8,128)(2,1)S(1)}, u32[]{:S(2)}) copy-start(bf16[64,640]{1,0:T(8,128)(2,1)S(1)} %collective-permute-done.8.before_ref) | copy-start | bytes 245764
  80.0 8.9 %copy-start.15 = (bf16[64,640]{1,0:T(8,128)(2,1)}, bf16[64,640]{1,0:T(8,128)(2,1)S(1)}, u32[]{:S(2)}) copy-start(bf16[64,640]{1,0:T(8,128)(2,1)S(1)} %collective-permute-done.9.after_ref) | copy-start | bytes 245764
  80.0 13.7 %copy-start.9 = (bf16[80,3840]{1,0:T(8,128)(2,1)}, bf16[80,3840]{1,0:T(8,128)(2,1)S(1)}, u32[]{:S(2)}) copy-start(bf16[80,3840]{1,0:T(8,128)(2,1)S(1)} %collective-permute-done.6.refs_5_) | copy-start | bytes 1843204
  80.0 13.7 %copy-start.10 = (bf16[80,3840]{1,0:T(8,128)(2,1)}, bf16[80,3840]{1,0:T(8,128)(2,1)S(1)}, u32[]{:S(2)}) copy-start(bf16[80,3840]{1,0:T(8,128)(2,1)S(1)} %collective-permute-done.7.refs_6_) | copy-start | bytes 1843204
  80.0 13.6 %collective-permute-start.10 = (bf16[48,3840]{1,0:T(8,128)(2,1)S(1)}, bf16[48,3840]{1,0:T(8,128)(2,1)S(1)}, u32[]{:S(2)}, u32[]{:S(2)}) collective-permute-start(bf16[48,3840]{1,0:T(8,128)(2,1)S(1)} %slice.10), channel_id=1, source_target_pairs={{0,8},{8,16},{16,24},{24,32},{32,40},{40,48},{48,56},{56,0},{1,9},... | collective-permute-start | bytes 1105928 | tf_op jit(solution)/shard_map/ppermute | solution.py:34
  84.9 8.7 %collective-permute-start.11 = (bf16[32,3840]{1,0:T(8,128)(2,1)}, bf16[32,3840]{1,0:T(8,128)(2,1)}, u32[]{:S(2)}, u32[]{:S(2)}) collective-permute-start(bf16[32,3840]{1,0:T(8,128)(2,1)} %slice.11), channel_id=1, source_target_pairs={{0,56},{8,0},{16,8},{24,16},{32,24},{40,32},{48,40},{56,48},{1,57}... | collective-permute-start | bytes 737288 | tf_op jit(solution)/shard_map/ppermute | solution.py:34
  93.7 0.8 copy-start.13
  102.5 22.3 %all-to-all-start.2 = ((bf16[32,8,1280]{2,1,0:T(8,128)(2,1)}), bf16[32,8,1280]{2,1,0:T(8,128)(2,1)S(1)}, u32[]{:S(2)}, u32[]{:S(2)}) async-start(bf16[32,8,1280]{2,1,0:T(8,128)(2,1)} %bitcast.24), calls=%async_computation.2 | async-start | bytes 1310720 | tf_op jit(solution)/shard_map/all_to_all | solution.py:411
  124.8 0.8 copy-start.7
  127.7 8.7 %collective-permute-start.12 = (bf16[64,640]{1,0:T(8,128)(2,1)}, bf16[64,640]{1,0:T(8,128)(2,1)S(1)}, u32[]{:S(2)}, u32[]{:S(2)}) collective-permute-start(bf16[64,640]{1,0:T(8,128)(2,1)} %get-tuple-element.48), channel_id=1, source_target_pairs={{0,2},{2,4},{4,6},{6,8},{8,10},{10,12},{12,14},{14,16},{16,18},{18... | collective-permute-start | bytes 245768 | tf_op jit(solution)/shard_map/ppermute | solution.py:417
  130.3 6.2 %collective-permute-start.13 = (bf16[64,640]{1,0:T(8,128)(2,1)}, bf16[64,640]{1,0:T(8,128)(2,1)S(1)}, u32[]{:S(2)}, u32[]{:S(2)}) collective-permute-start(bf16[64,640]{1,0:T(8,128)(2,1)} %get-tuple-element.50), channel_id=1, source_target_pairs={{2,0},{4,2},{6,4},{8,6},{10,8},{12,10},{14,12},{16,14},{18,16},{20... | collective-permute-start | bytes 245768 | tf_op jit(solution)/shard_map/ppermute | solution.py:417
  136.5 0.6 copy-start.18
  137.1 0.6 copy-start.19
  143.3 20.5 %all-to-all-start.3 = ((bf16[32,8,896]{2,1,0:T(8,128)(2,1)}), bf16[32,8,896]{2,1,0:T(8,128)(2,1)S(1)}, u32[]{:S(2)}, u32[]{:S(2)}) async-start(bf16[32,8,896]{2,1,0:T(8,128)(2,1)} %bitcast.20), calls=%async_computation.3 | async-start | bytes 917504 | tf_op jit(solution)/shard_map/all_to_all | solution.py:411
  163.8 12.0 %copy-start = (bf16[32,8,896]{2,1,0:T(8,128)(2,1)}, bf16[32,8,896]{2,1,0:T(8,128)(2,1)S(1)}, u32[]{:S(2)}) copy-start(bf16[32,8,896]{2,1,0:T(8,128)(2,1)S(1)} %all-to-all-done.3) | copy-start | bytes 1376260
  163.8 40.0 %collective-permute-start.15 = (f32[128,3840]{1,0:T(8,128)}, f32[128,3840]{1,0:T(8,128)S(1)}, u32[]{:S(2)}, u32[]{:S(2)}) collective-permute-start(f32[128,3840]{1,0:T(8,128)} %get-tuple-element.56), channel_id=1, source_target_pairs={{0,1},{1,0},{2,3},{3,2},{4,5},{5,4},{6,7},{7,6},{8,9},{9,8},{10,11... | collective-permute-start | bytes 5898248 | tf_op jit(solution)/shard_map/ppermute | solution.py:24
  177.7 20.8 %collective-permute-start.14 = (bf16[128,640]{1,0:T(8,128)(2,1)}, bf16[128,640]{1,0:T(8,128)(2,1)S(1)}, u32[]{:S(2)}, u32[]{:S(2)}) collective-permute-start(bf16[128,640]{1,0:T(8,128)(2,1)} %shard_map.93), channel_id=1, source_target_pairs={{0,1},{1,0},{2,3},{3,2},{4,5},{5,4},{6,7},{7,6},{8,9},{9,8},{10,11... | collective-permute-start | bytes 491528 | tf_op jit(solution)/shard_map/ppermute | solution.py:24
  199.9 13.4 %all-to-all-start.5 = ((f32[32,8,128]{2,1,0:T(8,128)}), f32[32,8,128]{2,1,0:T(8,128)S(1)}, u32[]{:S(2)}, u32[]{:S(2)}) async-start(f32[32,8,128]{2,1,0:T(8,128)} %shard_map.94), calls=%async_computation.5 | async-start | bytes 262144 | tf_op jit(solution)/shard_map/all_to_all | solution.py:405
  203.9 15.7 %copy-start.1 = (bf16[32,8,896]{2,1,0:T(8,128)(2,1)S(1)}, bf16[32,8,896]{2,1,0:T(8,128)(2,1)}, u32[]{:S(2)}) copy-start(bf16[32,8,896]{2,1,0:T(8,128)(2,1)} %copy-done) | copy-start | bytes 1376260
  203.9 15.7 %copy-start.5 = (s32[2]{0:T(128)S(1)}, s32[2]{0:T(128)}, u32[]{:S(2)}) copy-start(s32[2]{0:T(128)} %pad_add_fusion.where_ref) | copy-start | bytes 28
  213.3 6.3 %collective-permute-start.16 = (f32[32,8,128]{2,1,0:T(8,128)S(1)}, f32[32,8,128]{2,1,0:T(8,128)S(1)}, u32[]{:S(2)}, u32[]{:S(2)}) collective-permute-start(f32[32,8,128]{2,1,0:T(8,128)S(1)} %all-to-all-done.5.tiles_ref), channel_id=1, source_target_pairs={{0,1},{1,0},{2,3},{3,2},{4,5},{5,4},{6,7},{7,6},{8,9},{9,8},{10,11... | collective-permute-start | bytes 393224 | tf_op jit(solution)/shard_map/ppermute | solution.py:24

commit v5 on v4

--- a/solution.py
+++ b/solution.py
@@ -477,14 +477,15 @@
     back = conv_rows(cells_d, before_d, after_d, kern, cell_column, sums)
     landed = after(landed, back)
     keep, send = project(where, landed, whole)
-    landed_d = exchange(back)
+    landed_d, keep = lax.optimization_barrier((exchange(back), keep))
     tile = jax.ShapeDtypeStruct((planes, 8, 128), F32)
     tiles = lax.all_to_all(in_vmem(landed_sum_kernel, tile, landed_d), "z", 0, 0, tiled=True)
+    send, landed_d = lax.optimization_barrier((send, landed_d, tiles))[:2]
+    tiles = sum_spread(tiles, ("y", "x"), CHIPS)
     other_rows = jax.ShapeDtypeStruct((TOK, local), BF16)
     d_other = swap(in_vmem(other_kernel, other_rows, where, landed_d, scalars=1))
-    tiles = sum_spread(after(tiles, d_other), ("y", "x"), CHIPS)
-    projected = (keep + swap(after(send, landed_d))).astype(BF16)
-    tiles, projected = lax.optimization_barrier((tiles, projected))
+    projected = (keep + swap(send)).astype(BF16)
+    tiles, projected, d_other = lax.optimization_barrier((tiles, projected, d_other))
 
     d_tokens, d_kernel = in_vmem(
         last_kernel,

time: 224 us -> 221 us (0.987)
  waiting for transfers between devices: 40.7 us -> 37 us
    all_to_all x1, waiting for transfers between devices: 6.7 us -> 3.04 us  [sum_spread(): return lax.all_to_all(sent, axis, 0, 0, tiled=True)]
  transfers between devices with their start and end apart: 21 -> 21, of which waited for: 8 -> 8; matrix products, arithmetic and copies ran while one was open for 4% -> 4% of each run, Pallas kernels for 12% -> 11%
where the time goes in v5:
time: 221 us; the launch traced here: 219 us
  starting transfers between devices  89.6 us (41%)
  Pallas kernels  44.9 us (20%)
  waiting for transfers between devices  37 us (17%)
  blocking collectives  31.4 us (14%)
  local copies, waits for them, and re-layouts  10.8 us (5%)
  other arithmetic  4.02 us (2%)
    ppermute x5, starting transfers between devices, swap(): return lax.ppermute(value, 'c', [(0, 1), (1, 0)])  33.8 us
    ppermute x8, starting transfers between devices, shift(): lax.ppermute(value, axis, [(i, (i + step) % size) for i in range(size)])  23.7 us
    all_to_all x3, starting transfers between devices, exchange(): lax.all_to_all(sent, ('y', 'x'), 0, 0, tiled=True).reshape(count, width)  20.8 us
    all_to_all x3, waiting for transfers between devices, exchange(): lax.all_to_all(sent, ('y', 'x'), 0, 0, tiled=True).reshape(count, width)  19.5 us
    all_to_all x1, blocking collectives, shards(): lax.all_to_all(in_vmem(landed_sum_kernel, tile, landed_d), 'z', 0, 0, til...  17.2 us
    pallas_call x7, Pallas kernels, in_vmem(): pl.pallas_call(body, out_shape=out_shape, in_specs=[SMEM] * scalars + [VM...  14.4 us
    all_to_all x1, blocking collectives, spread(): lax.all_to_all(jnp.broadcast_to(value[None], (size, *value.shape)), axis,...  14.2 us
    pallas_call x2, Pallas kernels, conv_rows(): pl.pallas_call(functools.partial(conv_body, False) if sums is None else b...  10.3 us
  transfers between devices with their start and end apart: 21, of which 8 were waited for; matrix products, arithmetic and copies ran while one was open for 4% of the time, Pallas kernels for 11%

profile of v5, /device:TPU:1, one launch (start us, length us, event | category | flops | bytes accessed | tf_op | source)
XLA Modules:
  0.0 218.8 jit_solution(552669919123270623)
XLA Ops:
  0.6 8.9 %collective-permute-start = (bf16[128,3840]{1,0:T(8,128)(2,1)}, bf16[128,3840]{1,0:T(8,128)(2,1)S(1)}, u32[]{:S(2)}, u32[]{:S(2)}) collective-permute-start(bf16[128,3840]{1,0:T(8,128)(2,1)} %bitcast.21), channel_id=1, source_target_pairs={{0,1},{1,0},{2,3},{3,2},{4,5},{5,4},{6,7},{7,6},{8,9},{9,8},{10,11... | collective-permute-start | bytes 2949128 | tf_op jit(solution)/shard_map/ppermute | solution.py:24
  9.6 1.0 broadcast_in_dim.6
  10.5 14.2 %all_to_all.30 = bf16[4,20,3840]{2,1,0:T(8,128)(2,1)S(1)} all-to-all(bf16[4,20,3840]{2,1,0:T(8,128)(2,1)S(1)} %broadcast_in_dim.6), channel_id=1, replica_groups=mesh['z'=8,'y'=8,'x'=4,'c'=2] {'x'}, dimensions={0} | all-to-all | bytes 1228800 | tf_op jit(solution)/shard_map/all_to_all | solution.py:28
  24.8 0.1 reshape.103.refs_0_
  24.9 2.1 collective-permute-start.2
  27.0 3.4 %collective-permute-start.1 = (bf16[80,3840]{1,0:T(8,128)(2,1)S(1)}, bf16[80,3840]{1,0:T(8,128)(2,1)}, u32[]{:S(2)}, u32[]{:S(2)}) collective-permute-start(bf16[80,3840]{1,0:T(8,128)(2,1)S(1)} %reshape.103.refs_0_), channel_id=1, source_target_pairs={{0,8},{8,16},{16,24},{24,32},{32,40},{40,48},{48,56},{56,0},{1,9},... | collective-permute-start | bytes 1843208 | tf_op jit(solution)/shard_map/ppermute | solution.py:34
  30.4 0.8 reshape.104
  31.2 3.9 %all-to-all-start.1 = ((bf16[32,4,1280]{2,1,0:T(4,128)(2,1)}), bf16[32,4,1280]{2,1,0:T(4,128)(2,1)S(1)}, u32[]{:S(2)}, u32[]{:S(2)}) async-start(bf16[32,4,1280]{2,1,0:T(4,128)(2,1)} %reshape.104), calls=%async_computation.1 | async-start | bytes 655360 | tf_op jit(solution)/shard_map/all_to_all | solution.py:411
  35.1 9.1 %collective-permute-done.2.refs_2_ = bf16[80,3840]{1,0:T(8,128)(2,1)S(1)} collective-permute-done((bf16[80,3840]{1,0:T(8,128)(2,1)S(1)}, bf16[80,3840]{1,0:T(8,128)(2,1)S(1)}, u32[]{:S(2)}, u32[]{:S(2)}) %collective-permute-start.2) | collective-permute-done | bytes 614432 | tf_op jit(solution)/shard_map/ppermute | solution.py:34
  44.2 1.9 collective-permute-start.5
  46.1 3.4 %collective-permute-start.4 = (bf16[80,3840]{1,0:T(8,128)(2,1)}, bf16[80,3840]{1,0:T(8,128)(2,1)}, u32[]{:S(2)}, u32[]{:S(2)}) collective-permute-start(bf16[80,3840]{1,0:T(8,128)(2,1)} %collective-permute-done.1.refs_1_), channel_id=1, source_target_pairs={{0,8},{8,16},{16,24},{24,32},{32,40},{40,48},{48,56},{56,0},{1,9},... | collective-permute-start | bytes 1843208 | tf_op jit(solution)/shard_map/ppermute | solution.py:34
  49.5 1.5 all-to-all-done.1
  51.2 2.7 %shard_map.85 = (bf16[128,640]{1,0:T(8,128)(2,1)S(1)}, bf16[144,640]{1,0:T(8,128)(2,1)S(1)}, f32[27,640]{1,0:T(8,128)S(1)}) custom-call(s32[1,640]{1,0:T(1,128)S(1)} %get-tuple-element.72.own_ref.own_ch, s32[1,640]{1,0:T(1,128)S(1)} %get-tuple-element.71.other_ref.other_ch, bf16[128,1280]{1,0:T(8,128)(2,1)S(1)} %reshape.105.rows_ref, ...), custom_call_target="tpu_custom_call" | custom-call | tf_op jit(solution)/shard_map/pallas_call | solution.py:214
  53.9 0.6 copy-done.2
  54.5 0.7 copy-done.4
  55.2 6.0 %collective-permute-start.3 = (bf16[144,640]{1,0:T(8,128)(2,1)S(1)}, bf16[144,640]{1,0:T(8,128)(2,1)S(1)}, u32[]{:S(2)}, u32[]{:S(2)}) collective-permute-start(bf16[144,640]{1,0:T(8,128)(2,1)S(1)} %get-tuple-element.38), channel_id=1, source_target_pairs={{0,1},{1,0},{2,3},{3,2},{4,5},{5,4},{6,7},{7,6},{8,9},{9,8},{10,11... | collective-permute-start | bytes 552968 | tf_op jit(solution)/shard_map/ppermute | solution.py:24
  61.2 3.3 %collective-permute-start.6 = (bf16[80,3840]{1,0:T(8,128)(2,1)}, bf16[80,3840]{1,0:T(8,128)(2,1)S(1)}, u32[]{:S(2)}, u32[]{:S(2)}) collective-permute-start(bf16[80,3840]{1,0:T(8,128)(2,1)} %collective-permute-done.4.refs_3_), channel_id=1, source_target_pairs={{0,8},{8,16},{16,24},{24,32},{32,40},{40,48},{48,56},{56,0},{1,9},... | collective-permute-start | bytes 1843208 | tf_op jit(solution)/shard_map/ppermute | solution.py:34
  64.6 3.2 %collective-permute-start.7 = (bf16[80,3840]{1,0:T(8,128)(2,1)}, bf16[80,3840]{1,0:T(8,128)(2,1)S(1)}, u32[]{:S(2)}, u32[]{:S(2)}) collective-permute-start(bf16[80,3840]{1,0:T(8,128)(2,1)} %collective-permute-done.5.refs_4_), channel_id=1, source_target_pairs={{0,56},{8,0},{16,8},{24,16},{32,24},{40,32},{48,40},{56,48},{1,57}... | collective-permute-start | bytes 1843208 | tf_op jit(solution)/shard_map/ppermute | solution.py:34
  67.8 0.6 copy-done.17
  68.4 0.2 stack.18
  68.7 0.2 stack.19
  69.2 0.2 reshape.106
  69.3 0.6 broadcast_select_fusion.2
  69.9 2.0 shard_map.86
  71.9 2.3 %collective-permute-start.8 = (bf16[64,640]{1,0:T(8,128)(2,1)}, bf16[64,640]{1,0:T(8,128)(2,1)S(1)}, u32[]{:S(2)}, u32[]{:S(2)}) collective-permute-start(bf16[64,640]{1,0:T(8,128)(2,1)} %get-tuple-element.43), channel_id=1, source_target_pairs={{0,2},{2,4},{4,6},{6,8},{8,10},{10,12},{12,14},{14,16},{16,18},{18... | collective-permute-start | bytes 245768 | tf_op jit(solution)/shard_map/ppermute | solution.py:417
  74.3 1.3 collective-permute-start.9
  75.6 0.5 collective-permute-done.8.before_ref
  76.1 3.9 %collective-permute-done.9.after_ref = bf16[64,640]{1,0:T(8,128)(2,1)S(1)} collective-permute-done((bf16[64,640]{1,0:T(8,128)(2,1)}, bf16[64,640]{1,0:T(8,128)(2,1)S(1)}, u32[]{:S(2)}, u32[]{:S(2)}) %collective-permute-start.9) | collective-permute-done | bytes 81952 | tf_op jit(solution)/shard_map/ppermute | solution.py:417
  80.0 4.1 %collective-permute-start.10 = (bf16[48,3840]{1,0:T(8,128)(2,1)S(1)}, bf16[48,3840]{1,0:T(8,128)(2,1)S(1)}, u32[]{:S(2)}, u32[]{:S(2)}) collective-permute-start(bf16[48,3840]{1,0:T(8,128)(2,1)S(1)} %slice.10), channel_id=1, source_target_pairs={{0,8},{8,16},{16,24},{24,32},{32,40},{40,48},{48,56},{56,0},{1,9},... | collective-permute-start | bytes 1105928 | tf_op jit(solution)/shard_map/ppermute | solution.py:34
  84.1 0.7 slice.11
  84.9 2.4 %collective-permute-start.11 = (bf16[32,3840]{1,0:T(8,128)(2,1)}, bf16[32,3840]{1,0:T(8,128)(2,1)}, u32[]{:S(2)}, u32[]{:S(2)}) collective-permute-start(bf16[32,3840]{1,0:T(8,128)(2,1)} %slice.11), channel_id=1, source_target_pairs={{0,56},{8,0},{16,8},{24,16},{32,24},{40,32},{48,40},{56,48},{1,57}... | collective-permute-start | bytes 737288 | tf_op jit(solution)/shard_map/ppermute | solution.py:34
  87.3 0.6 pad_add_fusion.where_ref
  87.9 0.1 copy.18
  88.0 0.8 broadcast_in_dim_reshape.8.index_ref
  88.8 4.8 %shard_map.87.y_ref = bf16[256,640]{1,0:T(8,128)(2,1)} custom-call(s32[256,1]{1,0:T(8,128)} %broadcast_in_dim_reshape.8.index_ref, f32[27,640]{1,0:T(8,128)} %copy-done.2, bf16[64,640]{1,0:T(8,128)(2,1)} %copy-done.14, bf16[256,640]{1,0:T(8,128)(2,1)} %get-tuple-element.46.cells_ref, bf16[64,640]{1,0:T(8,128)(2,1)} %copy-done.15), custom_call_target="tpu_custom_call" | custom-call | tf_op jit(solution)/shard_map/pallas_call | solution.py:308
  93.7 0.7 copy-done.13
  94.4 8.0 %shard_map.88 = (bf16[256,1280]{1,0:T(8,128)(2,1)}, bf16[640,3840]{1,0:T(8,128)(2,1)}) custom-call(s32[2]{0:T(128)} %pad_add_fusion.where_ref, bf16[256,640]{1,0:T(8,128)(2,1)} %shard_map.87.y_ref, bf16[128,3840]{1,0:T(8,128)(2,1)} %bitcast.22, bf16[128,3840]{1,0:T(8,128)(2,1)} %copy-done.11, bf16[80,3840]{1,0:T(8,128)(2,1)} %copy-done.8, ...), custom_call_target="tpu_custom_call" | custom-call | tf_op jit(solution)/shard_map/pallas_call | solution.py:129
  102.5 8.5 %all-to-all-start.2 = ((bf16[32,8,1280]{2,1,0:T(8,128)(2,1)}), bf16[32,8,1280]{2,1,0:T(8,128)(2,1)S(1)}, u32[]{:S(2)}, u32[]{:S(2)}) async-start(bf16[32,8,1280]{2,1,0:T(8,128)(2,1)} %bitcast.24), calls=%async_computation.2 | async-start | bytes 1310720 | tf_op jit(solution)/shard_map/all_to_all | solution.py:411
  111.0 0.7 broadcast_in_dim_reshape.7.cell_ref
  111.7 13.0 %all-to-all-done.2 = bf16[32,8,1280]{2,1,0:T(8,128)(2,1)S(1)} async-done(((bf16[32,8,1280]{2,1,0:T(8,128)(2,1)}), bf16[32,8,1280]{2,1,0:T(8,128)(2,1)S(1)}, u32[]{:S(2)}, u32[]{:S(2)}) %all-to-all-start.2) | async-done | bytes 655392 | tf_op jit(solution)/shard_map/all_to_all | solution.py:411
  124.8 0.8 copy-done.7
  125.6 2.1 shard_map.89
  127.7 2.5 %collective-permute-start.12 = (bf16[64,640]{1,0:T(8,128)(2,1)}, bf16[64,640]{1,0:T(8,128)(2,1)S(1)}, u32[]{:S(2)}, u32[]{:S(2)}) collective-permute-start(bf16[64,640]{1,0:T(8,128)(2,1)} %get-tuple-element.51), channel_id=1, source_target_pairs={{0,2},{2,4},{4,6},{6,8},{8,10},{10,12},{12,14},{14,16},{16,18},{18... | collective-permute-start | bytes 245768 | tf_op jit(solution)/shard_map/ppermute | solution.py:417
  130.3 1.3 collective-permute-start.13
  131.6 4.9 %shard_map.90.sums_ref = f32[256,128]{1,0:T(8,128)} custom-call(bf16[256,640]{1,0:T(8,128)(2,1)} %get-tuple-element.52.grad_ref.cells_ref, bf16[64,640]{1,0:T(8,128)(2,1)} %copy-done.14, bf16[256,640]{1,0:T(8,128)(2,1)} %get-tuple-element.46.cells_ref, bf16[64,640]{1,0:T(8,128)(2,1)} %copy-done.15), custom_call_target="tpu_custom_call" | custom-call | tf_op jit(solution)/shard_map/pallas_call | solution.py:341
  136.5 0.6 copy-done.18
  137.1 0.6 copy-done.19
  137.8 5.5 %shard_map.91 = bf16[256,896]{1,0:T(8,128)(2,1)} custom-call(s32[256,1]{1,0:T(8,128)} %broadcast_in_dim_reshape.8.index_ref, f32[27,640]{1,0:T(8,128)} %copy-done.2, bf16[64,640]{1,0:T(8,128)(2,1)} %copy-done.18, bf16[256,640]{1,0:T(8,128)(2,1)} %get-tuple-element.52.grad_ref.cells_ref, bf16[64,640]{1,0:T(8,128)(2,1)} %copy-done.19, ...), custom_call_target="tpu_custom_call" | custom-call | tf_op jit(solution)/shard_map/pallas_call | solution.py:308
  143.3 8.4 %all-to-all-start.3 = ((bf16[32,8,896]{2,1,0:T(8,128)(2,1)}), bf16[32,8,896]{2,1,0:T(8,128)(2,1)S(1)}, u32[]{:S(2)}, u32[]{:S(2)}) async-start(bf16[32,8,896]{2,1,0:T(8,128)(2,1)} %bitcast.20), calls=%async_computation.3 | async-start | bytes 917504 | tf_op jit(solution)/shard_map/all_to_all | solution.py:411
  151.7 7.2 %shard_map.92 = (f32[128,3840]{1,0:T(8,128)}, f32[128,3840]{1,0:T(8,128)}) custom-call(s32[2]{0:T(128)} %pad_add_fusion.where_ref, bf16[256,1280]{1,0:T(8,128)(2,1)} %bitcast.19, bf16[640,3840]{1,0:T(8,128)(2,1)} %get-tuple-element.55.whole_ref), custom_call_target="tpu_custom_call" | custom-call | flops 1258291200 | bytes 20000000 | tf_op jit(solution)/shard_map/pallas_call | solution.py:160
  158.9 4.9 %all-to-all-done.3 = bf16[32,8,896]{2,1,0:T(8,128)(2,1)S(1)} async-done(((bf16[32,8,896]{2,1,0:T(8,128)(2,1)}), bf16[32,8,896]{2,1,0:T(8,128)(2,1)S(1)}, u32[]{:S(2)}, u32[]{:S(2)}) %all-to-all-start.3) | async-done | bytes 458784 | tf_op jit(solution)/shard_map/all_to_all | solution.py:411
  163.8 0.8 copy-done
  164.6 1.7 shard_map.93
  166.3 17.2 %all_to_all.31.parts_ref = f32[8,8,128]{2,1,0:T(8,128)} all-to-all(f32[8,8,128]{2,1,0:T(8,128)} %shard_map.93), channel_id=1, replica_groups=mesh['z'=8,'y'=8,'x'=4,'c'=2] {'z'}, dimensions={0} | all-to-all | bytes 65536 | tf_op jit(solution)/shard_map/all_to_all | solution.py:482
  183.4 13.3 %collective-permute-start.14 = (f32[128,3840]{1,0:T(8,128)}, f32[128,3840]{1,0:T(8,128)S(1)}, u32[]{:S(2)}, u32[]{:S(2)}) collective-permute-start(f32[128,3840]{1,0:T(8,128)} %get-tuple-element.60), channel_id=1, source_target_pairs={{0,1},{1,0},{2,3},{3,2},{4,5},{5,4},{6,7},{7,6},{8,9},{9,8},{10,11... | collective-permute-start | bytes 5898248 | tf_op jit(solution)/shard_map/ppermute | solution.py:24
  196.7 1.4 shard_map.94
  198.1 3.9 %all-to-all-start.5 = ((f32[32,8,128]{2,1,0:T(8,128)}), f32[32,8,128]{2,1,0:T(8,128)S(1)}, u32[]{:S(2)}, u32[]{:S(2)}) async-start(f32[32,8,128]{2,1,0:T(8,128)} %shard_map.94), calls=%async_computation.5 | async-start | bytes 262144 | tf_op jit(solution)/shard_map/all_to_all | solution.py:405
  202.0 1.9 shard_map.95
  203.9 2.3 %collective-permute-start.15 = (bf16[128,640]{1,0:T(8,128)(2,1)}, bf16[128,640]{1,0:T(8,128)(2,1)S(1)}, u32[]{:S(2)}, u32[]{:S(2)}) collective-permute-start(bf16[128,640]{1,0:T(8,128)(2,1)} %shard_map.95), channel_id=1, source_target_pairs={{0,1},{1,0},{2,3},{3,2},{4,5},{5,4},{6,7},{7,6},{8,9},{9,8},{10,11... | collective-permute-start | bytes 491528 | tf_op jit(solution)/shard_map/ppermute | solution.py:24
  206.3 2.7 %add_convert_fusion = bf16[128,3840]{1,0:T(8,128)(2,1)} fusion(f32[128,3840]{1,0:T(8,128)} %get-tuple-element.58, f32[128,3840]{1,0:T(8,128)S(1)} %collective-permute-done.14), kind=kLoop, calls=%fused_computation | loop fusion | flops 983040 | bytes 4915200 | tf_op jit(solution)/shard_map/convert_element_type | solution.py:487
  209.0 3.0 %all-to-all-done.5.tiles_ref = f32[32,8,128]{2,1,0:T(8,128)S(1)} async-done(((f32[32,8,128]{2,1,0:T(8,128)}), f32[32,8,128]{2,1,0:T(8,128)S(1)}, u32[]{:S(2)}, u32[]{:S(2)}) %all-to-all-start.5) | async-done | bytes 131104 | tf_op jit(solution)/shard_map/all_to_all | solution.py:405
  212.0 3.3 %collective-permute-start.16 = (f32[32,8,128]{2,1,0:T(8,128)S(1)}, f32[32,8,128]{2,1,0:T(8,128)S(1)}, u32[]{:S(2)}, u32[]{:S(2)}) collective-permute-start(f32[32,8,128]{2,1,0:T(8,128)S(1)} %all-to-all-done.5.tiles_ref), channel_id=1, source_target_pairs={{0,1},{1,0},{2,3},{3,2},{4,5},{5,4},{6,7},{7,6},{8,9},{9,8},{10,11... | collective-permute-start | bytes 393224 | tf_op jit(solution)/shard_map/ppermute | solution.py:24
  215.3 1.0 collective-permute-done.16.other_ref
  216.3 2.6 %shard_map.96 = (bf16[128,1280]{1,0:T(8,128)(2,1)}, f32[27,1280]{1,0:T(8,128)}) custom-call(s32[2]{0:T(128)S(1)} %copy-done.5, s32[1,640]{1,0:T(1,128)S(1)} %get-tuple-element.72.own_ref.own_ch, s32[1,640]{1,0:T(1,128)S(1)} %get-tuple-element.71.other_ref.other_ch, bf16[256,896]{1,0:T(8,128)(2,1)S(1)} %bitcast.17, ...), custom_call_target="tpu_custom_call" | custom-call | tf_op jit(solution)/shard_map/pallas_call | solution.py:214
  (55 shorter events, 0.6 us)
Async XLA Ops:
  0.6 29.7 %copy-start.16 = (bf16[1,128,1280]{2,1,0:T(8,128)(2,1)S(1)}, bf16[1,128,1280]{2,1,0:T(8,128)(2,1)}, u32[]{:S(2)}) copy-start(bf16[1,128,1280]{2,1,0:T(8,128)(2,1)} %param.6) | copy-start | bytes 983044
  0.6 24.1 %collective-permute-start = (bf16[128,3840]{1,0:T(8,128)(2,1)}, bf16[128,3840]{1,0:T(8,128)(2,1)S(1)}, u32[]{:S(2)}, u32[]{:S(2)}) collective-permute-start(bf16[128,3840]{1,0:T(8,128)(2,1)} %bitcast.21), channel_id=1, source_target_pairs={{0,1},{1,0},{2,3},{3,2},{4,5},{5,4},{6,7},{7,6},{8,9},{9,8},{10,11... | collective-permute-start | bytes 2949128 | tf_op jit(solution)/shard_map/ppermute | solution.py:24
  24.8 26.4 %copy-start.3 = (f32[27,1280]{1,0:T(8,128)S(1)}, f32[27,1280]{1,0:T(8,128)}, u32[]{:S(2)}) copy-start(f32[27,1280]{1,0:T(8,128)} %kernel_ref.1) | copy-start | bytes 414724
  24.8 26.4 %copy-start.6 = (s32[1,128]{1,0:T(1,128)S(1)}, s32[1,128]{1,0:T(1,128)}, u32[]{:S(2)}) copy-start(s32[1,128]{1,0:T(1,128)} %place_ref.1) | copy-start | bytes 1540
  24.8 44.1 %copy-start.11 = (bf16[128,3840]{1,0:T(8,128)(2,1)}, bf16[128,3840]{1,0:T(8,128)(2,1)S(1)}, u32[]{:S(2)}) copy-start(bf16[128,3840]{1,0:T(8,128)(2,1)S(1)} %collective-permute-done.other_ref) | copy-start | bytes 2949124
  24.9 59.9 %copy-start.8 = (bf16[80,3840]{1,0:T(8,128)(2,1)}, bf16[80,3840]{1,0:T(8,128)(2,1)S(1)}, u32[]{:S(2)}) copy-start(bf16[80,3840]{1,0:T(8,128)(2,1)S(1)} %reshape.103.refs_0_) | copy-start | bytes 1843204
  24.9 19.3 %collective-permute-start.2 = (bf16[80,3840]{1,0:T(8,128)(2,1)S(1)}, bf16[80,3840]{1,0:T(8,128)(2,1)S(1)}, u32[]{:S(2)}, u32[]{:S(2)}) collective-permute-start(bf16[80,3840]{1,0:T(8,128)(2,1)S(1)} %reshape.103.refs_0_), channel_id=1, source_target_pairs={{0,56},{8,0},{16,8},{24,16},{32,24},{40,32},{48,40},{56,48},{1,57}... | collective-permute-start | bytes 1843208 | tf_op jit(solution)/shard_map/ppermute | solution.py:34
  27.0 19.1 %collective-permute-start.1 = (bf16[80,3840]{1,0:T(8,128)(2,1)S(1)}, bf16[80,3840]{1,0:T(8,128)(2,1)}, u32[]{:S(2)}, u32[]{:S(2)}) collective-permute-start(bf16[80,3840]{1,0:T(8,128)(2,1)S(1)} %reshape.103.refs_0_), channel_id=1, source_target_pairs={{0,8},{8,16},{16,24},{24,32},{32,40},{40,48},{48,56},{56,0},{1,9},... | collective-permute-start | bytes 1843208 | tf_op jit(solution)/shard_map/ppermute | solution.py:34
  31.2 19.9 %all-to-all-start.1 = ((bf16[32,4,1280]{2,1,0:T(4,128)(2,1)}), bf16[32,4,1280]{2,1,0:T(4,128)(2,1)S(1)}, u32[]{:S(2)}, u32[]{:S(2)}) async-start(bf16[32,4,1280]{2,1,0:T(4,128)(2,1)} %reshape.104), calls=%async_computation.1 | async-start | bytes 655360 | tf_op jit(solution)/shard_map/all_to_all | solution.py:411
  44.2 49.4 %copy-start.12 = (bf16[80,3840]{1,0:T(8,128)(2,1)}, bf16[80,3840]{1,0:T(8,128)(2,1)S(1)}, u32[]{:S(2)}) copy-start(bf16[80,3840]{1,0:T(8,128)(2,1)S(1)} %collective-permute-done.2.refs_2_) | copy-start | bytes 1843204
  44.2 17.0 %collective-permute-start.5 = (bf16[80,3840]{1,0:T(8,128)(2,1)S(1)}, bf16[80,3840]{1,0:T(8,128)(2,1)}, u32[]{:S(2)}, u32[]{:S(2)}) collective-permute-start(bf16[80,3840]{1,0:T(8,128)(2,1)S(1)} %collective-permute-done.2.refs_2_), channel_id=1, source_target_pairs={{0,56},{8,0},{16,8},{24,16},{32,24},{40,32},{48,40},{56,48},{1,57}... | collective-permute-start | bytes 1843208 | tf_op jit(solution)/shard_map/ppermute | solution.py:34
  46.1 15.1 %collective-permute-start.4 = (bf16[80,3840]{1,0:T(8,128)(2,1)}, bf16[80,3840]{1,0:T(8,128)(2,1)}, u32[]{:S(2)}, u32[]{:S(2)}) collective-permute-start(bf16[80,3840]{1,0:T(8,128)(2,1)} %collective-permute-done.1.refs_1_), channel_id=1, source_target_pairs={{0,8},{8,16},{16,24},{24,32},{32,40},{40,48},{48,56},{56,0},{1,9},... | collective-permute-start | bytes 1843208 | tf_op jit(solution)/shard_map/ppermute | solution.py:34
  53.9 0.6 copy-start.2
  54.5 0.7 copy-start.4
  55.2 12.5 %collective-permute-start.3 = (bf16[144,640]{1,0:T(8,128)(2,1)S(1)}, bf16[144,640]{1,0:T(8,128)(2,1)S(1)}, u32[]{:S(2)}, u32[]{:S(2)}) collective-permute-start(bf16[144,640]{1,0:T(8,128)(2,1)S(1)} %get-tuple-element.38), channel_id=1, source_target_pairs={{0,1},{1,0},{2,3},{3,2},{4,5},{5,4},{6,7},{7,6},{8,9},{9,8},{10,11... | collective-permute-start | bytes 552968 | tf_op jit(solution)/shard_map/ppermute | solution.py:24
  61.2 18.7 %collective-permute-start.6 = (bf16[80,3840]{1,0:T(8,128)(2,1)}, bf16[80,3840]{1,0:T(8,128)(2,1)S(1)}, u32[]{:S(2)}, u32[]{:S(2)}) collective-permute-start(bf16[80,3840]{1,0:T(8,128)(2,1)} %collective-permute-done.4.refs_3_), channel_id=1, source_target_pairs={{0,8},{8,16},{16,24},{24,32},{32,40},{40,48},{48,56},{56,0},{1,9},... | collective-permute-start | bytes 1843208 | tf_op jit(solution)/shard_map/ppermute | solution.py:34
  64.6 15.4 %collective-permute-start.7 = (bf16[80,3840]{1,0:T(8,128)(2,1)}, bf16[80,3840]{1,0:T(8,128)(2,1)S(1)}, u32[]{:S(2)}, u32[]{:S(2)}) collective-permute-start(bf16[80,3840]{1,0:T(8,128)(2,1)} %collective-permute-done.5.refs_4_), channel_id=1, source_target_pairs={{0,56},{8,0},{16,8},{24,16},{32,24},{40,32},{48,40},{56,48},{1,57}... | collective-permute-start | bytes 1843208 | tf_op jit(solution)/shard_map/ppermute | solution.py:34
  67.8 0.7 copy-start.17
  71.9 4.1 %collective-permute-start.8 = (bf16[64,640]{1,0:T(8,128)(2,1)}, bf16[64,640]{1,0:T(8,128)(2,1)S(1)}, u32[]{:S(2)}, u32[]{:S(2)}) collective-permute-start(bf16[64,640]{1,0:T(8,128)(2,1)} %get-tuple-element.43), channel_id=1, source_target_pairs={{0,2},{2,4},{4,6},{6,8},{8,10},{10,12},{12,14},{14,16},{16,18},{18... | collective-permute-start | bytes 245768 | tf_op jit(solution)/shard_map/ppermute | solution.py:417
  74.3 5.7 %collective-permute-start.9 = (bf16[64,640]{1,0:T(8,128)(2,1)}, bf16[64,640]{1,0:T(8,128)(2,1)S(1)}, u32[]{:S(2)}, u32[]{:S(2)}) collective-permute-start(bf16[64,640]{1,0:T(8,128)(2,1)} %get-tuple-element.44), channel_id=1, source_target_pairs={{2,0},{4,2},{6,4},{8,6},{10,8},{12,10},{14,12},{16,14},{18,16},{20... | collective-permute-start | bytes 245768 | tf_op jit(solution)/shard_map/ppermute | solution.py:417
  76.1 12.8 %copy-start.14 = (bf16[64,640]{1,0:T(8,128)(2,1)}, bf16[64,640]{1,0:T(8,128)(2,1)S(1)}, u32[]{:S(2)}) copy-start(bf16[64,640]{1,0:T(8,128)(2,1)S(1)} %collective-permute-done.8.before_ref) | copy-start | bytes 245764
  80.0 8.9 %copy-start.15 = (bf16[64,640]{1,0:T(8,128)(2,1)}, bf16[64,640]{1,0:T(8,128)(2,1)S(1)}, u32[]{:S(2)}) copy-start(bf16[64,640]{1,0:T(8,128)(2,1)S(1)} %collective-permute-done.9.after_ref) | copy-start | bytes 245764
  80.0 13.7 %copy-start.9 = (bf16[80,3840]{1,0:T(8,128)(2,1)}, bf16[80,3840]{1,0:T(8,128)(2,1)S(1)}, u32[]{:S(2)}) copy-start(bf16[80,3840]{1,0:T(8,128)(2,1)S(1)} %collective-permute-done.6.refs_5_) | copy-start | bytes 1843204
  80.0 13.7 %copy-start.10 = (bf16[80,3840]{1,0:T(8,128)(2,1)}, bf16[80,3840]{1,0:T(8,128)(2,1)S(1)}, u32[]{:S(2)}) copy-start(bf16[80,3840]{1,0:T(8,128)(2,1)S(1)} %collective-permute-done.7.refs_6_) | copy-start | bytes 1843204
  80.0 13.6 %collective-permute-start.10 = (bf16[48,3840]{1,0:T(8,128)(2,1)S(1)}, bf16[48,3840]{1,0:T(8,128)(2,1)S(1)}, u32[]{:S(2)}, u32[]{:S(2)}) collective-permute-start(bf16[48,3840]{1,0:T(8,128)(2,1)S(1)} %slice.10), channel_id=1, source_target_pairs={{0,8},{8,16},{16,24},{24,32},{32,40},{40,48},{48,56},{56,0},{1,9},... | collective-permute-start | bytes 1105928 | tf_op jit(solution)/shard_map/ppermute | solution.py:34
  84.9 8.8 %collective-permute-start.11 = (bf16[32,3840]{1,0:T(8,128)(2,1)}, bf16[32,3840]{1,0:T(8,128)(2,1)}, u32[]{:S(2)}, u32[]{:S(2)}) collective-permute-start(bf16[32,3840]{1,0:T(8,128)(2,1)} %slice.11), channel_id=1, source_target_pairs={{0,56},{8,0},{16,8},{24,16},{32,24},{40,32},{48,40},{56,48},{1,57}... | collective-permute-start | bytes 737288 | tf_op jit(solution)/shard_map/ppermute | solution.py:34
  93.7 0.8 copy-start.13
  102.5 22.3 %all-to-all-start.2 = ((bf16[32,8,1280]{2,1,0:T(8,128)(2,1)}), bf16[32,8,1280]{2,1,0:T(8,128)(2,1)S(1)}, u32[]{:S(2)}, u32[]{:S(2)}) async-start(bf16[32,8,1280]{2,1,0:T(8,128)(2,1)} %bitcast.24), calls=%async_computation.2 | async-start | bytes 1310720 | tf_op jit(solution)/shard_map/all_to_all | solution.py:411
  124.8 0.8 copy-start.7
  127.7 8.8 %collective-permute-start.12 = (bf16[64,640]{1,0:T(8,128)(2,1)}, bf16[64,640]{1,0:T(8,128)(2,1)S(1)}, u32[]{:S(2)}, u32[]{:S(2)}) collective-permute-start(bf16[64,640]{1,0:T(8,128)(2,1)} %get-tuple-element.51), channel_id=1, source_target_pairs={{0,2},{2,4},{4,6},{6,8},{8,10},{10,12},{12,14},{14,16},{16,18},{18... | collective-permute-start | bytes 245768 | tf_op jit(solution)/shard_map/ppermute | solution.py:417
  130.3 6.2 %collective-permute-start.13 = (bf16[64,640]{1,0:T(8,128)(2,1)}, bf16[64,640]{1,0:T(8,128)(2,1)S(1)}, u32[]{:S(2)}, u32[]{:S(2)}) collective-permute-start(bf16[64,640]{1,0:T(8,128)(2,1)} %get-tuple-element.53), channel_id=1, source_target_pairs={{2,0},{4,2},{6,4},{8,6},{10,8},{12,10},{14,12},{16,14},{18,16},{20... | collective-permute-start | bytes 245768 | tf_op jit(solution)/shard_map/ppermute | solution.py:417
  136.5 0.6 copy-start.18
  137.1 0.6 copy-start.19
  143.3 20.5 %all-to-all-start.3 = ((bf16[32,8,896]{2,1,0:T(8,128)(2,1)}), bf16[32,8,896]{2,1,0:T(8,128)(2,1)S(1)}, u32[]{:S(2)}, u32[]{:S(2)}) async-start(bf16[32,8,896]{2,1,0:T(8,128)(2,1)} %bitcast.20), calls=%async_computation.3 | async-start | bytes 917504 | tf_op jit(solution)/shard_map/all_to_all | solution.py:411
  163.8 0.8 copy-start
  183.4 22.9 %collective-permute-start.14 = (f32[128,3840]{1,0:T(8,128)}, f32[128,3840]{1,0:T(8,128)S(1)}, u32[]{:S(2)}, u32[]{:S(2)}) collective-permute-start(f32[128,3840]{1,0:T(8,128)} %get-tuple-element.60), channel_id=1, source_target_pairs={{0,1},{1,0},{2,3},{3,2},{4,5},{5,4},{6,7},{7,6},{8,9},{9,8},{10,11... | collective-permute-start | bytes 5898248 | tf_op jit(solution)/shard_map/ppermute | solution.py:24
  198.1 13.9 %all-to-all-start.5 = ((f32[32,8,128]{2,1,0:T(8,128)}), f32[32,8,128]{2,1,0:T(8,128)S(1)}, u32[]{:S(2)}, u32[]{:S(2)}) async-start(f32[32,8,128]{2,1,0:T(8,128)} %shard_map.94), calls=%async_computation.5 | async-start | bytes 262144 | tf_op jit(solution)/shard_map/all_to_all | solution.py:405
  203.9 12.3 %copy-start.1 = (bf16[32,8,896]{2,1,0:T(8,128)(2,1)S(1)}, bf16[32,8,896]{2,1,0:T(8,128)(2,1)}, u32[]{:S(2)}) copy-start(bf16[32,8,896]{2,1,0:T(8,128)(2,1)} %copy-done) | copy-start | bytes 1376260
  203.9 12.3 %copy-start.5 = (s32[2]{0:T(128)S(1)}, s32[2]{0:T(128)}, u32[]{:S(2)}) copy-start(s32[2]{0:T(128)} %pad_add_fusion.where_ref) | copy-start | bytes 28
  203.9 5.0 %collective-permute-start.15 = (bf16[128,640]{1,0:T(8,128)(2,1)}, bf16[128,640]{1,0:T(8,128)(2,1)S(1)}, u32[]{:S(2)}, u32[]{:S(2)}) collective-permute-start(bf16[128,640]{1,0:T(8,128)(2,1)} %shard_map.95), channel_id=1, source_target_pairs={{0,1},{1,0},{2,3},{3,2},{4,5},{5,4},{6,7},{7,6},{8,9},{9,8},{10,11... | collective-permute-start | bytes 491528 | tf_op jit(solution)/shard_map/ppermute | solution.py:24
  212.0 4.3 %collective-permute-start.16 = (f32[32,8,128]{2,1,0:T(8,128)S(1)}, f32[32,8,128]{2,1,0:T(8,128)S(1)}, u32[]{:S(2)}, u32[]{:S(2)}) collective-permute-start(f32[32,8,128]{2,1,0:T(8,128)S(1)} %all-to-all-done.5.tiles_ref), channel_id=1, source_target_pairs={{0,1},{1,0},{2,3},{3,2},{4,5},{5,4},{6,7},{7,6},{8,9},{9,8},{10,11... | collective-permute-start | bytes 393224 | tf_op jit(solution)/shard_map/ppermute | solution.py:24

commit v6 on v5

--- a/solution.py
+++ b/solution.py
@@ -424,8 +424,7 @@
     width = rows_x.shape[1]
     local = width // NC
 
-    other_d = swap(rows_d)
-    block = after(spread(proj_weight, "x", NX), other_d).reshape(ROWS, proj_weight.shape[1])
+    block = spread(proj_weight, "x", NX).reshape(ROWS, proj_weight.shape[1])
     landed_x = exchange(after(rows_x, block))
     near = ring(block, block)
     second_near = ring(*near)
@@ -461,7 +460,9 @@
 
     layer = jax.ShapeDtypeStruct((LAYER, local), BF16)
     pair = (jax.ShapeDtypeStruct((2 * TOK, local), BF16), layer, layer)
-    third_near = ring(*lax.optimization_barrier((*second_near, own_x))[:2])
+    other_d = swap(after(rows_d, landed_x))
+    *second_near, own_x, other_d = lax.optimization_barrier((*second_near, own_x, other_d))
+    third_near = ring(*second_near)
     cells_x, first_x, last_x = in_vmem(join_kernel, pair, stacked, own_x, other_x)
     before_x, after_x = faces(first_x, last_x)
     up, down, before_x, after_x = lax.optimization_barrier((*third_near, before_x, after_x))

time: 221 us -> 230 us (1.041)
  starting transfers between devices: 89.6 us -> 95.7 us
  waiting for transfers between devices: 37 us -> 42.6 us
    all_to_all x3, starting transfers between devices: 20.8 us -> 29.7 us  [exchange(): lax.all_to_all(sent, ('y', 'x'), 0, 0, tiled=True).reshape(count, width)]
    ppermute x5, starting transfers between devices: 33.8 us -> 27.8 us  [swap(): return lax.ppermute(value, 'c', [(0, 1), (1, 0)])]
    all_to_all x3, waiting for transfers between devices: 19.5 us -> 24 us  [exchange(): lax.all_to_all(sent, ('y', 'x'), 0, 0, tiled=True).reshape(count, width)]
  transfers between devices with their start and end apart: 21 -> 21, of which waited for: 8 -> 10; matrix products, arithmetic and copies ran while one was open for 4% -> 3% of each run, Pallas kernels for 11% -> 11%
where the time goes in v6:
time: 230 us; the launch traced here: 228 us
  starting transfers between devices  95.7 us (42%)
  Pallas kernels  44.9 us (20%)
  waiting for transfers between devices  42.6 us (19%)
  blocking collectives  29.7 us (13%)
  local copies, waits for them, and re-layouts  10.2 us (4%)
  other arithmetic  4.04 us (2%)
    all_to_all x3, starting transfers between devices, exchange(): lax.all_to_all(sent, ('y', 'x'), 0, 0, tiled=True).reshape(count, width)  29.7 us
    ppermute x5, starting transfers between devices, swap(): return lax.ppermute(value, 'c', [(0, 1), (1, 0)])  27.8 us
    ppermute x8, starting transfers between devices, shift(): lax.ppermute(value, axis, [(i, (i + step) % size) for i in range(size)])  25 us
    all_to_all x3, waiting for transfers between devices, exchange(): lax.all_to_all(sent, ('y', 'x'), 0, 0, tiled=True).reshape(count, width)  24 us
    all_to_all x1, blocking collectives, shards(): lax.all_to_all(in_vmem(landed_sum_kernel, tile, landed_d), 'z', 0, 0, til...  17 us
    pallas_call x7, Pallas kernels, in_vmem(): pl.pallas_call(body, out_shape=out_shape, in_specs=[SMEM] * scalars + [VM...  14.4 us
    all_to_all x1, blocking collectives, spread(): lax.all_to_all(jnp.broadcast_to(value[None], (size, *value.shape)), axis,...  12.7 us
    pallas_call x2, Pallas kernels, conv_rows(): pl.pallas_call(functools.partial(conv_body, False) if sums is None else b...  10.3 us
  transfers between devices with their start and end apart: 21, of which 10 were waited for; matrix products, arithmetic and copies ran while one was open for 3% of the time, Pallas kernels for 11%

profile of v6, /device:TPU:1, one launch (start us, length us, event | category | flops | bytes accessed | tf_op | source)
XLA Modules:
  0.0 228.1 jit_solution(11512247720327372266)
XLA Ops:
  0.6 1.0 broadcast_in_dim.6
  1.7 12.7 %all_to_all.30 = bf16[4,20,3840]{2,1,0:T(8,128)(2,1)S(1)} all-to-all(bf16[4,20,3840]{2,1,0:T(8,128)(2,1)S(1)} %broadcast_in_dim.6), channel_id=1, replica_groups=mesh['z'=8,'y'=8,'x'=4,'c'=2] {'x'}, dimensions={0} | all-to-all | bytes 1228800 | tf_op jit(solution)/shard_map/all_to_all | solution.py:28
  14.4 0.1 reshape.103.refs_0_
  14.5 0.8 reshape.104
  15.3 10.6 %all-to-all-start.1 = ((bf16[32,4,1280]{2,1,0:T(4,128)(2,1)}), bf16[32,4,1280]{2,1,0:T(4,128)(2,1)S(1)}, u32[]{:S(2)}, u32[]{:S(2)}) async-start(bf16[32,4,1280]{2,1,0:T(4,128)(2,1)} %reshape.104), calls=%async_computation.1 | async-start | bytes 655360 | tf_op jit(solution)/shard_map/all_to_all | solution.py:411
  25.9 4.4 %collective-permute-start.1 = (bf16[80,3840]{1,0:T(8,128)(2,1)S(1)}, bf16[80,3840]{1,0:T(8,128)(2,1)S(1)}, u32[]{:S(2)}, u32[]{:S(2)}) collective-permute-start(bf16[80,3840]{1,0:T(8,128)(2,1)S(1)} %reshape.103.refs_0_), channel_id=1, source_target_pairs={{0,56},{8,0},{16,8},{24,16},{32,24},{40,32},{48,40},{56,48},{1,57}... | collective-permute-start | bytes 1843208 | tf_op jit(solution)/shard_map/ppermute | solution.py:34
  30.4 1.9 collective-permute-start
  32.3 4.4 %all-to-all-done.1 = bf16[32,4,1280]{2,1,0:T(4,128)(2,1)S(1)} async-done(((bf16[32,4,1280]{2,1,0:T(4,128)(2,1)}), bf16[32,4,1280]{2,1,0:T(4,128)(2,1)S(1)}, u32[]{:S(2)}, u32[]{:S(2)}) %all-to-all-start.1) | async-done | bytes 327712 | tf_op jit(solution)/shard_map/all_to_all | solution.py:411
  36.8 7.0 %collective-permute-start.5 = (bf16[128,3840]{1,0:T(8,128)(2,1)S(1)}, bf16[128,3840]{1,0:T(8,128)(2,1)}, u32[]{:S(2)}, u32[]{:S(2)}) collective-permute-start(bf16[128,3840]{1,0:T(8,128)(2,1)S(1)} %bitcast.22), channel_id=1, source_target_pairs={{0,1},{1,0},{2,3},{3,2},{4,5},{5,4},{6,7},{7,6},{8,9},{9,8},{10,11... | collective-permute-start | bytes 2949128 | tf_op jit(solution)/shard_map/ppermute | solution.py:24
  43.8 3.3 %collective-permute-done.1.refs_2_ = bf16[80,3840]{1,0:T(8,128)(2,1)S(1)} collective-permute-done((bf16[80,3840]{1,0:T(8,128)(2,1)S(1)}, bf16[80,3840]{1,0:T(8,128)(2,1)S(1)}, u32[]{:S(2)}, u32[]{:S(2)}) %collective-permute-start.1) | collective-permute-done | bytes 614432 | tf_op jit(solution)/shard_map/ppermute | solution.py:34
  47.1 3.7 %collective-permute-start.4 = (bf16[80,3840]{1,0:T(8,128)(2,1)S(1)}, bf16[80,3840]{1,0:T(8,128)(2,1)}, u32[]{:S(2)}, u32[]{:S(2)}) collective-permute-start(bf16[80,3840]{1,0:T(8,128)(2,1)S(1)} %collective-permute-done.1.refs_2_), channel_id=1, source_target_pairs={{0,56},{8,0},{16,8},{24,16},{32,24},{40,32},{48,40},{56,48},{1,57}... | collective-permute-start | bytes 1843208 | tf_op jit(solution)/shard_map/ppermute | solution.py:34
  50.9 1.9 collective-permute-start.3
  52.9 2.7 %shard_map.85 = (bf16[128,640]{1,0:T(8,128)(2,1)S(1)}, bf16[144,640]{1,0:T(8,128)(2,1)S(1)}, f32[27,640]{1,0:T(8,128)S(1)}) custom-call(s32[1,640]{1,0:T(1,128)S(1)} %get-tuple-element.76.own_ref.own_ch, s32[1,640]{1,0:T(1,128)S(1)} %get-tuple-element.75.other_ref.other_ch, bf16[128,1280]{1,0:T(8,128)(2,1)S(1)} %reshape.105.rows_ref, ...), custom_call_target="tpu_custom_call" | custom-call | tf_op jit(solution)/shard_map/pallas_call | solution.py:214
  55.6 0.6 copy-done.2
  56.3 0.7 copy-done.4
  56.9 4.0 %collective-permute-start.2 = (bf16[144,640]{1,0:T(8,128)(2,1)S(1)}, bf16[144,640]{1,0:T(8,128)(2,1)S(1)}, u32[]{:S(2)}, u32[]{:S(2)}) collective-permute-start(bf16[144,640]{1,0:T(8,128)(2,1)S(1)} %get-tuple-element.39), channel_id=1, source_target_pairs={{0,1},{1,0},{2,3},{3,2},{4,5},{5,4},{6,7},{7,6},{8,9},{9,8},{10,11... | collective-permute-start | bytes 552968 | tf_op jit(solution)/shard_map/ppermute | solution.py:24
  60.9 1.6 collective-permute-done.4.refs_4_
  62.5 5.2 %collective-permute-done.3.refs_3_ = bf16[80,3840]{1,0:T(8,128)(2,1)} collective-permute-done((bf16[80,3840]{1,0:T(8,128)(2,1)}, bf16[80,3840]{1,0:T(8,128)(2,1)}, u32[]{:S(2)}, u32[]{:S(2)}) %collective-permute-start.3) | collective-permute-done | bytes 614432 | tf_op jit(solution)/shard_map/ppermute | solution.py:34
  67.8 1.9 collective-permute-start.6
  69.7 4.6 %collective-permute-start.7 = (bf16[80,3840]{1,0:T(8,128)(2,1)}, bf16[80,3840]{1,0:T(8,128)(2,1)S(1)}, u32[]{:S(2)}, u32[]{:S(2)}) collective-permute-start(bf16[80,3840]{1,0:T(8,128)(2,1)} %collective-permute-done.4.refs_4_), channel_id=1, source_target_pairs={{0,56},{8,0},{16,8},{24,16},{32,24},{40,32},{48,40},{56,48},{1,57}... | collective-permute-start | bytes 1843208 | tf_op jit(solution)/shard_map/ppermute | solution.py:34
  74.3 0.2 stack.18
  74.6 0.2 stack.19
  75.0 0.2 reshape.106
  75.2 0.6 broadcast_select_fusion.2
  75.8 2.0 shard_map.86
  77.8 3.6 %collective-permute-start.8 = (bf16[64,640]{1,0:T(8,128)(2,1)}, bf16[64,640]{1,0:T(8,128)(2,1)S(1)}, u32[]{:S(2)}, u32[]{:S(2)}) collective-permute-start(bf16[64,640]{1,0:T(8,128)(2,1)} %get-tuple-element.46), channel_id=1, source_target_pairs={{0,2},{2,4},{4,6},{6,8},{8,10},{10,12},{12,14},{14,16},{16,18},{18... | collective-permute-start | bytes 245768 | tf_op jit(solution)/shard_map/ppermute | solution.py:417
  81.5 1.3 collective-permute-start.9
  82.8 0.5 collective-permute-done.8.before_ref
  83.3 3.9 %collective-permute-done.9.after_ref = bf16[64,640]{1,0:T(8,128)(2,1)S(1)} collective-permute-done((bf16[64,640]{1,0:T(8,128)(2,1)}, bf16[64,640]{1,0:T(8,128)(2,1)S(1)}, u32[]{:S(2)}, u32[]{:S(2)}) %collective-permute-start.9) | collective-permute-done | bytes 81952 | tf_op jit(solution)/shard_map/ppermute | solution.py:417
  87.2 2.6 %collective-permute-start.10 = (bf16[48,3840]{1,0:T(8,128)(2,1)S(1)}, bf16[48,3840]{1,0:T(8,128)(2,1)S(1)}, u32[]{:S(2)}, u32[]{:S(2)}) collective-permute-start(bf16[48,3840]{1,0:T(8,128)(2,1)S(1)} %slice.10), channel_id=1, source_target_pairs={{0,8},{8,16},{16,24},{24,32},{32,40},{40,48},{48,56},{56,0},{1,9},... | collective-permute-start | bytes 1105928 | tf_op jit(solution)/shard_map/ppermute | solution.py:34
  89.9 0.7 slice.11
  90.6 3.8 %collective-permute-start.11 = (bf16[32,3840]{1,0:T(8,128)(2,1)}, bf16[32,3840]{1,0:T(8,128)(2,1)}, u32[]{:S(2)}, u32[]{:S(2)}) collective-permute-start(bf16[32,3840]{1,0:T(8,128)(2,1)} %slice.11), channel_id=1, source_target_pairs={{0,56},{8,0},{16,8},{24,16},{32,24},{40,32},{48,40},{56,48},{1,57}... | collective-permute-start | bytes 737288 | tf_op jit(solution)/shard_map/ppermute | solution.py:34
  94.5 0.7 pad_add_fusion.where_ref
  95.2 0.8 broadcast_in_dim_reshape.8.index_ref
  96.0 4.8 %shard_map.87.y_ref = bf16[256,640]{1,0:T(8,128)(2,1)} custom-call(s32[256,1]{1,0:T(8,128)} %broadcast_in_dim_reshape.8.index_ref, f32[27,640]{1,0:T(8,128)} %copy-done.2, bf16[64,640]{1,0:T(8,128)(2,1)} %copy-done.14, bf16[256,640]{1,0:T(8,128)(2,1)} %get-tuple-element.49.cells_ref, bf16[64,640]{1,0:T(8,128)(2,1)} %copy-done.15), custom_call_target="tpu_custom_call" | custom-call | tf_op jit(solution)/shard_map/pallas_call | solution.py:308
  100.9 0.7 copy-done.13
  101.6 8.0 %shard_map.88 = (bf16[256,1280]{1,0:T(8,128)(2,1)}, bf16[640,3840]{1,0:T(8,128)(2,1)}) custom-call(s32[2]{0:T(128)} %pad_add_fusion.where_ref, bf16[256,640]{1,0:T(8,128)(2,1)} %shard_map.87.y_ref, bf16[128,3840]{1,0:T(8,128)(2,1)} %bitcast.21, bf16[128,3840]{1,0:T(8,128)(2,1)} %collective-permute-done.5.other_ref, bf16[80,3840]{1,0:T(8,128)(2,1)} %copy-done.8, ...), custom_call_target="tpu_custom_call" | custom-call | tf_op jit(solution)/shard_map/pallas_call | solution.py:129
  109.6 11.3 %all-to-all-start.2 = ((bf16[32,8,1280]{2,1,0:T(8,128)(2,1)}), bf16[32,8,1280]{2,1,0:T(8,128)(2,1)S(1)}, u32[]{:S(2)}, u32[]{:S(2)}) async-start(bf16[32,8,1280]{2,1,0:T(8,128)(2,1)} %bitcast.24), calls=%async_computation.2 | async-start | bytes 1310720 | tf_op jit(solution)/shard_map/all_to_all | solution.py:411
  121.0 0.7 broadcast_in_dim_reshape.7.cell_ref
  121.7 14.7 %all-to-all-done.2 = bf16[32,8,1280]{2,1,0:T(8,128)(2,1)S(1)} async-done(((bf16[32,8,1280]{2,1,0:T(8,128)(2,1)}), bf16[32,8,1280]{2,1,0:T(8,128)(2,1)S(1)}, u32[]{:S(2)}, u32[]{:S(2)}) %all-to-all-start.2) | async-done | bytes 655392 | tf_op jit(solution)/shard_map/all_to_all | solution.py:411
  136.4 0.8 copy-done.7
  137.2 2.1 shard_map.89
  139.3 3.1 %collective-permute-start.12 = (bf16[64,640]{1,0:T(8,128)(2,1)}, bf16[64,640]{1,0:T(8,128)(2,1)S(1)}, u32[]{:S(2)}, u32[]{:S(2)}) collective-permute-start(bf16[64,640]{1,0:T(8,128)(2,1)} %get-tuple-element.55), channel_id=1, source_target_pairs={{0,2},{2,4},{4,6},{6,8},{8,10},{10,12},{12,14},{14,16},{16,18},{18... | collective-permute-start | bytes 245768 | tf_op jit(solution)/shard_map/ppermute | solution.py:417
  142.4 1.3 collective-permute-start.13
  143.7 4.9 %shard_map.90.sums_ref = f32[256,128]{1,0:T(8,128)} custom-call(bf16[256,640]{1,0:T(8,128)(2,1)} %get-tuple-element.56.grad_ref.cells_ref, bf16[64,640]{1,0:T(8,128)(2,1)} %copy-done.14, bf16[256,640]{1,0:T(8,128)(2,1)} %get-tuple-element.49.cells_ref, bf16[64,640]{1,0:T(8,128)(2,1)} %copy-done.15), custom_call_target="tpu_custom_call" | custom-call | tf_op jit(solution)/shard_map/pallas_call | solution.py:341
  148.6 0.6 copy-done.18
  149.3 0.6 copy-done.19
  149.9 5.5 %shard_map.91 = bf16[256,896]{1,0:T(8,128)(2,1)} custom-call(s32[256,1]{1,0:T(8,128)} %broadcast_in_dim_reshape.8.index_ref, f32[27,640]{1,0:T(8,128)} %copy-done.2, bf16[64,640]{1,0:T(8,128)(2,1)} %copy-done.18, bf16[256,640]{1,0:T(8,128)(2,1)} %get-tuple-element.56.grad_ref.cells_ref, bf16[64,640]{1,0:T(8,128)(2,1)} %copy-done.19, ...), custom_call_target="tpu_custom_call" | custom-call | tf_op jit(solution)/shard_map/pallas_call | solution.py:308
  155.4 7.8 %all-to-all-start.3 = ((bf16[32,8,896]{2,1,0:T(8,128)(2,1)}), bf16[32,8,896]{2,1,0:T(8,128)(2,1)S(1)}, u32[]{:S(2)}, u32[]{:S(2)}) async-start(bf16[32,8,896]{2,1,0:T(8,128)(2,1)} %bitcast.20), calls=%async_computation.3 | async-start | bytes 917504 | tf_op jit(solution)/shard_map/all_to_all | solution.py:411
  163.2 7.2 %shard_map.92 = (f32[128,3840]{1,0:T(8,128)}, f32[128,3840]{1,0:T(8,128)}) custom-call(s32[2]{0:T(128)} %pad_add_fusion.where_ref, bf16[256,1280]{1,0:T(8,128)(2,1)} %bitcast.19, bf16[640,3840]{1,0:T(8,128)(2,1)} %get-tuple-element.59.whole_ref), custom_call_target="tpu_custom_call" | custom-call | flops 1258291200 | bytes 20000000 | tf_op jit(solution)/shard_map/pallas_call | solution.py:160
  170.4 4.9 %all-to-all-done.3 = bf16[32,8,896]{2,1,0:T(8,128)(2,1)S(1)} async-done(((bf16[32,8,896]{2,1,0:T(8,128)(2,1)}), bf16[32,8,896]{2,1,0:T(8,128)(2,1)S(1)}, u32[]{:S(2)}, u32[]{:S(2)}) %all-to-all-start.3) | async-done | bytes 458784 | tf_op jit(solution)/shard_map/all_to_all | solution.py:411
  175.4 0.8 copy-done
  176.1 1.7 shard_map.93
  177.8 17.0 %all_to_all.31.parts_ref = f32[8,8,128]{2,1,0:T(8,128)} all-to-all(f32[8,8,128]{2,1,0:T(8,128)} %shard_map.93), channel_id=1, replica_groups=mesh['z'=8,'y'=8,'x'=4,'c'=2] {'z'}, dimensions={0} | all-to-all | bytes 65536 | tf_op jit(solution)/shard_map/all_to_all | solution.py:483
  194.8 11.1 %collective-permute-start.14 = (f32[128,3840]{1,0:T(8,128)}, f32[128,3840]{1,0:T(8,128)S(1)}, u32[]{:S(2)}, u32[]{:S(2)}) collective-permute-start(f32[128,3840]{1,0:T(8,128)} %get-tuple-element.64), channel_id=1, source_target_pairs={{0,1},{1,0},{2,3},{3,2},{4,5},{5,4},{6,7},{7,6},{8,9},{9,8},{10,11... | collective-permute-start | bytes 5898248 | tf_op jit(solution)/shard_map/ppermute | solution.py:24
  206.0 1.4 shard_map.94
  207.4 3.9 %all-to-all-start.5 = ((f32[32,8,128]{2,1,0:T(8,128)}), f32[32,8,128]{2,1,0:T(8,128)S(1)}, u32[]{:S(2)}, u32[]{:S(2)}) async-start(f32[32,8,128]{2,1,0:T(8,128)} %shard_map.94), calls=%async_computation.5 | async-start | bytes 262144 | tf_op jit(solution)/shard_map/all_to_all | solution.py:405
  211.3 1.9 shard_map.95
  213.2 2.3 %collective-permute-start.15 = (bf16[128,640]{1,0:T(8,128)(2,1)}, bf16[128,640]{1,0:T(8,128)(2,1)S(1)}, u32[]{:S(2)}, u32[]{:S(2)}) collective-permute-start(bf16[128,640]{1,0:T(8,128)(2,1)} %shard_map.95), channel_id=1, source_target_pairs={{0,1},{1,0},{2,3},{3,2},{4,5},{5,4},{6,7},{7,6},{8,9},{9,8},{10,11... | collective-permute-start | bytes 491528 | tf_op jit(solution)/shard_map/ppermute | solution.py:24
  215.6 2.7 %add_convert_fusion = bf16[128,3840]{1,0:T(8,128)(2,1)} fusion(f32[128,3840]{1,0:T(8,128)} %get-tuple-element.62, f32[128,3840]{1,0:T(8,128)S(1)} %collective-permute-done.14), kind=kLoop, calls=%fused_computation | loop fusion | flops 983040 | bytes 4915200 | tf_op jit(solution)/shard_map/convert_element_type | solution.py:488
  218.2 3.0 %all-to-all-done.5.tiles_ref = f32[32,8,128]{2,1,0:T(8,128)S(1)} async-done(((f32[32,8,128]{2,1,0:T(8,128)}), f32[32,8,128]{2,1,0:T(8,128)S(1)}, u32[]{:S(2)}, u32[]{:S(2)}) %all-to-all-start.5) | async-done | bytes 131104 | tf_op jit(solution)/shard_map/all_to_all | solution.py:405
  221.3 3.3 %collective-permute-start.16 = (f32[32,8,128]{2,1,0:T(8,128)S(1)}, f32[32,8,128]{2,1,0:T(8,128)S(1)}, u32[]{:S(2)}, u32[]{:S(2)}) collective-permute-start(f32[32,8,128]{2,1,0:T(8,128)S(1)} %all-to-all-done.5.tiles_ref), channel_id=1, source_target_pairs={{0,1},{1,0},{2,3},{3,2},{4,5},{5,4},{6,7},{7,6},{8,9},{9,8},{10,11... | collective-permute-start | bytes 393224 | tf_op jit(solution)/shard_map/ppermute | solution.py:24
  224.6 1.0 collective-permute-done.16.other_ref
  225.6 2.6 %shard_map.96 = (bf16[128,1280]{1,0:T(8,128)(2,1)}, f32[27,1280]{1,0:T(8,128)}) custom-call(s32[2]{0:T(128)S(1)} %copy-done.5, s32[1,640]{1,0:T(1,128)S(1)} %get-tuple-element.76.own_ref.own_ch, s32[1,640]{1,0:T(1,128)S(1)} %get-tuple-element.75.other_ref.other_ch, bf16[256,896]{1,0:T(8,128)(2,1)S(1)} %bitcast.17, ...), custom_call_target="tpu_custom_call" | custom-call | tf_op jit(solution)/shard_map/pallas_call | solution.py:214
  (55 shorter events, 0.8 us)
Async XLA Ops:
  0.6 13.9 %copy-start.16 = (bf16[1,128,1280]{2,1,0:T(8,128)(2,1)S(1)}, bf16[1,128,1280]{2,1,0:T(8,128)(2,1)}, u32[]{:S(2)}) copy-start(bf16[1,128,1280]{2,1,0:T(8,128)(2,1)} %param.6) | copy-start | bytes 983044
  14.4 22.4 %copy-start.11 = (bf16[1,128,3840]{2,1,0:T(8,128)(2,1)S(1)}, bf16[1,128,3840]{2,1,0:T(8,128)(2,1)}, u32[]{:S(2)}) copy-start(bf16[1,128,3840]{2,1,0:T(8,128)(2,1)} %param.10) | copy-start | bytes 2949124
  14.4 38.5 %copy-start.3 = (f32[27,1280]{1,0:T(8,128)S(1)}, f32[27,1280]{1,0:T(8,128)}, u32[]{:S(2)}) copy-start(f32[27,1280]{1,0:T(8,128)} %kernel_ref.1) | copy-start | bytes 414724
  14.4 38.5 %copy-start.6 = (s32[1,128]{1,0:T(1,128)S(1)}, s32[1,128]{1,0:T(1,128)}, u32[]{:S(2)}) copy-start(s32[1,128]{1,0:T(1,128)} %place_ref.1) | copy-start | bytes 1540
  14.5 76.1 %copy-start.8 = (bf16[80,3840]{1,0:T(8,128)(2,1)}, bf16[80,3840]{1,0:T(8,128)(2,1)S(1)}, u32[]{:S(2)}) copy-start(bf16[80,3840]{1,0:T(8,128)(2,1)S(1)} %reshape.103.refs_0_) | copy-start | bytes 1843204
  15.3 21.4 %all-to-all-start.1 = ((bf16[32,4,1280]{2,1,0:T(4,128)(2,1)}), bf16[32,4,1280]{2,1,0:T(4,128)(2,1)S(1)}, u32[]{:S(2)}, u32[]{:S(2)}) async-start(bf16[32,4,1280]{2,1,0:T(4,128)(2,1)} %reshape.104), calls=%async_computation.1 | async-start | bytes 655360 | tf_op jit(solution)/shard_map/all_to_all | solution.py:411
  25.9 21.2 %collective-permute-start.1 = (bf16[80,3840]{1,0:T(8,128)(2,1)S(1)}, bf16[80,3840]{1,0:T(8,128)(2,1)S(1)}, u32[]{:S(2)}, u32[]{:S(2)}) collective-permute-start(bf16[80,3840]{1,0:T(8,128)(2,1)S(1)} %reshape.103.refs_0_), channel_id=1, source_target_pairs={{0,56},{8,0},{16,8},{24,16},{32,24},{40,32},{48,40},{56,48},{1,57}... | collective-permute-start | bytes 1843208 | tf_op jit(solution)/shard_map/ppermute | solution.py:34
  30.4 20.5 %collective-permute-start = (bf16[80,3840]{1,0:T(8,128)(2,1)S(1)}, bf16[80,3840]{1,0:T(8,128)(2,1)}, u32[]{:S(2)}, u32[]{:S(2)}) collective-permute-start(bf16[80,3840]{1,0:T(8,128)(2,1)S(1)} %reshape.103.refs_0_), channel_id=1, source_target_pairs={{0,8},{8,16},{16,24},{24,32},{32,40},{40,48},{48,56},{56,0},{1,9},... | collective-permute-start | bytes 1843208 | tf_op jit(solution)/shard_map/ppermute | solution.py:34
  36.8 31.0 %collective-permute-start.5 = (bf16[128,3840]{1,0:T(8,128)(2,1)S(1)}, bf16[128,3840]{1,0:T(8,128)(2,1)}, u32[]{:S(2)}, u32[]{:S(2)}) collective-permute-start(bf16[128,3840]{1,0:T(8,128)(2,1)S(1)} %bitcast.22), channel_id=1, source_target_pairs={{0,1},{1,0},{2,3},{3,2},{4,5},{5,4},{6,7},{7,6},{8,9},{9,8},{10,11... | collective-permute-start | bytes 2949128 | tf_op jit(solution)/shard_map/ppermute | solution.py:24
  47.1 53.7 %copy-start.12 = (bf16[80,3840]{1,0:T(8,128)(2,1)}, bf16[80,3840]{1,0:T(8,128)(2,1)S(1)}, u32[]{:S(2)}) copy-start(bf16[80,3840]{1,0:T(8,128)(2,1)S(1)} %collective-permute-done.1.refs_2_) | copy-start | bytes 1843204
  47.1 15.4 %collective-permute-start.4 = (bf16[80,3840]{1,0:T(8,128)(2,1)S(1)}, bf16[80,3840]{1,0:T(8,128)(2,1)}, u32[]{:S(2)}, u32[]{:S(2)}) collective-permute-start(bf16[80,3840]{1,0:T(8,128)(2,1)S(1)} %collective-permute-done.1.refs_2_), channel_id=1, source_target_pairs={{0,56},{8,0},{16,8},{24,16},{32,24},{40,32},{48,40},{56,48},{1,57}... | collective-permute-start | bytes 1843208 | tf_op jit(solution)/shard_map/ppermute | solution.py:34
  50.9 16.8 %collective-permute-start.3 = (bf16[80,3840]{1,0:T(8,128)(2,1)}, bf16[80,3840]{1,0:T(8,128)(2,1)}, u32[]{:S(2)}, u32[]{:S(2)}) collective-permute-start(bf16[80,3840]{1,0:T(8,128)(2,1)} %collective-permute-done.refs_1_), channel_id=1, source_target_pairs={{0,8},{8,16},{16,24},{24,32},{32,40},{40,48},{48,56},{56,0},{1,9},... | collective-permute-start | bytes 1843208 | tf_op jit(solution)/shard_map/ppermute | solution.py:34
  55.6 0.6 copy-start.2
  56.3 0.7 copy-start.4
  56.9 17.3 %collective-permute-start.2 = (bf16[144,640]{1,0:T(8,128)(2,1)S(1)}, bf16[144,640]{1,0:T(8,128)(2,1)S(1)}, u32[]{:S(2)}, u32[]{:S(2)}) collective-permute-start(bf16[144,640]{1,0:T(8,128)(2,1)S(1)} %get-tuple-element.39), channel_id=1, source_target_pairs={{0,1},{1,0},{2,3},{3,2},{4,5},{5,4},{6,7},{7,6},{8,9},{9,8},{10,11... | collective-permute-start | bytes 552968 | tf_op jit(solution)/shard_map/ppermute | solution.py:24
  67.8 19.4 %collective-permute-start.6 = (bf16[80,3840]{1,0:T(8,128)(2,1)}, bf16[80,3840]{1,0:T(8,128)(2,1)S(1)}, u32[]{:S(2)}, u32[]{:S(2)}) collective-permute-start(bf16[80,3840]{1,0:T(8,128)(2,1)} %collective-permute-done.3.refs_3_), channel_id=1, source_target_pairs={{0,8},{8,16},{16,24},{24,32},{32,40},{40,48},{48,56},{56,0},{1,9},... | collective-permute-start | bytes 1843208 | tf_op jit(solution)/shard_map/ppermute | solution.py:34
  69.7 17.5 %collective-permute-start.7 = (bf16[80,3840]{1,0:T(8,128)(2,1)}, bf16[80,3840]{1,0:T(8,128)(2,1)S(1)}, u32[]{:S(2)}, u32[]{:S(2)}) collective-permute-start(bf16[80,3840]{1,0:T(8,128)(2,1)} %collective-permute-done.4.refs_4_), channel_id=1, source_target_pairs={{0,56},{8,0},{16,8},{24,16},{32,24},{40,32},{48,40},{56,48},{1,57}... | collective-permute-start | bytes 1843208 | tf_op jit(solution)/shard_map/ppermute | solution.py:34
  74.3 1.5 copy-start.17
  77.8 5.4 %collective-permute-start.8 = (bf16[64,640]{1,0:T(8,128)(2,1)}, bf16[64,640]{1,0:T(8,128)(2,1)S(1)}, u32[]{:S(2)}, u32[]{:S(2)}) collective-permute-start(bf16[64,640]{1,0:T(8,128)(2,1)} %get-tuple-element.46), channel_id=1, source_target_pairs={{0,2},{2,4},{4,6},{6,8},{8,10},{10,12},{12,14},{14,16},{16,18},{18... | collective-permute-start | bytes 245768 | tf_op jit(solution)/shard_map/ppermute | solution.py:417
  81.5 5.7 %collective-permute-start.9 = (bf16[64,640]{1,0:T(8,128)(2,1)}, bf16[64,640]{1,0:T(8,128)(2,1)S(1)}, u32[]{:S(2)}, u32[]{:S(2)}) collective-permute-start(bf16[64,640]{1,0:T(8,128)(2,1)} %get-tuple-element.47), channel_id=1, source_target_pairs={{2,0},{4,2},{6,4},{8,6},{10,8},{12,10},{14,12},{16,14},{18,16},{20... | collective-permute-start | bytes 245768 | tf_op jit(solution)/shard_map/ppermute | solution.py:417
  83.3 12.8 %copy-start.14 = (bf16[64,640]{1,0:T(8,128)(2,1)}, bf16[64,640]{1,0:T(8,128)(2,1)S(1)}, u32[]{:S(2)}) copy-start(bf16[64,640]{1,0:T(8,128)(2,1)S(1)} %collective-permute-done.8.before_ref) | copy-start | bytes 245764
  87.2 8.8 %copy-start.15 = (bf16[64,640]{1,0:T(8,128)(2,1)}, bf16[64,640]{1,0:T(8,128)(2,1)S(1)}, u32[]{:S(2)}) copy-start(bf16[64,640]{1,0:T(8,128)(2,1)S(1)} %collective-permute-done.9.after_ref) | copy-start | bytes 245764
  87.2 13.7 %copy-start.9 = (bf16[80,3840]{1,0:T(8,128)(2,1)}, bf16[80,3840]{1,0:T(8,128)(2,1)S(1)}, u32[]{:S(2)}) copy-start(bf16[80,3840]{1,0:T(8,128)(2,1)S(1)} %collective-permute-done.6.refs_5_) | copy-start | bytes 1843204
  87.2 13.7 %copy-start.10 = (bf16[80,3840]{1,0:T(8,128)(2,1)}, bf16[80,3840]{1,0:T(8,128)(2,1)S(1)}, u32[]{:S(2)}) copy-start(bf16[80,3840]{1,0:T(8,128)(2,1)S(1)} %collective-permute-done.7.refs_6_) | copy-start | bytes 1843204
  87.2 13.6 %collective-permute-start.10 = (bf16[48,3840]{1,0:T(8,128)(2,1)S(1)}, bf16[48,3840]{1,0:T(8,128)(2,1)S(1)}, u32[]{:S(2)}, u32[]{:S(2)}) collective-permute-start(bf16[48,3840]{1,0:T(8,128)(2,1)S(1)} %slice.10), channel_id=1, source_target_pairs={{0,8},{8,16},{16,24},{24,32},{32,40},{40,48},{48,56},{56,0},{1,9},... | collective-permute-start | bytes 1105928 | tf_op jit(solution)/shard_map/ppermute | solution.py:34
  90.6 10.2 %collective-permute-start.11 = (bf16[32,3840]{1,0:T(8,128)(2,1)}, bf16[32,3840]{1,0:T(8,128)(2,1)}, u32[]{:S(2)}, u32[]{:S(2)}) collective-permute-start(bf16[32,3840]{1,0:T(8,128)(2,1)} %slice.11), channel_id=1, source_target_pairs={{0,56},{8,0},{16,8},{24,16},{32,24},{40,32},{48,40},{56,48},{1,57}... | collective-permute-start | bytes 737288 | tf_op jit(solution)/shard_map/ppermute | solution.py:34
  100.9 0.8 copy-start.13
  109.6 26.7 %all-to-all-start.2 = ((bf16[32,8,1280]{2,1,0:T(8,128)(2,1)}), bf16[32,8,1280]{2,1,0:T(8,128)(2,1)S(1)}, u32[]{:S(2)}, u32[]{:S(2)}) async-start(bf16[32,8,1280]{2,1,0:T(8,128)(2,1)} %bitcast.24), calls=%async_computation.2 | async-start | bytes 1310720 | tf_op jit(solution)/shard_map/all_to_all | solution.py:411
  136.4 0.8 copy-start.7
  139.3 9.3 %collective-permute-start.12 = (bf16[64,640]{1,0:T(8,128)(2,1)}, bf16[64,640]{1,0:T(8,128)(2,1)S(1)}, u32[]{:S(2)}, u32[]{:S(2)}) collective-permute-start(bf16[64,640]{1,0:T(8,128)(2,1)} %get-tuple-element.55), channel_id=1, source_target_pairs={{0,2},{2,4},{4,6},{6,8},{8,10},{10,12},{12,14},{14,16},{16,18},{18... | collective-permute-start | bytes 245768 | tf_op jit(solution)/shard_map/ppermute | solution.py:417
  142.4 6.2 %collective-permute-start.13 = (bf16[64,640]{1,0:T(8,128)(2,1)}, bf16[64,640]{1,0:T(8,128)(2,1)S(1)}, u32[]{:S(2)}, u32[]{:S(2)}) collective-permute-start(bf16[64,640]{1,0:T(8,128)(2,1)} %get-tuple-element.57), channel_id=1, source_target_pairs={{2,0},{4,2},{6,4},{8,6},{10,8},{12,10},{14,12},{16,14},{18,16},{20... | collective-permute-start | bytes 245768 | tf_op jit(solution)/shard_map/ppermute | solution.py:417
  148.6 0.6 copy-start.18
  149.3 0.6 copy-start.19
  155.4 19.9 %all-to-all-start.3 = ((bf16[32,8,896]{2,1,0:T(8,128)(2,1)}), bf16[32,8,896]{2,1,0:T(8,128)(2,1)S(1)}, u32[]{:S(2)}, u32[]{:S(2)}) async-start(bf16[32,8,896]{2,1,0:T(8,128)(2,1)} %bitcast.20), calls=%async_computation.3 | async-start | bytes 917504 | tf_op jit(solution)/shard_map/all_to_all | solution.py:411
  175.3 0.8 copy-start
  194.8 20.8 %collective-permute-start.14 = (f32[128,3840]{1,0:T(8,128)}, f32[128,3840]{1,0:T(8,128)S(1)}, u32[]{:S(2)}, u32[]{:S(2)}) collective-permute-start(f32[128,3840]{1,0:T(8,128)} %get-tuple-element.64), channel_id=1, source_target_pairs={{0,1},{1,0},{2,3},{3,2},{4,5},{5,4},{6,7},{7,6},{8,9},{9,8},{10,11... | collective-permute-start | bytes 5898248 | tf_op jit(solution)/shard_map/ppermute | solution.py:24
  207.4 13.9 %all-to-all-start.5 = ((f32[32,8,128]{2,1,0:T(8,128)}), f32[32,8,128]{2,1,0:T(8,128)S(1)}, u32[]{:S(2)}, u32[]{:S(2)}) async-start(f32[32,8,128]{2,1,0:T(8,128)} %shard_map.94), calls=%async_computation.5 | async-start | bytes 262144 | tf_op jit(solution)/shard_map/all_to_all | solution.py:405
  213.2 12.3 %copy-start.1 = (bf16[32,8,896]{2,1,0:T(8,128)(2,1)S(1)}, bf16[32,8,896]{2,1,0:T(8,128)(2,1)}, u32[]{:S(2)}) copy-start(bf16[32,8,896]{2,1,0:T(8,128)(2,1)} %copy-done) | copy-start | bytes 1376260
  213.2 12.3 %copy-start.5 = (s32[2]{0:T(128)S(1)}, s32[2]{0:T(128)}, u32[]{:S(2)}) copy-start(s32[2]{0:T(128)} %pad_add_fusion.where_ref) | copy-start | bytes 28
  213.2 5.0 %collective-permute-start.15 = (bf16[128,640]{1,0:T(8,128)(2,1)}, bf16[128,640]{1,0:T(8,128)(2,1)S(1)}, u32[]{:S(2)}, u32[]{:S(2)}) collective-permute-start(bf16[128,640]{1,0:T(8,128)(2,1)} %shard_map.95), channel_id=1, source_target_pairs={{0,1},{1,0},{2,3},{3,2},{4,5},{5,4},{6,7},{7,6},{8,9},{9,8},{10,11... | collective-permute-start | bytes 491528 | tf_op jit(solution)/shard_map/ppermute | solution.py:24
  221.3 4.3 %collective-permute-start.16 = (f32[32,8,128]{2,1,0:T(8,128)S(1)}, f32[32,8,128]{2,1,0:T(8,128)S(1)}, u32[]{:S(2)}, u32[]{:S(2)}) collective-permute-start(f32[32,8,128]{2,1,0:T(8,128)S(1)} %all-to-all-done.5.tiles_ref), channel_id=1, source_target_pairs={{0,1},{1,0},{2,3},{3,2},{4,5},{5,4},{6,7},{7,6},{8,9},{9,8},{10,11... | collective-permute-start | bytes 393224 | tf_op jit(solution)/shard_map/ppermute | solution.py:24
